TPU v7x, 32 devices: a whole 2x2x4 slice. The times are simulated.
32 devices in a mesh: req: 32 (over z, y, x, core).
Axes of the slice: x: 2, y: 2, z: 4, core: 2. Of those that a mesh axis runs over, the one named last changes fastest.
Arguments:
- queries: bfloat16 [4096, 2560], P('req'), may hold values from -8 to 8
- prefix_keys: bfloat16 [8192, 640], P('req'), may hold values from -6 to 6
- prefix_values: bfloat16 [8192, 640], P('req'), may hold values from -6 to 6
- pool_keys: bfloat16 [4096, 16, 640], P('req'), may hold values from -6 to 6
- pool_values: bfloat16 [4096, 16, 640], P('req'), may hold values from -6 to 6
- page_table: int32 [4096, 8], P('req'), may hold values from 0 to 127
- private_length: int32 [4096], P('req'), may hold values from 1 to 128
- group_ids: int32 [4096, 1], P('req'), may hold values from 0 to 31; in each aligned block of 128 rows (0 to 127, 128 to 255, ...) at most 8 rows name the same one
- live_rows: int32 [32], P('req'), may hold values from 1 to 128, 2048 in all
- out_weight: bfloat16 [2560, 2560], replicated, may hold values from -0.75 to 0.75
Outputs:
- projected: bfloat16 [4096, 2560], P('req')
Inputs may be any that keep to these rules, and one draw needn't show every extreme that they name: `group_ids`: the group of a row is also the index of the device that holds that group's prompt; at most 8 rows of one device name one group. `live_rows`: the counts sum to 2048.
All inputs are finite; a program needn't handle non-finite values. No bound on the sum of `live_rows` on one device may be relied on, other than what follows from the above.
Results may differ from a plain program's by a relative error of at most 0.007.
Values may be sent and summed in bfloat16 or wider, within the bound.
No kernel may reach another device: no remote copies, remote signals or barrier semaphores. Data moves between devices by JAX's collectives and lax.ppermute only.
A program may use at most 128 MiB of HBM per device.

v0:
```python
import jax
import jax.numpy as jnp
from jax import lax
from jax.sharding import PartitionSpec as P

H = 32
KVH = 8
HD = 80


def weigh_values(scores, values, spec):
    largest = jnp.max(scores, axis=-1, keepdims=True)
    weights = jnp.exp(scores - largest)
    weight_sum = jnp.sum(weights, axis=-1)
    summed = jnp.einsum(
        spec, weights.astype(jnp.bfloat16), values, preferred_element_type=jnp.float32
    )
    return (summed / weight_sum[..., None], largest[..., 0] + jnp.log(weight_sum))


def shared_prefix(query_rows, prefix_keys, prefix_values):
    row_count = query_rows.shape[0]
    group_size = H // KVH
    scale = HD ** (-0.5)
    head_rows = jnp.moveaxis(query_rows.reshape(row_count, KVH, group_size, HD), 1, 0)
    key_heads = jnp.moveaxis(prefix_keys.reshape(-1, KVH, HD), 1, 0)
    value_heads = jnp.moveaxis(prefix_values.reshape(-1, KVH, HD), 1, 0)

    def shared_per_head(operands):
        query_head, key_head, value_head = operands
        scores = (
            jnp.einsum("rgd,td->rgt", query_head, key_head, preferred_element_type=jnp.float32)
            * scale
        )
        return weigh_values(scores, value_head, "rgt,td->rgd")

    result, log_total = lax.map(shared_per_head, (head_rows, key_heads, value_heads))
    result = jnp.moveaxis(result, 0, 1).reshape(row_count, H * HD).astype(jnp.bfloat16)
    log_total = jnp.moveaxis(log_total, 0, 1).reshape(row_count, H)
    return (result, log_total)


def private_part(queries, pool_keys, pool_values, page_table, private_length):
    row_count = queries.shape[0]
    group_size = H // KVH
    scale = HD ** (-0.5)
    page_size = pool_keys.shape[1]
    token_count = pool_keys.shape[0] * page_size
    token_index = jnp.arange(token_count, dtype=jnp.int32)
    page_of = token_index // page_size
    within = token_index % page_size
    multiple = jnp.zeros((row_count, token_count), jnp.float32)
    for column in range(page_table.shape[1]):
        same_page = page_table[:, column : column + 1] == page_of[None, :]
        seen = (column * page_size + within)[None, :] < private_length[:, None]
        multiple = multiple + (same_page & seen).astype(jnp.float32)
    present = multiple > 0.0
    head_rows = jnp.moveaxis(queries.reshape(row_count, KVH, group_size, HD), 1, 0)
    key_heads = jnp.moveaxis(pool_keys.reshape(token_count, KVH, HD), 1, 0)
    value_heads = jnp.moveaxis(pool_values.reshape(token_count, KVH, HD), 1, 0)

    def private_per_head(operands):
        query_head, key_head, value_head = operands
        scores = (
            jnp.einsum("rgd,td->rgt", query_head, key_head, preferred_element_type=jnp.float32)
            * scale
        )
        scores = jnp.where(present[:, None, :], scores, -1e30)
        largest = jnp.max(scores, axis=-1, keepdims=True)
        weights = jnp.exp(scores - largest)
        counted = weights * multiple[:, None, :]
        weight_sum = jnp.sum(counted, axis=-1)
        rounded = weights.astype(jnp.bfloat16).astype(jnp.float32) * multiple[:, None, :]
        summed = jnp.einsum(
            "rgt,td->rgd", rounded, value_head.astype(jnp.float32), precision=lax.Precision.HIGHEST
        )
        return (summed / weight_sum[..., None], largest[..., 0] + jnp.log(weight_sum))

    result, log_total = lax.map(private_per_head, (head_rows, key_heads, value_heads))
    return (jnp.moveaxis(result, 0, 1), jnp.moveaxis(log_total, 0, 1))


def per_device(
    queries,
    prefix_keys,
    prefix_values,
    pool_keys,
    pool_values,
    page_table,
    private_length,
    group_ids,
    live_rows,
    out_weight,
):
    devices = lax.axis_size("req")
    row_count = queries.shape[0]
    slot_count = 2 * row_count // devices
    group_size = H // KVH
    groups = group_ids[:, 0]
    row_order = jnp.arange(row_count, dtype=jnp.int32)
    same_group = (groups[:, None] == groups[None, :]) & (row_order[None, :] < row_order[:, None])
    group_rank = jnp.sum(same_group.astype(jnp.int32), axis=1)
    slot_place = groups * slot_count + group_rank
    matches = slot_place[None, :] == jnp.arange(devices * slot_count, dtype=jnp.int32)[:, None]
    spread = matches.astype(jnp.bfloat16)
    outgoing = jnp.dot(spread, queries, preferred_element_type=jnp.float32).astype(jnp.bfloat16)
    outgoing = outgoing.reshape(devices, slot_count, -1)
    slot_items = lax.all_to_all(outgoing, "req", split_axis=0, concat_axis=0, tiled=True)
    item_count = slot_items.shape[1]
    result, log_total = shared_prefix(
        slot_items.reshape(devices * item_count, -1), prefix_keys, prefix_values
    )
    result = result.reshape(devices, item_count, -1)
    log_total = log_total.reshape(devices, item_count, -1)
    result_back = lax.all_to_all(result, "req", split_axis=0, concat_axis=0, tiled=True)
    lse_returned = lax.all_to_all(log_total, "req", split_axis=0, concat_axis=0, tiled=True)
    gather_back = spread.T
    prefix_out = jnp.dot(
        gather_back,
        result_back.reshape(devices * slot_count, -1),
        preferred_element_type=jnp.float32,
    )
    prefix_out = prefix_out.reshape(row_count, KVH, group_size, HD)
    prefix_lse = jnp.dot(
        matches.T.astype(jnp.float32),
        lse_returned.reshape(devices * slot_count, -1),
        precision=lax.Precision.HIGHEST,
    )
    prefix_lse = prefix_lse.reshape(row_count, KVH, group_size)
    private_out, private_lse = private_part(
        queries, pool_keys, pool_values, page_table, private_length
    )
    largest = jnp.maximum(prefix_lse, private_lse)
    prefix_share = jnp.exp(prefix_lse - largest)
    private_share = jnp.exp(private_lse - largest)
    combined = (prefix_share[..., None] * prefix_out + private_share[..., None] * private_out) / (
        prefix_share + private_share
    )[..., None]
    attended = combined.reshape(row_count, -1).astype(jnp.bfloat16)
    is_live = row_order < live_rows[0]
    projected = jnp.dot(attended, out_weight, preferred_element_type=jnp.float32)
    return jnp.where(is_live[:, None], projected, 0.0).astype(jnp.bfloat16)


def solution(mesh):
    placed = (
        P("req", None),
        P("req", None),
        P("req", None),
        P("req", None, None),
        P("req", None, None),
        P("req", None),
        P("req"),
        P("req", None),
        P("req"),
        P(),
    )
    return jax.shard_map(
        per_device, mesh=mesh, in_specs=placed, out_specs=P("req", None), check_vma=False
    )
```

profile of v0, /device:TPU:0, one launch (start us, length us, event | category | flops | bytes accessed | tf_op | source)
XLA Modules:
  0.0 199.9 jit_solution(11651800434809078721)
XLA Ops:
  1.6 2.7 %fusion.49 = bf16[32,8,2560]{2,1,0:T(8,128)(2,1)} fusion(bf16[128,2560]{1,0:T(8,128)(2,1)} %param.14, s32[128]{0:T(128)S(1)} %multiply_add_fusion), kind=kOutput, calls=%fused_computation.50 | convolution fusion | flops 168460288 | bytes 1966592 | tf_op jit(solution)/shard_map/dot_general | solution.py:106
  4.3 7.3 %all-to-all-start = ((bf16[32,8,2560]{2,1,0:T(8,128)(2,1)}), bf16[32,8,2560]{2,1,0:T(8,128)(2,1)S(1)}, u32[]{:S(2)}, u32[]{:S(2)}) async-start(bf16[32,8,2560]{2,1,0:T(8,128)(2,1)} %fusion.49), calls=%async_computation | async-start | bytes 2621440 | tf_op jit(solution)/shard_map/all_to_all | solution.py:108
  12.7 7.8 %reshape.137 = bf16[2048,8,80]{2,1,0:T(8,128)(2,1)} reshape(bf16[128,16,640]{2,1,0:T(8,128)(2,1)} %param.17) | data formatting | bytes 5242880 | tf_op jit(solution)/shard_map/reshape | solution.py:59
  20.5 6.3 %copy.62 = bf16[8,2048,80]{1,2,0:T(8,128)(2,1)} copy(bf16[8,2048,80]{2,0,1:T(8,128)(2,1)} %bitcast.134) | data formatting | bytes 5242880
  26.8 7.8 %reshape.138 = bf16[2048,8,80]{2,1,0:T(8,128)(2,1)} reshape(bf16[128,16,640]{2,1,0:T(8,128)(2,1)} %param.18) | data formatting | bytes 5242880 | tf_op jit(solution)/shard_map/reshape | solution.py:60
  34.6 6.4 %copy.63 = bf16[8,2048,80]{1,2,0:T(8,128)(2,1)} copy(bf16[8,2048,80]{2,0,1:T(8,128)(2,1)} %bitcast.135) | data formatting | bytes 5242880
  43.7 2.7 %reshape_reshape.6 = bf16[256,8,4,80]{3,2,1,0:T(4,128)(2,1)S(1)} reshape(bf16[32,8,2560]{2,1,0:T(8,128)(2,1)S(1)} %all-to-all-done) | data formatting | bytes 2621440 | tf_op jit(solution)/shard_map/reshape;reshape | solution.py:25
  46.4 1.6 copy.57
  48.0 24.5 %while.26 = (s32[]{:T(128)}, bf16[8,256,4,80]{1,3,2,0:T(8,128)(2,1)}, f32[8,256,4]{1,2,0:T(4,128)S(1)}, bf16[8,256,4,80]{1,3,2,0:T(8,128)(2,1)S(1)}, bf16[8,256,...) while((s32[]{:T(128)}, bf16[8,256,4,80]{1,3,2,0:T(8,128)(2,1)}, f32[8,256,4]{1,2,0:T(4,128)S(1)}, ...), condition=%wide.region_4.5_spmd, body=%wide.region_1.4_spmd.sunk | while | flops 85539840 | bytes 3754065 | solution.py:37
  48.0 1.1 fusion.92
  49.3 1.8 fusion.94
  51.1 1.1 fusion.92
  52.4 1.8 fusion.94
  54.1 1.1 fusion.92
  55.4 1.8 fusion.94
  57.2 1.1 fusion.92
  58.5 1.8 fusion.94
  60.3 1.1 fusion.92
  61.6 1.8 fusion.94
  63.3 1.1 fusion.92
  64.6 1.7 fusion.94
  66.4 1.1 fusion.92
  67.7 1.8 fusion.94
  69.4 1.1 fusion.92
  70.7 1.8 fusion.94
  73.9 5.1 %all-to-all-start.1 = ((f32[32,1,256]{2,1,0:T(1,128)}), f32[32,1,256]{2,1,0:T(1,128)S(1)}, u32[]{:S(2)}, u32[]{:S(2)}) async-start(f32[32,1,256]{2,1,0:T(1,128)} %reshape.146), calls=%async_computation.1 | async-start | bytes 65536 | tf_op jit(solution)/shard_map/all_to_all | solution.py:116
  79.0 3.3 %copy.66 = bf16[256,8,4,80]{3,2,1,0:T(4,128)(2,1)S(1)} copy(bf16[256,8,4,80]{0,3,2,1:T(8,128)(2,1)} %bitcast.140) | data formatting | bytes 2621440 | tf_op jit(solution)/shard_map/convert_element_type | solution.py:38
  82.3 5.0 %convert_element_type.73 = bf16[32,8,2560]{2,1,0:T(8,128)(2,1)} reshape(bf16[256,8,4,80]{3,2,1,0:T(4,128)(2,1)S(1)} %copy.66) | data formatting | bytes 2621440 | tf_op jit(solution)/shard_map/convert_element_type | solution.py:38
  87.3 6.0 %all-to-all-start.2 = ((bf16[32,8,2560]{2,1,0:T(8,128)(2,1)}), bf16[32,8,2560]{2,1,0:T(8,128)(2,1)S(1)}, u32[]{:S(2)}, u32[]{:S(2)}) async-start(bf16[32,8,2560]{2,1,0:T(8,128)(2,1)} %convert_element_type.73), calls=%async_computation.2 | async-start | bytes 2621440 | tf_op jit(solution)/shard_map/all_to_all | solution.py:115
  93.4 94.2 %while.27 = (s32[]{:T(128)}, f32[8,128,4,80]{1,3,2,0:T(8,128)}, f32[8,128,4]{1,0,2:T(8,128)S(1)}, bf16[8,128,4,80]{1,3,2,0:T(8,128)(2,1)}, bf16[8,2048,80]{1,2,0...) while((s32[]{:T(128)}, f32[8,128,4,80]{1,3,2,0:T(8,128)}, ...), condition=%wide.region_8.9_spmd.clone.clone, body=%wide.region_5.8_spmd.clone.clone.sunk | while | flops 1199611392 | bytes 34556676 | solution.py:79
  93.4 1.6 broadcast_compare_fusion.2
  95.0 2.1 %fusion.97 = (f32[128,4]{0,1:T(4,128)S(1)}, f32[128,4,2048]{2,0,1:T(8,128)S(1)}) fusion(pred[128,2048]{1,0:T(8,128)(4,1)S(1)} %get-tuple-element.660, bf16[8,2048,80]{1,2,0:T(8,128)(2,1)} %get-tuple-element.741, s32[]{:T(128)} %get-tuple-element.711, bf16[8,128,4,80]{1,3,2,0:T(8,128)(2,1)} %get-tuple-element.740), kind=kOutput, calls=%fused_computation.25.clone.1 | convolution fusion | flops 170917376 | bytes 4869120 | tf_op jit(solution)/shard_map/while/body/eval_jaxpr/rgd,td->rgt/dot_general | solution.py:65
  97.1 1.2 multiply_reduce_fusion.2
  99.0 6.1 %fusion.98 = f32[8,128,4,80]{1,3,2,0:T(8,128)} fusion(f32[8,128,4,80]{1,3,2,0:T(8,128)} %get-tuple-element.712, s32[]{:T(128)} %get-tuple-element.711, f32[128,4,2048]{2,0,1:T(8,128)} %copy-done, f32[128,2048]{1,0:T(8,128)S(1)} %get-tuple-element.662, f32[128,4]{0,1:T(4,128)S(1)} %get-tuple-element.663, ...), kind=kOutput, calls=%fused_computation.34.clone.1 | convolution fusion | flops 1012965376 | bytes 6001664 | tf_op jit(solution)/shard_map/while/body/eval_jaxpr/rgt,td->rgd/dot_general | solution.py:74
  105.2 1.6 broadcast_compare_fusion.2
  106.8 2.0 %fusion.97 = (f32[128,4]{0,1:T(4,128)S(1)}, f32[128,4,2048]{2,0,1:T(8,128)S(1)}) fusion(pred[128,2048]{1,0:T(8,128)(4,1)S(1)} %get-tuple-element.660, bf16[8,2048,80]{1,2,0:T(8,128)(2,1)} %get-tuple-element.741, s32[]{:T(128)} %get-tuple-element.711, bf16[8,128,4,80]{1,3,2,0:T(8,128)(2,1)} %get-tuple-element.740), kind=kOutput, calls=%fused_computation.25.clone.1 | convolution fusion | flops 170917376 | bytes 4869120 | tf_op jit(solution)/shard_map/while/body/eval_jaxpr/rgd,td->rgt/dot_general | solution.py:65
  108.8 1.2 multiply_reduce_fusion.2
  110.8 6.1 %fusion.98 = f32[8,128,4,80]{1,3,2,0:T(8,128)} fusion(f32[8,128,4,80]{1,3,2,0:T(8,128)} %get-tuple-element.712, s32[]{:T(128)} %get-tuple-element.711, f32[128,4,2048]{2,0,1:T(8,128)} %copy-done, f32[128,2048]{1,0:T(8,128)S(1)} %get-tuple-element.662, f32[128,4]{0,1:T(4,128)S(1)} %get-tuple-element.663, ...), kind=kOutput, calls=%fused_computation.34.clone.1 | convolution fusion | flops 1012965376 | bytes 6001664 | tf_op jit(solution)/shard_map/while/body/eval_jaxpr/rgt,td->rgd/dot_general | solution.py:74
  116.9 1.6 broadcast_compare_fusion.2
  118.6 2.1 %fusion.97 = (f32[128,4]{0,1:T(4,128)S(1)}, f32[128,4,2048]{2,0,1:T(8,128)S(1)}) fusion(pred[128,2048]{1,0:T(8,128)(4,1)S(1)} %get-tuple-element.660, bf16[8,2048,80]{1,2,0:T(8,128)(2,1)} %get-tuple-element.741, s32[]{:T(128)} %get-tuple-element.711, bf16[8,128,4,80]{1,3,2,0:T(8,128)(2,1)} %get-tuple-element.740), kind=kOutput, calls=%fused_computation.25.clone.1 | convolution fusion | flops 170917376 | bytes 4869120 | tf_op jit(solution)/shard_map/while/body/eval_jaxpr/rgd,td->rgt/dot_general | solution.py:65
  120.6 1.2 multiply_reduce_fusion.2
  122.6 6.1 %fusion.98 = f32[8,128,4,80]{1,3,2,0:T(8,128)} fusion(f32[8,128,4,80]{1,3,2,0:T(8,128)} %get-tuple-element.712, s32[]{:T(128)} %get-tuple-element.711, f32[128,4,2048]{2,0,1:T(8,128)} %copy-done, f32[128,2048]{1,0:T(8,128)S(1)} %get-tuple-element.662, f32[128,4]{0,1:T(4,128)S(1)} %get-tuple-element.663, ...), kind=kOutput, calls=%fused_computation.34.clone.1 | convolution fusion | flops 1012965376 | bytes 6001664 | tf_op jit(solution)/shard_map/while/body/eval_jaxpr/rgt,td->rgd/dot_general | solution.py:74
  128.7 1.6 broadcast_compare_fusion.2
  130.3 2.1 %fusion.97 = (f32[128,4]{0,1:T(4,128)S(1)}, f32[128,4,2048]{2,0,1:T(8,128)S(1)}) fusion(pred[128,2048]{1,0:T(8,128)(4,1)S(1)} %get-tuple-element.660, bf16[8,2048,80]{1,2,0:T(8,128)(2,1)} %get-tuple-element.741, s32[]{:T(128)} %get-tuple-element.711, bf16[8,128,4,80]{1,3,2,0:T(8,128)(2,1)} %get-tuple-element.740), kind=kOutput, calls=%fused_computation.25.clone.1 | convolution fusion | flops 170917376 | bytes 4869120 | tf_op jit(solution)/shard_map/while/body/eval_jaxpr/rgd,td->rgt/dot_general | solution.py:65
  132.4 1.2 multiply_reduce_fusion.2
  134.4 6.1 %fusion.98 = f32[8,128,4,80]{1,3,2,0:T(8,128)} fusion(f32[8,128,4,80]{1,3,2,0:T(8,128)} %get-tuple-element.712, s32[]{:T(128)} %get-tuple-element.711, f32[128,4,2048]{2,0,1:T(8,128)} %copy-done, f32[128,2048]{1,0:T(8,128)S(1)} %get-tuple-element.662, f32[128,4]{0,1:T(4,128)S(1)} %get-tuple-element.663, ...), kind=kOutput, calls=%fused_computation.34.clone.1 | convolution fusion | flops 1012965376 | bytes 6001664 | tf_op jit(solution)/shard_map/while/body/eval_jaxpr/rgt,td->rgd/dot_general | solution.py:74
  140.5 1.6 broadcast_compare_fusion.2
  142.1 2.0 %fusion.97 = (f32[128,4]{0,1:T(4,128)S(1)}, f32[128,4,2048]{2,0,1:T(8,128)S(1)}) fusion(pred[128,2048]{1,0:T(8,128)(4,1)S(1)} %get-tuple-element.660, bf16[8,2048,80]{1,2,0:T(8,128)(2,1)} %get-tuple-element.741, s32[]{:T(128)} %get-tuple-element.711, bf16[8,128,4,80]{1,3,2,0:T(8,128)(2,1)} %get-tuple-element.740), kind=kOutput, calls=%fused_computation.25.clone.1 | convolution fusion | flops 170917376 | bytes 4869120 | tf_op jit(solution)/shard_map/while/body/eval_jaxpr/rgd,td->rgt/dot_general | solution.py:65
  144.2 1.2 multiply_reduce_fusion.2
  146.1 6.1 %fusion.98 = f32[8,128,4,80]{1,3,2,0:T(8,128)} fusion(f32[8,128,4,80]{1,3,2,0:T(8,128)} %get-tuple-element.712, s32[]{:T(128)} %get-tuple-element.711, f32[128,4,2048]{2,0,1:T(8,128)} %copy-done, f32[128,2048]{1,0:T(8,128)S(1)} %get-tuple-element.662, f32[128,4]{0,1:T(4,128)S(1)} %get-tuple-element.663, ...), kind=kOutput, calls=%fused_computation.34.clone.1 | convolution fusion | flops 1012965376 | bytes 6001664 | tf_op jit(solution)/shard_map/while/body/eval_jaxpr/rgt,td->rgd/dot_general | solution.py:74
  152.3 1.6 broadcast_compare_fusion.2
  153.9 2.1 %fusion.97 = (f32[128,4]{0,1:T(4,128)S(1)}, f32[128,4,2048]{2,0,1:T(8,128)S(1)}) fusion(pred[128,2048]{1,0:T(8,128)(4,1)S(1)} %get-tuple-element.660, bf16[8,2048,80]{1,2,0:T(8,128)(2,1)} %get-tuple-element.741, s32[]{:T(128)} %get-tuple-element.711, bf16[8,128,4,80]{1,3,2,0:T(8,128)(2,1)} %get-tuple-element.740), kind=kOutput, calls=%fused_computation.25.clone.1 | convolution fusion | flops 170917376 | bytes 4869120 | tf_op jit(solution)/shard_map/while/body/eval_jaxpr/rgd,td->rgt/dot_general | solution.py:65
  155.9 1.2 multiply_reduce_fusion.2
  157.9 6.1 %fusion.98 = f32[8,128,4,80]{1,3,2,0:T(8,128)} fusion(f32[8,128,4,80]{1,3,2,0:T(8,128)} %get-tuple-element.712, s32[]{:T(128)} %get-tuple-element.711, f32[128,4,2048]{2,0,1:T(8,128)} %copy-done, f32[128,2048]{1,0:T(8,128)S(1)} %get-tuple-element.662, f32[128,4]{0,1:T(4,128)S(1)} %get-tuple-element.663, ...), kind=kOutput, calls=%fused_computation.34.clone.1 | convolution fusion | flops 1012965376 | bytes 6001664 | tf_op jit(solution)/shard_map/while/body/eval_jaxpr/rgt,td->rgd/dot_general | solution.py:74
  164.0 1.6 broadcast_compare_fusion.2
  165.6 2.0 %fusion.97 = (f32[128,4]{0,1:T(4,128)S(1)}, f32[128,4,2048]{2,0,1:T(8,128)S(1)}) fusion(pred[128,2048]{1,0:T(8,128)(4,1)S(1)} %get-tuple-element.660, bf16[8,2048,80]{1,2,0:T(8,128)(2,1)} %get-tuple-element.741, s32[]{:T(128)} %get-tuple-element.711, bf16[8,128,4,80]{1,3,2,0:T(8,128)(2,1)} %get-tuple-element.740), kind=kOutput, calls=%fused_computation.25.clone.1 | convolution fusion | flops 170917376 | bytes 4869120 | tf_op jit(solution)/shard_map/while/body/eval_jaxpr/rgd,td->rgt/dot_general | solution.py:65
  167.7 1.2 multiply_reduce_fusion.2
  169.7 6.1 %fusion.98 = f32[8,128,4,80]{1,3,2,0:T(8,128)} fusion(f32[8,128,4,80]{1,3,2,0:T(8,128)} %get-tuple-element.712, s32[]{:T(128)} %get-tuple-element.711, f32[128,4,2048]{2,0,1:T(8,128)} %copy-done, f32[128,2048]{1,0:T(8,128)S(1)} %get-tuple-element.662, f32[128,4]{0,1:T(4,128)S(1)} %get-tuple-element.663, ...), kind=kOutput, calls=%fused_computation.34.clone.1 | convolution fusion | flops 1012965376 | bytes 6001664 | tf_op jit(solution)/shard_map/while/body/eval_jaxpr/rgt,td->rgd/dot_general | solution.py:74
  175.8 1.6 broadcast_compare_fusion.2
  177.4 2.1 %fusion.97 = (f32[128,4]{0,1:T(4,128)S(1)}, f32[128,4,2048]{2,0,1:T(8,128)S(1)}) fusion(pred[128,2048]{1,0:T(8,128)(4,1)S(1)} %get-tuple-element.660, bf16[8,2048,80]{1,2,0:T(8,128)(2,1)} %get-tuple-element.741, s32[]{:T(128)} %get-tuple-element.711, bf16[8,128,4,80]{1,3,2,0:T(8,128)(2,1)} %get-tuple-element.740), kind=kOutput, calls=%fused_computation.25.clone.1 | convolution fusion | flops 170917376 | bytes 4869120 | tf_op jit(solution)/shard_map/while/body/eval_jaxpr/rgd,td->rgt/dot_general | solution.py:65
  179.5 1.2 multiply_reduce_fusion.2
  181.5 6.1 %fusion.98 = f32[8,128,4,80]{1,3,2,0:T(8,128)} fusion(f32[8,128,4,80]{1,3,2,0:T(8,128)} %get-tuple-element.712, s32[]{:T(128)} %get-tuple-element.711, f32[128,4,2048]{2,0,1:T(8,128)} %copy-done, f32[128,2048]{1,0:T(8,128)S(1)} %get-tuple-element.662, f32[128,4]{0,1:T(4,128)S(1)} %get-tuple-element.663, ...), kind=kOutput, calls=%fused_computation.34.clone.1 | convolution fusion | flops 1012965376 | bytes 6001664 | tf_op jit(solution)/shard_map/while/body/eval_jaxpr/rgt,td->rgd/dot_general | solution.py:74
  190.5 1.8 fusion.53
  192.4 7.5 %fusion.50 = bf16[128,2560]{1,0:T(8,128)(2,1)} fusion(bf16[128,2560]{0,1:T(8,128)(2,1)S(1)} %bitcast.139, bf16[2560,2560]{1,0:T(8,128)(2,1)} %param.23, pred[128]{0:T(512)(128)(4,1)S(1)} %iota_compare_fusion.3), kind=kOutput, calls=%fused_computation.52 | convolution fusion | flops 1678376960 | bytes 14418048 | tf_op jit(solution)/shard_map/dot_general | solution.py:141
  (92 shorter events, 16.3 us)
Async XLA Ops:
  0.0 11.6 %copy-start.1 = (bf16[128,2560]{1,0:T(8,128)(2,1)S(1)}, bf16[128,2560]{1,0:T(8,128)(2,1)}, u32[]{:S(2)}) copy-start(bf16[128,2560]{1,0:T(8,128)(2,1)} %param.14) | copy-start | bytes 1966084
  4.3 39.4 %all-to-all-start = ((bf16[32,8,2560]{2,1,0:T(8,128)(2,1)}), bf16[32,8,2560]{2,1,0:T(8,128)(2,1)S(1)}, u32[]{:S(2)}, u32[]{:S(2)}) async-start(bf16[32,8,2560]{2,1,0:T(8,128)(2,1)} %fusion.49), calls=%async_computation | async-start | bytes 2621440 | tf_op jit(solution)/shard_map/all_to_all | solution.py:108
  34.6 6.4 %copy-start.2 = (bf16[256,640]{1,0:T(8,128)(2,1)S(1)}, bf16[256,640]{1,0:T(8,128)(2,1)}, u32[]{:S(2)}) copy-start(bf16[256,640]{1,0:T(8,128)(2,1)} %param.15) | copy-start | bytes 983044
  34.6 7.4 %copy-start.3 = (bf16[256,640]{1,0:T(8,128)(2,1)S(1)}, bf16[256,640]{1,0:T(8,128)(2,1)}, u32[]{:S(2)}) copy-start(bf16[256,640]{1,0:T(8,128)(2,1)} %param.16) | copy-start | bytes 983044
  34.6 8.3 %copy-start.5 = (s32[128,8]{0,1:T(8,128)S(1)}, s32[128,8]{0,1:T(8,128)}, u32[]{:S(2)}) copy-start(s32[128,8]{0,1:T(8,128)} %param.19) | copy-start | bytes 12292
  73.9 13.5 %all-to-all-start.1 = ((f32[32,1,256]{2,1,0:T(1,128)}), f32[32,1,256]{2,1,0:T(1,128)S(1)}, u32[]{:S(2)}, u32[]{:S(2)}) async-start(f32[32,1,256]{2,1,0:T(1,128)} %reshape.146), calls=%async_computation.1 | async-start | bytes 65536 | tf_op jit(solution)/shard_map/all_to_all | solution.py:116
  82.3 11.1 %copy-start.4 = (s32[128]{0:T(128)S(1)}, s32[128]{0:T(128)}, u32[]{:S(2)}) copy-start(s32[128]{0:T(128)} %param.20) | copy-start | bytes 1540
  82.3 11.1 %copy-start.6 = (f32[8,128,4]{1,0,2:T(8,128)S(1)}, f32[8,128,4]{1,0,2:T(8,128)}, u32[]{:S(2)}) copy-start(f32[8,128,4]{1,0,2:T(8,128)} %custom-call.3) | copy-start | bytes 49156
  87.3 102.6 %all-to-all-start.2 = ((bf16[32,8,2560]{2,1,0:T(8,128)(2,1)}), bf16[32,8,2560]{2,1,0:T(8,128)(2,1)S(1)}, u32[]{:S(2)}, u32[]{:S(2)}) async-start(bf16[32,8,2560]{2,1,0:T(8,128)(2,1)} %convert_element_type.73), calls=%async_computation.2 | async-start | bytes 2621440 | tf_op jit(solution)/shard_map/all_to_all | solution.py:115
  97.1 1.9 copy-start
  108.8 1.9 copy-start
  120.6 1.9 copy-start
  132.4 1.9 copy-start
  144.2 1.9 copy-start
  155.9 1.9 copy-start
  167.7 1.9 copy-start
  179.5 1.9 copy-start
where the time goes:
time: 202 us; the launch traced here: 200 us
  matrix products  101 us (50%)
  local copies, waits for them, and re-layouts  52.5 us (26%)
  other arithmetic  26.4 us (13%)
  starting transfers between devices  18.4 us (9%)
    dot_general x8, matrix products, private_per_head(): jnp.einsum('rgt,td->rgd', rounded, value_head.astype(jnp.float32), precis...  49 us
    unnamed x19, local copies, waits for them, and re-layouts  16.4 us
    dot_general x8, matrix products, private_per_head(): jnp.einsum('rgd,td->rgt', query_head, key_head, preferred_element_type=jn...  16.4 us
    dot_general x8, matrix products, weigh_values(): jnp.einsum(spec, weights.astype(jnp.bfloat16), values, preferred_element_...  14 us
    gt x8, other arithmetic, private_part(): present = multiple > 0.0  12.9 us
    reduce_sum x8, other arithmetic, private_per_head(): weight_sum = jnp.sum(counted, axis=-1)  9.79 us
    dot_general x8, matrix products, shared_per_head(): jnp.einsum('rgd,td->rgt', query_head, key_head, preferred_element_type=jn...  9.02 us
    convert_element_type x2, local copies, waits for them, and re-layouts, shared_prefix(): jnp.moveaxis(result, 0, 1).reshape(row_count, H * HD).astype(jnp.bfloat16)  8.33 us
  transfers between devices with their start and end apart: 3, of which 1 were waited for; matrix products, arithmetic and copies ran while one was open for 65% of the time, Pallas kernels for 0%

commit v1 on v0

v1 whole, which is shorter than its diff:
```python
import functools
import math

import jax
import jax.numpy as jnp
from jax import lax
from jax.experimental import pallas as pl
from jax.experimental.pallas import tpu as pltpu
from jax.sharding import PartitionSpec as P

H = 32
KVH = 8
HD = 80
GROUP = H // KVH
LANES = 128
WIN = 256
SCALE = HD ** (-0.5) * math.log2(math.e)
LN2 = math.log(2.0)
NEVER = -1e30
VMEM_LIMIT = 60 * 1024 * 1024


def window(start, width):
    base = min(start // LANES * LANES, width - WIN)
    return base, start - base


def iota(shape, axis):
    return lax.broadcasted_iota(jnp.int32, shape, axis)


def moved(block, source, target):
    shift = (target - source) % WIN
    if shift:
        block = pltpu.roll(block, shift, 1)
    lane = iota(block.shape, 1)
    return jnp.where((lane >= target) & (lane < target + HD), block, 0.0)


def padded_queries(q_ref, head, key_offset):
    base, offset = window(head * HD, q_ref.shape[1])
    block = q_ref[:, base : base + WIN].astype(jnp.float32)
    return moved(block, offset, key_offset).astype(jnp.bfloat16)


def as_row(column):
    n = column.shape[0]
    same = iota((n, n), 0) == iota((n, n), 1)
    return jnp.sum(jnp.where(same, column, 0), axis=0, keepdims=True)


def slots_of(groups, half, slot_count):
    n = groups.shape[0]
    row = as_row(groups)
    earlier = iota((n, n), 1) < iota((n, n), 0)
    rank = jnp.sum(jnp.where((groups == row) & earlier, 1, 0), axis=1, keepdims=True)
    upper = jnp.where(groups >= half, 1, 0)
    return (groups - upper * half) * slot_count + rank, upper


def place_kernel(half, slot_count, side_ref, groups_ref, q_ref, own_ref, other_ref):
    n = q_ref.shape[0]
    slot, upper = slots_of(groups_ref[...], half, slot_count)
    slot_row, upper_row = as_row(slot), as_row(upper)
    hit = slot_row == iota((n, n), 0)
    side = side_ref[0]
    for out_ref, wanted in ((own_ref, side), (other_ref, 1 - side)):
        spread = jnp.where(hit & (upper_row == wanted), 1.0, 0.0).astype(jnp.bfloat16)
        for base in range(0, q_ref.shape[1], 512):
            cols = slice(base, base + 512)
            out_ref[:, cols] = jnp.dot(
                spread, q_ref[:, cols], preferred_element_type=jnp.float32
            ).astype(jnp.bfloat16)


def place(queries, group_ids, side, half, slot_count):
    shape = jax.ShapeDtypeStruct(queries.shape, queries.dtype)
    return pl.pallas_call(
        functools.partial(place_kernel, half, slot_count),
        out_shape=(shape, shape),
        in_specs=[
            pl.BlockSpec(memory_space=pltpu.SMEM),
            pl.BlockSpec(memory_space=pltpu.VMEM),
            pl.BlockSpec(memory_space=pltpu.VMEM),
        ],
        out_specs=(pl.BlockSpec(memory_space=pltpu.VMEM),) * 2,
        compiler_params=pltpu.CompilerParams(vmem_limit_bytes=VMEM_LIMIT),
        cost_estimate=pl.CostEstimate(
            flops=4 * 128 * 128 * 2560, bytes_accessed=3 * 128 * 2560 * 2, transcendentals=0
        ),
        name="place",
    )(side, group_ids, queries)


def prefix_kernel(q_ref, k_ref, v_ref, out_ref, acc_ref):
    n, width = q_ref.shape
    acc_ref[...] = jnp.zeros_like(acc_ref)
    lane = iota((n, LANES), 1)
    lse = jnp.zeros((n, LANES), jnp.float32)
    for k in range(KVH):
        base, key_offset = window(k * HD, k_ref.shape[1])
        keys = k_ref[:, base : base + WIN]
        values = v_ref[:, base : base + WIN]
        for g in range(GROUP):
            head = k * GROUP + g
            q = padded_queries(q_ref, head, key_offset)
            scores = lax.dot_general(
                q, keys, (((1,), (1,)), ((), ())), preferred_element_type=jnp.float32
            )
            scores = scores * SCALE
            top = jnp.max(scores, axis=1, keepdims=True)
            weights = jnp.exp2(scores - top)
            total = jnp.sum(weights, axis=1, keepdims=True)
            summed = jnp.dot(
                weights.astype(jnp.bfloat16), values, preferred_element_type=jnp.float32
            )
            to, offset = window(head * HD, width)
            acc_ref[:, to : to + WIN] += moved(summed / total, key_offset, offset)
            lse = jnp.where(lane == head, (top + jnp.log2(total)) * LN2, lse)
    out_ref[:, :width] = acc_ref[...].astype(jnp.bfloat16)
    packed = jnp.zeros((n, LANES), jnp.float32)
    for part in range(3):
        piece = lse.astype(jnp.bfloat16).astype(jnp.float32)
        lse = lse - piece
        packed += pltpu.roll(piece, part * H, 1) if part else piece
    out_ref[:, width:] = packed.astype(jnp.bfloat16)


def prefix_part(rows, keys, values):
    n, width = rows.shape
    return pl.pallas_call(
        prefix_kernel,
        out_shape=jax.ShapeDtypeStruct((n, width + LANES), jnp.bfloat16),
        in_specs=[pl.BlockSpec(memory_space=pltpu.VMEM)] * 3,
        out_specs=pl.BlockSpec(memory_space=pltpu.VMEM),
        scratch_shapes=[pltpu.VMEM((n, width), jnp.float32)],
        compiler_params=pltpu.CompilerParams(vmem_limit_bytes=VMEM_LIMIT),
        cost_estimate=pl.CostEstimate(
            flops=4 * n * 256 * width, bytes_accessed=4 * n * width * 2, transcendentals=n * 256 * H
        ),
        name="prefix",
    )(rows, keys, values)


def private_bias(pages, lengths, token_count, page_size):
    n, most = pages.shape
    page_count = token_count // page_size
    page = iota((n, page_count), 1)
    full = jnp.zeros((n, page_count), jnp.float32)
    partial = jnp.zeros((n, page_count), jnp.float32)
    for j in range(most):
        same = pages[:, j : j + 1] == page
        whole = lengths >= (j + 1) * page_size
        some = (lengths > j * page_size) & (lengths < (j + 1) * page_size)
        full += jnp.where(same & whole, 1.0, 0.0)
        partial += jnp.where(same & some, 1.0, 0.0)
    token = iota((page_count, token_count), 1)
    first = iota((page_count, token_count), 0) * page_size
    expand = jnp.where((token >= first) & (token < first + page_size), 1.0, 0.0).astype(jnp.bfloat16)
    full = jnp.dot(full.astype(jnp.bfloat16), expand, preferred_element_type=jnp.float32)
    partial = jnp.dot(partial.astype(jnp.bfloat16), expand, preferred_element_type=jnp.float32)
    within = iota((n, token_count), 1) % page_size
    seen = within < lengths % page_size
    multiple = full + jnp.where(seen, partial, 0.0)
    return jnp.where(multiple > 0.0, jnp.log2(jnp.maximum(multiple, 1.0)), NEVER)


def private_kernel(
    first_head, heads, page_size, q_ref, k_ref, v_ref, pages_ref, lengths_ref,
    out_ref, lse_ref, qs_ref, bias_ref, sum_ref, acc_ref
):
    n = q_ref.shape[0]
    tokens, key_width = k_ref.shape
    bias_ref[...] = private_bias(pages_ref[...], lengths_ref[...], tokens, page_size)
    for i in range(heads):
        k = first_head + i
        _, key_offset = window(k * HD, key_width)
        for g in range(GROUP):
            qs_ref[i * GROUP + g] = padded_queries(q_ref, k * GROUP + g, key_offset)
    lane = iota((n, LANES), 1)

    def one(i, lse):
        k = first_head + i // GROUP
        base = pl.multiple_of(jnp.minimum(k * HD // LANES * LANES, key_width - WIN), LANES)
        scores = lax.dot_general(
            qs_ref[i],
            k_ref[:, pl.ds(base, WIN)],
            (((1,), (1,)), ((), ())),
            preferred_element_type=jnp.float32,
        )
        scores = scores * SCALE + bias_ref[...]
        top = jnp.max(scores, axis=1, keepdims=True)
        weights = jnp.exp2(scores - top)
        total = jnp.sum(weights, axis=1, keepdims=True)
        summed = jnp.dot(
            weights.astype(jnp.bfloat16),
            v_ref[:, pl.ds(base, WIN)],
            preferred_element_type=jnp.float32,
        )
        sum_ref[i] = summed / total
        return jnp.where(lane == i, (top + jnp.log2(total)) * LN2, lse)

    lse_ref[...] = lax.fori_loop(0, heads * GROUP, one, jnp.zeros((n, LANES), jnp.float32))
    acc_ref[...] = jnp.zeros_like(acc_ref)
    for i in range(heads):
        _, key_offset = window((first_head + i) * HD, key_width)
        for g in range(GROUP):
            to, offset = window((i * GROUP + g) * HD, acc_ref.shape[1])
            acc_ref[:, to : to + WIN] += moved(sum_ref[i * GROUP + g], key_offset, offset)
    out_ref[...] = acc_ref[...]


def private_part(queries, keys, values, page_table, lengths, page_size, first_head, heads):
    n = queries.shape[0]
    tokens = keys.shape[0]
    width = heads * GROUP * HD
    return pl.pallas_call(
        functools.partial(private_kernel, first_head, heads, page_size),
        out_shape=(
            jax.ShapeDtypeStruct((n, width), jnp.float32),
            jax.ShapeDtypeStruct((n, LANES), jnp.float32),
        ),
        in_specs=[pl.BlockSpec(memory_space=pltpu.VMEM)] * 5,
        out_specs=(pl.BlockSpec(memory_space=pltpu.VMEM),) * 2,
        scratch_shapes=[
            pltpu.VMEM((heads * GROUP, n, WIN), jnp.bfloat16),
            pltpu.VMEM((n, tokens), jnp.float32),
            pltpu.VMEM((heads * GROUP, n, WIN), jnp.float32),
            pltpu.VMEM((n, width), jnp.float32),
        ],
        compiler_params=pltpu.CompilerParams(vmem_limit_bytes=VMEM_LIMIT),
        cost_estimate=pl.CostEstimate(
            flops=4 * n * tokens * heads * GROUP * WIN,
            bytes_accessed=2 * tokens * 640 * 2,
            transcendentals=n * tokens * heads * GROUP,
        ),
        name="private",
    )(queries, keys, values, page_table, lengths)


def expand_heads(share, width):
    n = share.shape[0]
    lane = iota((n, LANES), 1)
    share = jnp.where(lane < H, share, 0.0)
    high = share.astype(jnp.bfloat16).astype(jnp.float32)
    both = (high + pltpu.roll(share - high, H, 1)).astype(jnp.bfloat16)
    row = iota((LANES, width), 0)
    head = jnp.where(row >= H, row - H, row)
    first = head * HD
    column = iota((LANES, width), 1)
    spread = (row < 2 * H) & (column >= first) & (column < first + HD)
    return jnp.dot(
        both, jnp.where(spread, 1.0, 0.0).astype(jnp.bfloat16), preferred_element_type=jnp.float32
    )


def finish_kernel(
    half, slot_count, chunk, side_ref, live_ref, groups_ref, own_ref, other_ref,
    low_ref, high_ref, low_lse_ref, high_lse_ref, w_hbm, out_ref, w_ref, sems
):
    n, width = out_ref.shape
    copies = []
    for i in range(width // chunk):
        cols = pl.ds(i * chunk, chunk)
        copy = pltpu.make_async_copy(w_hbm.at[:, cols], w_ref.at[:, cols], sems.at[i])
        copy.start()
        copies.append(copy)
    slot, upper = slots_of(groups_ref[...], half, slot_count)
    hit = slot == iota((n, n), 1)
    side = side_ref[0]
    own = jnp.where(hit & (upper == side), 1.0, 0.0).astype(jnp.bfloat16)
    other = jnp.where(hit & (upper != side), 1.0, 0.0).astype(jnp.bfloat16)
    pick = jnp.concatenate([own, other], axis=1)

    def picked(cols):
        both = jnp.concatenate([own_ref[:, cols], other_ref[:, cols]], axis=0)
        return jnp.dot(pick, both, preferred_element_type=jnp.float32)

    pieces = picked(slice(width, width + LANES))
    lane = iota((n, LANES), 1)
    prefix_lse = (
        pieces + pltpu.roll(pieces, LANES - H, 1) + pltpu.roll(pieces, LANES - 2 * H, 1)
    )
    prefix_lse = jnp.where(lane < H, prefix_lse, 0.0)
    private_lse = jnp.where(
        lane < H // 2, low_lse_ref[...], pltpu.roll(high_lse_ref[...], H // 2, 1)
    )
    private_lse = jnp.where(lane < H, private_lse, 0.0)
    top = jnp.maximum(prefix_lse, private_lse)
    a, b = jnp.exp(prefix_lse - top), jnp.exp(private_lse - top)
    prefix_share = expand_heads(a / (a + b), width)
    private_share = expand_heads(b / (a + b), width)
    private = jnp.concatenate([low_ref[...], high_ref[...]], axis=1)
    attended = prefix_share * picked(slice(0, width)) + private_share * private
    attended = attended.astype(jnp.bfloat16)
    is_live = iota((n, 1), 0) < live_ref[0]
    for i, copy in enumerate(copies):
        copy.wait()
        cols = slice(i * chunk, (i + 1) * chunk)
        projected = jnp.dot(attended, w_ref[:, cols], preferred_element_type=jnp.float32)
        out_ref[:, cols] = jnp.where(is_live, projected, 0.0).astype(out_ref.dtype)


def finish(side, live, group_ids, own, other, low, high, low_lse, high_lse, weight, half, slot_count):
    n = own.shape[0]
    width = weight.shape[1]
    chunk = 512
    vmem = pl.BlockSpec(memory_space=pltpu.VMEM)
    smem = pl.BlockSpec(memory_space=pltpu.SMEM)
    return pl.pallas_call(
        functools.partial(finish_kernel, half, slot_count, chunk),
        out_shape=jax.ShapeDtypeStruct((n, width), jnp.bfloat16),
        in_specs=[smem, smem] + [vmem] * 7 + [pl.BlockSpec(memory_space=pl.ANY)],
        out_specs=vmem,
        scratch_shapes=[
            pltpu.VMEM(weight.shape, weight.dtype),
            pltpu.SemaphoreType.DMA((width // chunk,)),
        ],
        compiler_params=pltpu.CompilerParams(vmem_limit_bytes=VMEM_LIMIT),
        cost_estimate=pl.CostEstimate(
            flops=2 * n * width * width, bytes_accessed=2 * width * width, transcendentals=0
        ),
        name="finish",
    )(side, live, group_ids, own, other, low, high, low_lse, high_lse, weight)


def per_device(
    queries,
    prefix_keys,
    prefix_values,
    pool_keys,
    pool_values,
    page_table,
    private_length,
    group_ids,
    live_rows,
    out_weight,
):
    devices = lax.axis_size("req")
    half = devices // 2
    row_count, width = queries.shape
    slot_count = 2 * row_count // devices
    page_size = pool_keys.shape[1]
    halves = [list(range(half)), list(range(half, devices))]
    across = [(i, (i + half) % devices) for i in range(devices)]
    side = (lax.axis_index("req") // half).astype(jnp.int32).reshape(1)

    far_keys = lax.ppermute(prefix_keys, "req", across)
    far_values = lax.ppermute(prefix_values, "req", across)
    own, other = place(queries, group_ids, side, half, slot_count)

    def exchange(rows):
        blocks = rows.reshape(half, slot_count, rows.shape[1])
        blocks = lax.all_to_all(
            blocks, "req", split_axis=0, concat_axis=0, tiled=True, axis_index_groups=halves
        )
        return blocks.reshape(rows.shape)

    own_back = exchange(prefix_part(exchange(own), prefix_keys, prefix_values))
    other_back = exchange(prefix_part(exchange(other), far_keys, far_values))

    lengths = private_length.reshape(row_count, 1)
    flat_keys = pool_keys.reshape(-1, pool_keys.shape[2])
    flat_values = pool_values.reshape(-1, pool_values.shape[2])
    private = functools.partial(
        private_part, queries, flat_keys, flat_values, page_table, lengths, page_size
    )
    low, low_lse = private(0, KVH // 2)
    high, high_lse = private(KVH // 2, KVH // 2)
    return finish(
        side, live_rows, group_ids, own_back, other_back, low, high, low_lse, high_lse,
        out_weight, half, slot_count,
    )


def solution(mesh):
    placed = (
        P("req", None),
        P("req", None),
        P("req", None),
        P("req", None, None),
        P("req", None, None),
        P("req", None),
        P("req"),
        P("req", None),
        P("req"),
        P(),
    )
    return jax.shard_map(
        per_device, mesh=mesh, in_specs=placed, out_specs=P("req", None), check_vma=False
    )
```

time: 202 us -> 152 us (0.75)
  matrix products: 101 us -> 0 us
  Pallas kernels: 0 us -> 82.6 us
  local copies, waits for them, and re-layouts: 52.5 us -> 4.54 us
  waiting for transfers between devices: 0.78 us -> 29.3 us
  other arithmetic: 26.4 us -> 0 us
  blocking collectives: 0 us -> 18.3 us
  starting transfers between devices: 18.4 us -> 15.6 us
    dot_general x36 -> x0, matrix products: 101 us -> none  [the longest x8 49 us: private_per_head(): jnp.einsum('rgt,td->rgd', rounded, value_head.astype(jnp.float32), precis...]
    pallas_call x0 -> x6, Pallas kernels: none -> 82.6 us  [the longest x2 47.8 us: private_part(): pl.pallas_call(functools.partial(private_kernel, first_head, heads, page_...]
    ppermute x0 -> x2, waiting for transfers between devices: none -> 29 us  [the longest x1 16.7 us: per_device(): far_values = lax.ppermute(prefix_values, 'req', across)]
    all_to_all x0 -> x1, blocking collectives: none -> 18.3 us  [exchange(): lax.all_to_all(blocks, 'req', split_axis=0, concat_axis=0, tiled=True, ax...]
    reshape x2 -> x1, local copies, waits for them, and re-layouts: 15.7 us -> 0.73 us  [per_device(): lengths = private_length.reshape(row_count, 1)]
    gt x8 -> x0, other arithmetic: 12.9 us -> none  [private_part(): present = multiple > 0.0]
    unnamed x19 -> x20, local copies, waits for them, and re-layouts: 16.4 us -> 3.81 us
    reduce_sum x17 -> x0, other arithmetic: 12 us -> none  [the longest x8 9.79 us: private_per_head(): weight_sum = jnp.sum(counted, axis=-1)]
  transfers between devices with their start and end apart: 3 -> 5, of which waited for: 1 -> 3; matrix products, arithmetic and copies ran while one was open for 65% -> 1% of each run, Pallas kernels for 0% -> 47%
where the time goes in v1:
time: 152 us; the launch traced here: 151 us
  Pallas kernels  82.6 us (54%)
  waiting for transfers between devices  29.3 us (19%)
  blocking collectives  18.3 us (12%)
  starting transfers between devices  15.6 us (10%)
  local copies, waits for them, and re-layouts  4.54 us (3%)
    pallas_call x2, Pallas kernels, private_part(): pl.pallas_call(functools.partial(private_kernel, first_head, heads, page_...  47.8 us
    pallas_call x2, Pallas kernels, prefix_part(): pl.pallas_call(prefix_kernel, out_shape=jax.ShapeDtypeStruct((n, width +...  24 us
    all_to_all x1, blocking collectives, exchange(): lax.all_to_all(blocks, 'req', split_axis=0, concat_axis=0, tiled=True, ax...  18.3 us
    ppermute x1, waiting for transfers between devices, per_device(): far_values = lax.ppermute(prefix_values, 'req', across)  16.7 us
    all_to_all x3, starting transfers between devices, exchange(): lax.all_to_all(blocks, 'req', split_axis=0, concat_axis=0, tiled=True, ax...  12.6 us
    ppermute x1, waiting for transfers between devices, per_device(): far_keys = lax.ppermute(prefix_keys, 'req', across)  12.3 us
    pallas_call x1, Pallas kernels, finish(): pl.pallas_call(functools.partial(finish_kernel, half, slot_count, chunk),...  8.01 us
    unnamed x20, local copies, waits for them, and re-layouts  3.81 us
  transfers between devices with their start and end apart: 5, of which 3 were waited for; matrix products, arithmetic and copies ran while one was open for 1% of the time, Pallas kernels for 47%

profile of v1, /device:TPU:0, one launch (start us, length us, event | category | flops | bytes accessed | tf_op | source)
XLA Modules:
  0.0 151.3 jit_solution(7800457577577130966)
XLA Ops:
  0.0 0.0 copy-start.3
  0.0 0.0 copy-start.4
  0.0 1.4 copy.16.groups_ref
  1.5 2.8 %place.1 = (bf16[128,2560]{1,0:T(8,128)(2,1)}, bf16[128,2560]{1,0:T(8,128)(2,1)}) custom-call(s32[1]{0:T(128)} %bitcast.side_ref, s32[128,1]{1,0:T(8,128)} %copy.16.groups_ref, bf16[128,2560]{1,0:T(8,128)(2,1)} %q_ref.5), custom_call_target="tpu_custom_call" | custom-call | flops 167772160 | bytes 1966080 | tf_op jit(solution)/shard_map/place/pallas_call | solution.py:78
  4.2 18.3 %all_to_all.20 = bf16[16,8,2560]{2,1,0:T(8,128)(2,1)} all-to-all(bf16[16,8,2560]{2,1,0:T(8,128)(2,1)} %bitcast.19), channel_id=1, replica_groups={{0,1,2,3,4,5,6,7,8,9,10,11,12,13,14,15},{16,17,18,19,20,21,22,23,24,25,..., dimensions={0} | all-to-all | bytes 1310720 | tf_op jit(solution)/shard_map/all_to_all | solution.py:354
  22.6 3.6 %all-to-all-start = ((bf16[16,8,2560]{2,1,0:T(8,128)(2,1)}), bf16[16,8,2560]{2,1,0:T(8,128)(2,1)S(1)}, u32[]{:S(2)}, u32[]{:S(2)}) async-start(bf16[16,8,2560]{2,1,0:T(8,128)(2,1)} %bitcast.18), calls=%async_computation | async-start | bytes 1310720 | tf_op jit(solution)/shard_map/all_to_all | solution.py:354
  26.2 0.0 copy-done.3
  26.2 2.7 %collective-permute-start = (bf16[256,640]{1,0:T(8,128)(2,1)S(1)}, bf16[256,640]{1,0:T(8,128)(2,1)S(1)}, u32[]{:S(2)}, u32[]{:S(2)}) collective-permute-start(bf16[256,640]{1,0:T(8,128)(2,1)S(1)} %copy-done.3), channel_id=1, source_target_pairs={{0,16},{1,17},{2,18},{3,19},{4,20},{5,21},{6,22},{7,23},{8,24},{9,... | collective-permute-start | bytes 983048 | tf_op jit(solution)/shard_map/ppermute | solution.py:348
  28.9 0.0 copy-done.4
  28.9 0.3 collective-permute-start.1
  29.2 12.3 %collective-permute-done.k_ref = bf16[256,640]{1,0:T(8,128)(2,1)S(1)} collective-permute-done((bf16[256,640]{1,0:T(8,128)(2,1)S(1)}, bf16[256,640]{1,0:T(8,128)(2,1)S(1)}, u32[]{:S(2)}, u32[]{:S(2)}) %collective-permute-start) | collective-permute-done | bytes 327712 | tf_op jit(solution)/shard_map/ppermute | solution.py:348
  41.5 0.0 copy-start.5
  41.5 16.7 %collective-permute-done.1.v_ref = bf16[256,640]{1,0:T(8,128)(2,1)S(1)} collective-permute-done((bf16[256,640]{1,0:T(8,128)(2,1)S(1)}, bf16[256,640]{1,0:T(8,128)(2,1)S(1)}, u32[]{:S(2)}, u32[]{:S(2)}) %collective-permute-start.1) | collective-permute-done | bytes 327712 | tf_op jit(solution)/shard_map/ppermute | solution.py:349
  58.2 0.0 copy-start.6
  58.2 0.0 copy-done.5
  58.2 0.7 copy-done.6
  58.9 12.0 %prefix.3 = bf16[128,2688]{1,0:T(8,128)(2,1)} custom-call(bf16[128,2560]{1,0:T(8,128)(2,1)} %bitcast.17, bf16[256,640]{1,0:T(8,128)(2,1)} %copy-done.5, bf16[256,640]{1,0:T(8,128)(2,1)} %copy-done.6), custom_call_target="tpu_custom_call" | custom-call | flops 335544320 | bytes 2621440 | tf_op jit(solution)/shard_map/prefix/pallas_call | solution.py:131
  70.9 0.0 copy-start.7
  70.9 0.0 copy-start.8
  70.9 0.0 all-to-all-done
  70.9 0.0 copy-start.2
  71.0 4.2 %all-to-all-start.3 = ((bf16[16,8,2688]{2,1,0:T(8,128)(2,1)}), bf16[16,8,2688]{2,1,0:T(8,128)(2,1)S(1)}, u32[]{:S(2)}, u32[]{:S(2)}) async-start(bf16[16,8,2688]{2,1,0:T(8,128)(2,1)} %bitcast.15), calls=%async_computation.3 | async-start | bytes 1376256 | tf_op jit(solution)/shard_map/all_to_all | solution.py:354
  75.1 0.0 copy-done.2
  75.1 12.0 %prefix.2 = bf16[128,2688]{1,0:T(8,128)(2,1)} custom-call(bf16[128,2560]{1,0:T(8,128)(2,1)} %bitcast.16, bf16[256,640]{1,0:T(8,128)(2,1)} %k_ref.1, bf16[256,640]{1,0:T(8,128)(2,1)} %v_ref.1), custom_call_target="tpu_custom_call" | custom-call | flops 335544320 | bytes 2621440 | tf_op jit(solution)/shard_map/prefix/pallas_call | solution.py:131
  87.2 0.3 all-to-all-done.3
  87.4 0.0 copy-start
  87.4 4.8 %all-to-all-start.1 = ((bf16[16,8,2688]{2,1,0:T(8,128)(2,1)}), bf16[16,8,2688]{2,1,0:T(8,128)(2,1)S(1)}, u32[]{:S(2)}, u32[]{:S(2)}) async-start(bf16[16,8,2688]{2,1,0:T(8,128)(2,1)} %bitcast.14), calls=%async_computation.1 | async-start | bytes 1376256 | tf_op jit(solution)/shard_map/all_to_all | solution.py:354
  92.3 0.0 copy-done.7
  92.3 0.7 copy.12.pages_ref
  93.0 0.0 copy-done.8
  93.0 0.7 copy.13.lengths_ref
  94.4 23.8 %private.2 = (f32[128,1280]{1,0:T(8,128)}, f32[128,128]{1,0:T(8,128)}) custom-call(bf16[128,2560]{1,0:T(8,128)(2,1)} %q_ref.5, bf16[2048,640]{1,0:T(8,128)(2,1)} %bitcast.21, bf16[2048,640]{1,0:T(8,128)(2,1)} %bitcast.23, s32[128,8]{1,0:T(8,128)} %copy.12.pages_ref, s32[128,1]{1,0:T(8,128)} %copy.13.lengths_ref), custom_call_target="tpu_custom_call" | custom-call | flops 4294967296 | bytes 5242880 | tf_op jit(solution)/shard_map/private/pallas_call | solution.py:217
  118.2 0.0 copy-done
  118.2 24.0 %private.3 = (f32[128,1280]{1,0:T(8,128)}, f32[128,128]{1,0:T(8,128)}) custom-call(bf16[128,2560]{1,0:T(8,128)(2,1)} %q_ref.5, bf16[2048,640]{1,0:T(8,128)(2,1)} %bitcast.22, bf16[2048,640]{1,0:T(8,128)(2,1)} %bitcast.24, s32[128,8]{1,0:T(8,128)} %copy.12.pages_ref, s32[128,1]{1,0:T(8,128)} %copy.13.lengths_ref), custom_call_target="tpu_custom_call" | custom-call | flops 4294967296 | bytes 5242880 | tf_op jit(solution)/shard_map/private/pallas_call | solution.py:217
  142.2 0.0 all-to-all-done.1
  142.2 0.0 copy-start.1
  142.2 0.9 copy-done.1
  143.1 8.0 %finish.1 = bf16[128,2560]{1,0:T(8,128)(2,1)} custom-call(s32[1]{0:T(128)} %bitcast.side_ref, s32[1]{0:T(128)S(6)} %copy.17.live_ref, s32[128,1]{1,0:T(8,128)} %copy.16.groups_ref, bf16[128,2688]{1,0:T(8,128)(2,1)} %bitcast.13, bf16[128,2688]{1,0:T(8,128)(2,1)} %bitcast.12, f32[128,1280]{1,0:T(8,128)} %get-tuple-element.13.low_ref, ...), custom_call_target="tpu_custom_call" | custom-call | flops 1677721600 | bytes 13107200 | tf_op jit(solution)/shard_map/finish/pallas_call | solution.py:310
Async XLA Ops:
  0.0 26.2 %copy-start.3 = (bf16[256,640]{1,0:T(8,128)(2,1)S(1)}, bf16[256,640]{1,0:T(8,128)(2,1)}, u32[]{:S(2)}) copy-start(bf16[256,640]{1,0:T(8,128)(2,1)} %k_ref.1) | copy-start | bytes 983044
  0.0 28.9 %copy-start.4 = (bf16[256,640]{1,0:T(8,128)(2,1)S(1)}, bf16[256,640]{1,0:T(8,128)(2,1)}, u32[]{:S(2)}) copy-start(bf16[256,640]{1,0:T(8,128)(2,1)} %v_ref.1) | copy-start | bytes 983044
  22.6 48.4 %all-to-all-start = ((bf16[16,8,2560]{2,1,0:T(8,128)(2,1)}), bf16[16,8,2560]{2,1,0:T(8,128)(2,1)S(1)}, u32[]{:S(2)}, u32[]{:S(2)}) async-start(bf16[16,8,2560]{2,1,0:T(8,128)(2,1)} %bitcast.18), calls=%async_computation | async-start | bytes 1310720 | tf_op jit(solution)/shard_map/all_to_all | solution.py:354
  26.2 15.3 %collective-permute-start = (bf16[256,640]{1,0:T(8,128)(2,1)S(1)}, bf16[256,640]{1,0:T(8,128)(2,1)S(1)}, u32[]{:S(2)}, u32[]{:S(2)}) collective-permute-start(bf16[256,640]{1,0:T(8,128)(2,1)S(1)} %copy-done.3), channel_id=1, source_target_pairs={{0,16},{1,17},{2,18},{3,19},{4,20},{5,21},{6,22},{7,23},{8,24},{9,... | collective-permute-start | bytes 983048 | tf_op jit(solution)/shard_map/ppermute | solution.py:348
  28.9 29.3 %collective-permute-start.1 = (bf16[256,640]{1,0:T(8,128)(2,1)S(1)}, bf16[256,640]{1,0:T(8,128)(2,1)S(1)}, u32[]{:S(2)}, u32[]{:S(2)}) collective-permute-start(bf16[256,640]{1,0:T(8,128)(2,1)S(1)} %copy-done.4), channel_id=1, source_target_pairs={{0,16},{1,17},{2,18},{3,19},{4,20},{5,21},{6,22},{7,23},{8,24},{9,... | collective-permute-start | bytes 983048 | tf_op jit(solution)/shard_map/ppermute | solution.py:349
  41.5 16.7 %copy-start.5 = (bf16[256,640]{1,0:T(8,128)(2,1)}, bf16[256,640]{1,0:T(8,128)(2,1)S(1)}, u32[]{:S(2)}) copy-start(bf16[256,640]{1,0:T(8,128)(2,1)S(1)} %collective-permute-done.k_ref) | copy-start | bytes 983044
  58.2 0.7 copy-start.6
  70.9 21.3 %copy-start.7 = (s32[128,8]{0,1:T(8,128)S(1)}, s32[128,8]{0,1:T(8,128)}, u32[]{:S(2)}) copy-start(s32[128,8]{0,1:T(8,128)} %param.15) | copy-start | bytes 12292
  70.9 22.1 %copy-start.8 = (s32[128]{0:T(128)S(1)}, s32[128]{0:T(128)}, u32[]{:S(2)}) copy-start(s32[128]{0:T(128)} %param.16) | copy-start | bytes 1540
  70.9 4.2 %copy-start.2 = (bf16[16,8,2560]{2,1,0:T(8,128)(2,1)}, bf16[16,8,2560]{2,1,0:T(8,128)(2,1)S(1)}, u32[]{:S(2)}) copy-start(bf16[16,8,2560]{2,1,0:T(8,128)(2,1)S(1)} %all-to-all-done) | copy-start | bytes 1966084
  71.0 16.5 %all-to-all-start.3 = ((bf16[16,8,2688]{2,1,0:T(8,128)(2,1)}), bf16[16,8,2688]{2,1,0:T(8,128)(2,1)S(1)}, u32[]{:S(2)}, u32[]{:S(2)}) async-start(bf16[16,8,2688]{2,1,0:T(8,128)(2,1)} %bitcast.15), calls=%async_computation.3 | async-start | bytes 1376256 | tf_op jit(solution)/shard_map/all_to_all | solution.py:354
  87.4 30.8 %copy-start = (bf16[16,8,2688]{2,1,0:T(8,128)(2,1)}, bf16[16,8,2688]{2,1,0:T(8,128)(2,1)S(1)}, u32[]{:S(2)}) copy-start(bf16[16,8,2688]{2,1,0:T(8,128)(2,1)S(1)} %all-to-all-done.3) | copy-start | bytes 2064388
  87.4 54.8 %all-to-all-start.1 = ((bf16[16,8,2688]{2,1,0:T(8,128)(2,1)}), bf16[16,8,2688]{2,1,0:T(8,128)(2,1)S(1)}, u32[]{:S(2)}, u32[]{:S(2)}) async-start(bf16[16,8,2688]{2,1,0:T(8,128)(2,1)} %bitcast.14), calls=%async_computation.1 | async-start | bytes 1376256 | tf_op jit(solution)/shard_map/all_to_all | solution.py:354
  142.2 0.9 copy-start.1

commit v2 on v1

v2 whole, which is shorter than its diff:
```python
import functools
import math

import jax
import jax.numpy as jnp
from jax import lax
from jax.experimental import pallas as pl
from jax.experimental.pallas import tpu as pltpu
from jax.sharding import PartitionSpec as P

H = 32
KVH = 8
HD = 80
GROUP = H // KVH
LANES = 128
WIN = 256
SCALE = HD ** (-0.5) * math.log2(math.e)
LN2 = math.log(2.0)
NEVER = -1e30
VMEM = pl.BlockSpec(memory_space=pltpu.VMEM)
SMEM = pl.BlockSpec(memory_space=pltpu.SMEM)
ANY = pl.BlockSpec(memory_space=pl.ANY)


def window(start, width):
    base = min(start // LANES * LANES, width - WIN)
    return base, start - base


def iota(shape, axis):
    return lax.broadcasted_iota(jnp.int32, shape, axis)


def params(mib):
    return pltpu.CompilerParams(vmem_limit_bytes=mib * 1024 * 1024)


def transpose_into(target, source):
    rows, cols = source.shape
    for c in range(0, cols, LANES):
        for r in range(0, rows, LANES):
            target[c : c + LANES, r : r + LANES] = source[r : r + LANES, c : c + LANES].T


def as_column(row):
    n = row.shape[1]
    same = iota((n, n), 0) == iota((n, n), 1)
    return jnp.sum(jnp.where(same, row, 0), axis=1, keepdims=True)


def slots_of(groups, half, slot_count):
    n = groups.shape[1]
    earlier = iota((n, n), 0) < iota((n, n), 1)
    same = (as_column(groups) == groups) & earlier
    rank = jnp.sum(jnp.where(same, 1, 0), axis=0, keepdims=True)
    upper = jnp.where(groups >= half, 1, 0)
    return (groups - upper * half) * slot_count + rank, upper


def place_kernel(half, slot_count, side_ref, groups_ref, q_ref, own_ref, other_ref):
    n = q_ref.shape[0]
    slot, upper = slots_of(groups_ref[...], half, slot_count)
    hit = slot == iota((n, n), 0)
    side = side_ref[0]
    own = jnp.where(hit & (upper == side), 1.0, 0.0).astype(jnp.bfloat16)
    other = jnp.where(hit & (upper != side), 1.0, 0.0).astype(jnp.bfloat16)
    spread = jnp.concatenate([own, other], axis=0)
    for base in range(0, q_ref.shape[1], 512):
        cols = slice(base, base + 512)
        both = jnp.dot(spread, q_ref[:, cols], preferred_element_type=jnp.float32)
        both = both.astype(jnp.bfloat16)
        own_ref[:, cols] = both[:n]
        other_ref[:, cols] = both[n:]


def place(queries, groups, side, half, slot_count):
    n, width = queries.shape
    shape = jax.ShapeDtypeStruct(queries.shape, queries.dtype)
    return pl.pallas_call(
        functools.partial(place_kernel, half, slot_count),
        out_shape=(shape, shape),
        in_specs=[SMEM, VMEM, VMEM],
        out_specs=(VMEM, VMEM),
        compiler_params=params(16),
        cost_estimate=pl.CostEstimate(
            flops=4 * n * n * width, bytes_accessed=6 * n * width, transcendentals=0
        ),
        name="place",
    )(side, groups, queries)


def place_queries(qs_ref, i, qt_ref, k, key_width):
    n = qt_ref.shape[1]
    _, first = window(k * HD, key_width)
    if first:
        qs_ref[i, :first] = jnp.zeros((first, GROUP * n), jnp.bfloat16)
    if first + HD < WIN:
        qs_ref[i, first + HD :] = jnp.zeros((WIN - first - HD, GROUP * n), jnp.bfloat16)
    for g in range(GROUP):
        row = (i * GROUP + g) * HD
        qs_ref[i, first : first + HD, g * n : (g + 1) * n] = qt_ref[row : row + HD]


def prefix_kernel(q_ref, k_ref, v_ref, after_ref, out_ref, qt_ref, vt_ref, qs_ref, ot_ref, lse_ref):
    del after_ref
    n, width = q_ref.shape
    key_width = k_ref.shape[1]
    transpose_into(qt_ref, q_ref)
    transpose_into(vt_ref, v_ref)
    for k in range(KVH):
        place_queries(qs_ref, k, qt_ref, k, key_width)
    for k in range(KVH):
        base, _ = window(k * HD, key_width)
        scores = jnp.dot(
            k_ref[:, base : base + WIN], qs_ref[k], preferred_element_type=jnp.float32
        )
        scores = scores * SCALE
        top = jnp.max(scores, axis=0, keepdims=True)
        weights = jnp.exp2(scores - top)
        total = jnp.sum(weights, axis=0, keepdims=True)
        summed = jnp.dot(
            vt_ref[k * HD : (k + 1) * HD],
            weights.astype(jnp.bfloat16),
            preferred_element_type=jnp.float32,
        )
        result = (summed * (1.0 / total)).astype(jnp.bfloat16)
        lse = (top + jnp.log2(total)) * LN2
        for g in range(GROUP):
            head = k * GROUP + g
            ot_ref[head * HD : (head + 1) * HD] = result[:, g * n : (g + 1) * n]
            lse_ref[head : head + 1] = lse[:, g * n : (g + 1) * n]
    transpose_into(out_ref.at[:, :width], ot_ref)
    lse = lse_ref[...]
    high = lse.astype(jnp.bfloat16).astype(jnp.float32)
    middle = (lse - high).astype(jnp.bfloat16).astype(jnp.float32)
    pieces = jnp.concatenate([high, middle, lse - high - middle, jnp.zeros_like(lse)], axis=0)
    out_ref[:, width:] = pieces.T.astype(jnp.bfloat16)


def prefix_part(rows, keys, values, after):
    n, width = rows.shape
    tokens, key_width = keys.shape
    return pl.pallas_call(
        prefix_kernel,
        out_shape=jax.ShapeDtypeStruct((n, width + LANES), jnp.bfloat16),
        in_specs=[VMEM, VMEM, VMEM, ANY],
        out_specs=VMEM,
        scratch_shapes=[
            pltpu.VMEM((width, n), jnp.bfloat16),
            pltpu.VMEM((key_width, tokens), jnp.bfloat16),
            pltpu.VMEM((KVH, WIN, GROUP * n), jnp.bfloat16),
            pltpu.VMEM((width, n), jnp.bfloat16),
            pltpu.VMEM((H, n), jnp.float32),
        ],
        compiler_params=params(24),
        cost_estimate=pl.CostEstimate(
            flops=4 * n * 256 * width, bytes_accessed=4 * n * width * 2, transcendentals=n * 256 * H
        ),
        name="prefix",
    )(rows, keys, values, after)


def fill_bias(bias_ref, pages, lengths, page_size):
    most, n = pages.shape
    page_count = bias_ref.shape[0] // page_size
    page = iota((page_count, n), 0)
    full = jnp.zeros((page_count, n), jnp.float32)
    partial = jnp.zeros((page_count, n), jnp.float32)
    for j in range(most):
        same = pages[j : j + 1] == page
        whole = lengths >= (j + 1) * page_size
        some = (lengths > j * page_size) & (lengths < (j + 1) * page_size)
        full += jnp.where(same & whole, 1.0, 0.0)
        partial += jnp.where(same & some, 1.0, 0.0)
    seen = jnp.where(iota((page_size, n), 0) < lengths % page_size, 1.0, 0.0)
    for p in range(page_count):
        multiple = full[p : p + 1] + seen * partial[p : p + 1]
        bias_ref[p * page_size : (p + 1) * page_size] = jnp.where(
            multiple > 0.0, jnp.log2(jnp.maximum(multiple, 1.0)), NEVER
        )


def private_kernel(
    first_head, heads, page_size, q_ref, k_ref, v_ref, pages_ref, lengths_ref, after_ref,
    out_ref, lse_ref, qt_ref, vt_ref, qs_ref, bias_ref, ot_ref, lses_ref,
    scores_a, scores_b, top_a, top_b, weights_ref
):
    del after_ref
    n = q_ref.shape[0]
    tokens, key_width = k_ref.shape
    rows = GROUP * n
    tile = 256
    query0 = first_head * GROUP * HD
    transpose_into(qt_ref, q_ref.at[:, query0 : query0 + heads * GROUP * HD])
    value0 = first_head * HD // LANES * LANES
    value1 = -(-(first_head + heads) * HD // LANES) * LANES
    transpose_into(vt_ref.at[value0:value1], v_ref.at[:, value0:value1])
    fill_bias(bias_ref, pages_ref[...], lengths_ref[...], page_size)
    for i in range(heads):
        place_queries(qs_ref, i, qt_ref, first_head + i, key_width)

    def score(i, scores_ref, top_ref):
        k = first_head + i
        base = pl.multiple_of(jnp.minimum(k * HD // LANES * LANES, key_width - WIN), LANES)
        top = None
        for t in range(0, tokens, tile):
            scores = jnp.dot(
                k_ref[t : t + tile, pl.ds(base, WIN)],
                qs_ref[i],
                preferred_element_type=jnp.float32,
            )
            bias = bias_ref[t : t + tile]
            scores = scores * SCALE + jnp.concatenate([bias] * GROUP, axis=1)
            scores_ref[t : t + tile] = scores
            highest = jnp.max(scores.reshape(tile // 8, 8, rows), axis=0)
            top = highest if top is None else jnp.maximum(top, highest)
        top_ref[...] = top

    def weigh(i, scores_ref, top_ref, lses):
        top = jnp.max(top_ref[...], axis=0, keepdims=True)
        total = jnp.zeros((8, rows), jnp.float32)
        for t in range(0, tokens, tile):
            weights = jnp.exp2(scores_ref[t : t + tile] - top)
            total += jnp.sum(weights.reshape(tile // 8, 8, rows), axis=0)
            weights_ref[t : t + tile] = weights.astype(jnp.bfloat16)
        total = jnp.sum(total, axis=0, keepdims=True)
        values = vt_ref[pl.ds(pl.multiple_of((first_head + i) * HD, 16), HD)]
        summed = jnp.dot(values, weights_ref[...], preferred_element_type=jnp.float32)
        result = summed * (1.0 / total)
        lse = (top + jnp.log2(total)) * LN2
        row = iota(lses.shape, 0)
        for g in range(GROUP):
            head = i * GROUP + g
            ot_ref[pl.ds(pl.multiple_of(head * HD, 16), HD)] = result[:, g * n : (g + 1) * n]
            lses = jnp.where(row == head, lse[:, g * n : (g + 1) * n], lses)
        return lses

    score(0, scores_a, top_a)

    def two(j, lses):
        i = 2 * j
        score(i + 1, scores_b, top_b)
        lses = weigh(i, scores_a, top_a, lses)
        score(jnp.minimum(i + 2, heads - 1), scores_a, top_a)
        return weigh(i + 1, scores_b, top_b, lses)

    lses_ref[...] = jnp.zeros_like(lses_ref)
    lses_ref[:H] = lax.fori_loop(0, heads // 2, two, jnp.zeros((H, n), jnp.float32))
    lse_ref[...] = lses_ref[...].T
    transpose_into(out_ref, ot_ref)


def private_part(queries, keys, values, pages, lengths, after, page_size, first_head, heads):
    n = queries.shape[0]
    tokens, key_width = keys.shape
    width = heads * GROUP * HD
    return pl.pallas_call(
        functools.partial(private_kernel, first_head, heads, page_size),
        out_shape=(
            jax.ShapeDtypeStruct((n, width), jnp.float32),
            jax.ShapeDtypeStruct((n, LANES), jnp.float32),
        ),
        in_specs=[VMEM] * 5 + [ANY],
        out_specs=(VMEM, VMEM),
        scratch_shapes=[
            pltpu.VMEM((width, n), jnp.bfloat16),
            pltpu.VMEM((key_width, tokens), jnp.bfloat16),
            pltpu.VMEM((heads, WIN, GROUP * n), jnp.bfloat16),
            pltpu.VMEM((tokens, n), jnp.float32),
            pltpu.VMEM((width, n), jnp.float32),
            pltpu.VMEM((LANES, n), jnp.float32),
            pltpu.VMEM((tokens, GROUP * n), jnp.float32),
            pltpu.VMEM((tokens, GROUP * n), jnp.float32),
            pltpu.VMEM((8, GROUP * n), jnp.float32),
            pltpu.VMEM((8, GROUP * n), jnp.float32),
            pltpu.VMEM((tokens, GROUP * n), jnp.bfloat16),
        ],
        compiler_params=params(36),
        cost_estimate=pl.CostEstimate(
            flops=4 * n * tokens * heads * GROUP * WIN,
            bytes_accessed=4 * tokens * key_width,
            transcendentals=n * tokens * heads * GROUP,
        ),
        name="private",
    )(queries, keys, values, pages, lengths, after)


def expand_heads(share, width):
    n = share.shape[0]
    lane = iota((n, LANES), 1)
    share = jnp.where(lane < H, share, 0.0)
    high = share.astype(jnp.bfloat16).astype(jnp.float32)
    both = (high + pltpu.roll(share - high, H, 1)).astype(jnp.bfloat16)
    row = iota((LANES, width), 0)
    head = jnp.where(row >= H, row - H, row)
    first = head * HD
    column = iota((LANES, width), 1)
    spread = (row < 2 * H) & (column >= first) & (column < first + HD)
    return jnp.dot(
        both, jnp.where(spread, 1.0, 0.0).astype(jnp.bfloat16), preferred_element_type=jnp.float32
    )


def finish_kernel(
    half, slot_count, chunk, side_ref, live_ref, groups_ref, own_ref, other_ref,
    low_ref, high_ref, low_lse_ref, high_lse_ref, w_hbm, out_ref, w_ref, sems
):
    n, width = out_ref.shape
    copies = []
    for i in range(width // chunk):
        cols = pl.ds(i * chunk, chunk)
        copy = pltpu.make_async_copy(w_hbm.at[:, cols], w_ref.at[:, cols], sems.at[i])
        copy.start()
        copies.append(copy)
    slot, upper = slots_of(groups_ref[...], half, slot_count)
    slot, upper = as_column(slot), as_column(upper)
    hit = slot == iota((n, n), 1)
    side = side_ref[0]
    own = jnp.where(hit & (upper == side), 1.0, 0.0).astype(jnp.bfloat16)
    other = jnp.where(hit & (upper != side), 1.0, 0.0).astype(jnp.bfloat16)
    pick = jnp.concatenate([own, other], axis=1)

    def picked(cols):
        both = jnp.concatenate([own_ref[:, cols], other_ref[:, cols]], axis=0)
        return jnp.dot(pick, both, preferred_element_type=jnp.float32)

    pieces = picked(slice(width, width + LANES))
    lane = iota((n, LANES), 1)
    prefix_lse = (
        pieces + pltpu.roll(pieces, LANES - H, 1) + pltpu.roll(pieces, LANES - 2 * H, 1)
    )
    prefix_lse = jnp.where(lane < H, prefix_lse, 0.0)
    private_lse = jnp.where(
        lane < H // 2, low_lse_ref[...], pltpu.roll(high_lse_ref[...], H // 2, 1)
    )
    private_lse = jnp.where(lane < H, private_lse, 0.0)
    top = jnp.maximum(prefix_lse, private_lse)
    a, b = jnp.exp(prefix_lse - top), jnp.exp(private_lse - top)
    prefix_share = expand_heads(a / (a + b), width)
    private_share = expand_heads(b / (a + b), width)
    private = jnp.concatenate([low_ref[...], high_ref[...]], axis=1)
    attended = prefix_share * picked(slice(0, width)) + private_share * private
    attended = attended.astype(jnp.bfloat16)
    is_live = iota((n, 1), 0) < live_ref[0]
    for i, copy in enumerate(copies):
        copy.wait()
        cols = slice(i * chunk, (i + 1) * chunk)
        projected = jnp.dot(attended, w_ref[:, cols], preferred_element_type=jnp.float32)
        out_ref[:, cols] = jnp.where(is_live, projected, 0.0).astype(out_ref.dtype)


def finish(side, live, groups, own, other, low, high, low_lse, high_lse, weight, half, slot_count):
    n = own.shape[0]
    width = weight.shape[1]
    chunk = 512
    return pl.pallas_call(
        functools.partial(finish_kernel, half, slot_count, chunk),
        out_shape=jax.ShapeDtypeStruct((n, width), jnp.bfloat16),
        in_specs=[SMEM, SMEM] + [VMEM] * 7 + [ANY],
        out_specs=VMEM,
        scratch_shapes=[
            pltpu.VMEM(weight.shape, weight.dtype),
            pltpu.SemaphoreType.DMA((width // chunk,)),
        ],
        compiler_params=params(32),
        cost_estimate=pl.CostEstimate(
            flops=2 * n * width * width, bytes_accessed=2 * width * width, transcendentals=0
        ),
        name="finish",
    )(side, live, groups, own, other, low, high, low_lse, high_lse, weight)


def per_device(
    queries,
    prefix_keys,
    prefix_values,
    pool_keys,
    pool_values,
    page_table,
    private_length,
    group_ids,
    live_rows,
    out_weight,
):
    devices = lax.axis_size("req")
    half = devices // 2
    row_count, width = queries.shape
    slot_count = 2 * row_count // devices
    page_size = pool_keys.shape[1]
    halves = [list(range(half)), list(range(half, devices))]
    across = [(i, (i + half) % devices) for i in range(devices)]
    side = (lax.axis_index("req") // half).astype(jnp.int32).reshape(1)

    groups = group_ids.reshape(1, row_count)
    lengths = private_length.reshape(1, row_count)
    pages = page_table.T
    flat_keys = pool_keys.reshape(-1, pool_keys.shape[2])
    flat_values = pool_values.reshape(-1, pool_values.shape[2])

    def exchange(rows):
        blocks = rows.reshape(half, slot_count, rows.shape[1])
        blocks = lax.all_to_all(
            blocks, "req", split_axis=0, concat_axis=0, tiled=True, axis_index_groups=halves
        )
        return blocks.reshape(rows.shape)

    far_keys = lax.ppermute(prefix_keys, "req", across)
    far_values = lax.ppermute(prefix_values, "req", across)
    own, other = place(queries, groups, side, half, slot_count)
    own_rows, other_rows = exchange(own), exchange(other)
    private = functools.partial(
        private_part, queries, flat_keys, flat_values, pages, lengths
    )
    low, low_lse = private(own, page_size, 0, KVH // 2)
    own_out = prefix_part(own_rows, prefix_keys, prefix_values, low_lse)
    own_back = exchange(own_out)
    other_out = prefix_part(other_rows, far_keys, far_values, own_out)
    other_back = exchange(other_out)
    high, high_lse = private(other_out, page_size, KVH // 2, KVH // 2)
    return finish(
        side, live_rows, groups, own_back, other_back, low, high, low_lse, high_lse,
        out_weight, half, slot_count,
    )


def solution(mesh):
    placed = (
        P("req", None),
        P("req", None),
        P("req", None),
        P("req", None, None),
        P("req", None, None),
        P("req", None),
        P("req"),
        P("req", None),
        P("req"),
        P(),
    )
    return jax.shard_map(
        per_device, mesh=mesh, in_specs=placed, out_specs=P("req", None), check_vma=False
    )
```

time: 152 us -> 109 us (0.72)
  Pallas kernels: 82.6 us -> 30 us
  local copies, waits for them, and re-layouts: 4.54 us -> 13.5 us
    pallas_call x2, Pallas kernels: 47.8 us -> 15.2 us  [private_part(): pl.pallas_call(functools.partial(private_kernel, first_head, heads, page_...]
    pallas_call x2, Pallas kernels: 24 us -> 7.88 us  [prefix_part(): pl.pallas_call(prefix_kernel, out_shape=jax.ShapeDtypeStruct((n, width +...]
    unnamed x20 -> x30, local copies, waits for them, and re-layouts: 3.81 us -> 13.5 us
    pallas_call x1, Pallas kernels: 8.01 us -> 5.49 us  [finish(): pl.pallas_call(functools.partial(finish_kernel, half, slot_count, chunk),...]
  transfers between devices with their start and end apart: 5 -> 5, of which waited for: 3 -> 3; matrix products, arithmetic and copies ran while one was open for 1% -> 0% of each run, Pallas kernels for 47% -> 21%
where the time goes in v2:
time: 109 us; the launch traced here: 108 us
  Pallas kernels  30 us (28%)
  waiting for transfers between devices  29.7 us (27%)
  blocking collectives  18 us (17%)
  starting transfers between devices  15.7 us (14%)
  local copies, waits for them, and re-layouts  13.5 us (12%)
    all_to_all x1, blocking collectives, exchange(): lax.all_to_all(blocks, 'req', split_axis=0, concat_axis=0, tiled=True, ax...  18 us
    ppermute x1, waiting for transfers between devices, per_device(): far_values = lax.ppermute(prefix_values, 'req', across)  16.5 us
    pallas_call x2, Pallas kernels, private_part(): pl.pallas_call(functools.partial(private_kernel, first_head, heads, page_...  15.2 us
    unnamed x30, local copies, waits for them, and re-layouts  13.5 us
    all_to_all x3, starting transfers between devices, exchange(): lax.all_to_all(blocks, 'req', split_axis=0, concat_axis=0, tiled=True, ax...  12.7 us
    ppermute x1, waiting for transfers between devices, per_device(): far_keys = lax.ppermute(prefix_keys, 'req', across)  12.6 us
    pallas_call x2, Pallas kernels, prefix_part(): pl.pallas_call(prefix_kernel, out_shape=jax.ShapeDtypeStruct((n, width +...  7.88 us
    pallas_call x1, Pallas kernels, finish(): pl.pallas_call(functools.partial(finish_kernel, half, slot_count, chunk),...  5.49 us
  transfers between devices with their start and end apart: 5, of which 3 were waited for; matrix products, arithmetic and copies ran while one was open for 0% of the time, Pallas kernels for 21%

profile of v2, /device:TPU:0, one launch (start us, length us, event | category | flops | bytes accessed | tf_op | source)
XLA Modules:
  0.0 107.9 jit_solution(4900526881525867059)
XLA Ops:
  0.0 0.0 copy-start.14
  0.0 0.0 copy-start.13
  0.0 0.0 copy-start.1
  0.0 1.1 %copy-done.1 = bf16[128,2560]{1,0:T(8,128)(2,1)S(1)} copy-done((bf16[128,2560]{1,0:T(8,128)(2,1)S(1)}, bf16[128,2560]{1,0:T(8,128)(2,1)}, u32[]{:S(2)}) %copy-start.1) | copy-done | bytes 655384
  1.1 0.0 copy-start.7
  1.1 0.7 copy-done.7
  1.8 0.0 copy-start.2
  1.8 1.4 %place.1 = (bf16[128,2560]{1,0:T(8,128)(2,1)S(1)}, bf16[128,2560]{1,0:T(8,128)(2,1)}) custom-call(s32[1]{0:T(128)} %bitcast.side_ref, s32[1,128]{1,0:T(1,128)S(1)} %bitcast.19, bf16[128,2560]{1,0:T(8,128)(2,1)S(1)} %copy-done.1), custom_call_target="tpu_custom_call" | custom-call | flops 167772160 | bytes 1966080 | tf_op jit(solution)/shard_map/place/pallas_call | solution.py:79
  3.2 18.0 %all_to_all.20 = bf16[16,8,2560]{2,1,0:T(8,128)(2,1)S(1)} all-to-all(bf16[16,8,2560]{2,1,0:T(8,128)(2,1)S(1)} %bitcast.18), channel_id=1, replica_groups={{0,1,2,3,4,5,6,7,8,9,10,11,12,13,14,15},{16,17,18,19,20,21,22,23,24,25,..., dimensions={0} | all-to-all | bytes 1310720 | tf_op jit(solution)/shard_map/all_to_all | solution.py:402
  21.2 3.6 %all-to-all-start.2 = ((bf16[16,8,2560]{2,1,0:T(8,128)(2,1)}), bf16[16,8,2560]{2,1,0:T(8,128)(2,1)S(1)}, u32[]{:S(2)}, u32[]{:S(2)}) async-start(bf16[16,8,2560]{2,1,0:T(8,128)(2,1)} %bitcast.10), calls=%async_computation.2 | async-start | bytes 1310720 | tf_op jit(solution)/shard_map/all_to_all | solution.py:402
  24.8 0.0 copy-done.14
  24.9 0.0 copy-done.13
  24.9 0.0 copy-done.2
  24.9 0.0 copy-start.9
  24.9 1.7 %copy-done.9 = bf16[128,16,640]{2,1,0:T(8,128)(2,1)S(1)} copy-done((bf16[128,16,640]{2,1,0:T(8,128)(2,1)S(1)}, bf16[128,16,640]{2,1,0:T(8,128)(2,1)}, u32[]{:S(2)}) %copy-start.9) | copy-done | bytes 2621464
  26.6 0.0 copy-start.11
  26.6 1.7 %copy-done.11 = bf16[128,16,640]{2,1,0:T(8,128)(2,1)S(1)} copy-done((bf16[128,16,640]{2,1,0:T(8,128)(2,1)S(1)}, bf16[128,16,640]{2,1,0:T(8,128)(2,1)}, u32[]{:S(2)}) %copy-start.11) | copy-done | bytes 2621464
  28.4 0.0 copy-start.3
  28.4 0.0 copy-start.5
  28.4 7.6 %private.2 = (f32[128,1280]{1,0:T(8,128)S(1)}, f32[128,128]{1,0:T(8,128)S(1)}) custom-call(bf16[128,2560]{1,0:T(8,128)(2,1)S(1)} %copy-done.2, bf16[2048,640]{1,0:T(8,128)(2,1)S(1)} %bitcast.21, bf16[2048,640]{1,0:T(8,128)(2,1)S(1)} %bitcast.23, s32[8,128]{1,0:T(8,128)S(1)} %bitcast.25, s32[1,128]{1,0:T(1,128)S(1)} %bitcast.27, ...), custom_call_target="tpu_custom_call" | custom-call | flops 4294967296 | bytes 5242880 | tf_op jit(solution)/shard_map/private/pallas_call | solution.py:257
  36.0 0.0 copy-start.4
  36.0 0.0 copy-start.6
  36.0 0.0 copy-done.3
  36.0 0.0 copy-done.5
  36.0 3.9 %prefix.2.after_ref = bf16[128,2688]{1,0:T(8,128)(2,1)} custom-call(bf16[128,2560]{1,0:T(8,128)(2,1)S(1)} %bitcast.16, bf16[256,640]{1,0:T(8,128)(2,1)S(1)} %copy-done.3, bf16[256,640]{1,0:T(8,128)(2,1)S(1)} %copy-done.5, f32[128,128]{1,0:T(8,128)S(1)} %get-tuple-element.12.after_ref.low_lse_ref), custom_call_target="tpu_custom_call" | custom-call | flops 335544320 | bytes 2621440 | tf_op jit(solution)/shard_map/prefix/pallas_call | solution.py:143
  40.0 0.0 all-to-all-done.2
  40.0 5.1 %all-to-all-start.1 = ((bf16[16,8,2688]{2,1,0:T(8,128)(2,1)}), bf16[16,8,2688]{2,1,0:T(8,128)(2,1)S(1)}, u32[]{:S(2)}, u32[]{:S(2)}) async-start(bf16[16,8,2688]{2,1,0:T(8,128)(2,1)} %bitcast.8), calls=%async_computation.1 | async-start | bytes 1376256 | tf_op jit(solution)/shard_map/all_to_all | solution.py:402
  45.0 0.0 copy-done.4
  45.0 2.7 %collective-permute-start = (bf16[256,640]{1,0:T(8,128)(2,1)S(1)}, bf16[256,640]{1,0:T(8,128)(2,1)S(1)}, u32[]{:S(2)}, u32[]{:S(2)}) collective-permute-start(bf16[256,640]{1,0:T(8,128)(2,1)S(1)} %copy-done.4), channel_id=1, source_target_pairs={{0,16},{1,17},{2,18},{3,19},{4,20},{5,21},{6,22},{7,23},{8,24},{9,... | collective-permute-start | bytes 983048 | tf_op jit(solution)/shard_map/ppermute | solution.py:407
  47.7 0.0 copy-done.6
  47.7 0.3 collective-permute-start.1
  48.0 12.6 %collective-permute-done.k_ref = bf16[256,640]{1,0:T(8,128)(2,1)S(1)} collective-permute-done((bf16[256,640]{1,0:T(8,128)(2,1)S(1)}, bf16[256,640]{1,0:T(8,128)(2,1)S(1)}, u32[]{:S(2)}, u32[]{:S(2)}) %collective-permute-start) | collective-permute-done | bytes 327712 | tf_op jit(solution)/shard_map/ppermute | solution.py:407
  60.7 16.5 %collective-permute-done.1.v_ref = bf16[256,640]{1,0:T(8,128)(2,1)S(1)} collective-permute-done((bf16[256,640]{1,0:T(8,128)(2,1)S(1)}, bf16[256,640]{1,0:T(8,128)(2,1)S(1)}, u32[]{:S(2)}, u32[]{:S(2)}) %collective-permute-start.1) | collective-permute-done | bytes 327712 | tf_op jit(solution)/shard_map/ppermute | solution.py:408
  77.2 4.0 %prefix.3.after_ref = bf16[128,2688]{1,0:T(8,128)(2,1)} custom-call(bf16[128,2560]{1,0:T(8,128)(2,1)S(1)} %bitcast.17, bf16[256,640]{1,0:T(8,128)(2,1)S(1)} %collective-permute-done.k_ref, bf16[256,640]{1,0:T(8,128)(2,1)S(1)} %collective-permute-done.1.v_ref, bf16[128,2688]{1,0:T(8,128)(2,1)} %prefix.2.after_ref), custom_call_target="tpu_custom_call" | custom-call | flops 335544320 | bytes 2621440 | tf_op jit(solution)/shard_map/prefix/pallas_call | solution.py:143
  81.1 0.0 all-to-all-done.1
  81.1 4.1 %all-to-all-start.3 = ((bf16[16,8,2688]{2,1,0:T(8,128)(2,1)}), bf16[16,8,2688]{2,1,0:T(8,128)(2,1)S(1)}, u32[]{:S(2)}, u32[]{:S(2)}) async-start(bf16[16,8,2688]{2,1,0:T(8,128)(2,1)} %bitcast.12), calls=%async_computation.3 | async-start | bytes 1376256 | tf_op jit(solution)/shard_map/all_to_all | solution.py:402
  85.8 0.0 copy-start.10
  85.8 1.7 %copy-done.10 = bf16[128,16,640]{2,1,0:T(8,128)(2,1)S(1)} copy-done((bf16[128,16,640]{2,1,0:T(8,128)(2,1)S(1)}, bf16[128,16,640]{2,1,0:T(8,128)(2,1)}, u32[]{:S(2)}) %copy-start.10) | copy-done | bytes 2621464
  87.6 0.0 copy-start.12
  87.6 1.7 %copy-done.12 = bf16[128,16,640]{2,1,0:T(8,128)(2,1)S(1)} copy-done((bf16[128,16,640]{2,1,0:T(8,128)(2,1)S(1)}, bf16[128,16,640]{2,1,0:T(8,128)(2,1)}, u32[]{:S(2)}) %copy-start.12) | copy-done | bytes 2621464
  89.3 0.0 copy-start.8
  89.3 7.6 %private.3 = (f32[128,1280]{1,0:T(8,128)S(1)}, f32[128,128]{1,0:T(8,128)S(1)}) custom-call(bf16[128,2560]{1,0:T(8,128)(2,1)S(1)} %copy-done.2, bf16[2048,640]{1,0:T(8,128)(2,1)S(1)} %bitcast.22, bf16[2048,640]{1,0:T(8,128)(2,1)S(1)} %bitcast.24, s32[8,128]{1,0:T(8,128)S(1)} %bitcast.26, s32[1,128]{1,0:T(1,128)S(1)} %bitcast.28, ...), custom_call_target="tpu_custom_call" | custom-call | flops 4294967296 | bytes 5242880 | tf_op jit(solution)/shard_map/private/pallas_call | solution.py:257
  96.9 0.5 all-to-all-done.3
  97.5 0.0 copy-done.8
  97.5 0.0 copy-start
  97.5 4.7 %copy-done = bf16[2560,2560]{1,0:T(8,128)(2,1)S(1)} copy-done((bf16[2560,2560]{1,0:T(8,128)(2,1)S(1)}, bf16[2560,2560]{1,0:T(8,128)(2,1)}, u32[]{:S(2)}) %copy-start) | copy-done | bytes 13107224
  102.2 5.5 %finish.1 = bf16[128,2560]{1,0:T(8,128)(2,1)} custom-call(s32[1]{0:T(128)} %bitcast.side_ref, s32[1]{0:T(128)S(6)} %copy.11.live_ref, s32[1,128]{1,0:T(1,128)S(1)} %bitcast.20, bf16[128,2688]{1,0:T(8,128)(2,1)S(1)} %bitcast.14, bf16[128,2688]{1,0:T(8,128)(2,1)S(1)} %bitcast.15, f32[128,1280]{1,0:T(8,128)S(1)} %get-tuple-element.14.low_ref, ...), custom_call_target="tpu_custom_call" | custom-call | flops 1677721600 | bytes 13107200 | tf_op jit(solution)/shard_map/finish/pallas_call | solution.py:356
Async XLA Ops:
  0.0 24.8 %copy-start.14 = (s32[128]{0:T(128)S(1)}, s32[128]{0:T(128)}, u32[]{:S(2)}) copy-start(s32[128]{0:T(128)} %param.16) | copy-start | bytes 1540
  0.0 24.9 %copy-start.13 = (s32[128,8]{0,1:T(8,128)S(1)}, s32[128,8]{0,1:T(8,128)}, u32[]{:S(2)}) copy-start(s32[128,8]{0,1:T(8,128)} %param.15) | copy-start | bytes 12292
  0.0 1.1 %copy-start.1 = (bf16[128,2560]{1,0:T(8,128)(2,1)S(1)}, bf16[128,2560]{1,0:T(8,128)(2,1)}, u32[]{:S(2)}) copy-start(bf16[128,2560]{1,0:T(8,128)(2,1)} %q_ref.5) | copy-start | bytes 1966084
  1.1 0.7 copy-start.7
  1.8 23.1 %copy-start.2 = (bf16[128,2560]{1,0:T(8,128)(2,1)S(1)}, bf16[128,2560]{1,0:T(8,128)(2,1)}, u32[]{:S(2)}) copy-start(bf16[128,2560]{1,0:T(8,128)(2,1)} %q_ref.5) | copy-start | bytes 1966084
  21.2 18.7 %all-to-all-start.2 = ((bf16[16,8,2560]{2,1,0:T(8,128)(2,1)}), bf16[16,8,2560]{2,1,0:T(8,128)(2,1)S(1)}, u32[]{:S(2)}, u32[]{:S(2)}) async-start(bf16[16,8,2560]{2,1,0:T(8,128)(2,1)} %bitcast.10), calls=%async_computation.2 | async-start | bytes 1310720 | tf_op jit(solution)/shard_map/all_to_all | solution.py:402
  24.9 1.7 %copy-start.9 = (bf16[128,16,640]{2,1,0:T(8,128)(2,1)S(1)}, bf16[128,16,640]{2,1,0:T(8,128)(2,1)}, u32[]{:S(2)}) copy-start(bf16[128,16,640]{2,1,0:T(8,128)(2,1)} %param.13) | copy-start | bytes 7864324
  26.6 1.7 %copy-start.11 = (bf16[128,16,640]{2,1,0:T(8,128)(2,1)S(1)}, bf16[128,16,640]{2,1,0:T(8,128)(2,1)}, u32[]{:S(2)}) copy-start(bf16[128,16,640]{2,1,0:T(8,128)(2,1)} %param.14) | copy-start | bytes 7864324
  28.4 7.6 %copy-start.3 = (bf16[256,640]{1,0:T(8,128)(2,1)S(1)}, bf16[256,640]{1,0:T(8,128)(2,1)}, u32[]{:S(2)}) copy-start(bf16[256,640]{1,0:T(8,128)(2,1)} %k_ref.1) | copy-start | bytes 983044
  28.4 7.7 %copy-start.5 = (bf16[256,640]{1,0:T(8,128)(2,1)S(1)}, bf16[256,640]{1,0:T(8,128)(2,1)}, u32[]{:S(2)}) copy-start(bf16[256,640]{1,0:T(8,128)(2,1)} %v_ref.1) | copy-start | bytes 983044
  36.0 9.1 %copy-start.4 = (bf16[256,640]{1,0:T(8,128)(2,1)S(1)}, bf16[256,640]{1,0:T(8,128)(2,1)}, u32[]{:S(2)}) copy-start(bf16[256,640]{1,0:T(8,128)(2,1)} %k_ref.1) | copy-start | bytes 983044
  36.0 11.7 %copy-start.6 = (bf16[256,640]{1,0:T(8,128)(2,1)S(1)}, bf16[256,640]{1,0:T(8,128)(2,1)}, u32[]{:S(2)}) copy-start(bf16[256,640]{1,0:T(8,128)(2,1)} %v_ref.1) | copy-start | bytes 983044
  40.0 41.2 %all-to-all-start.1 = ((bf16[16,8,2688]{2,1,0:T(8,128)(2,1)}), bf16[16,8,2688]{2,1,0:T(8,128)(2,1)S(1)}, u32[]{:S(2)}, u32[]{:S(2)}) async-start(bf16[16,8,2688]{2,1,0:T(8,128)(2,1)} %bitcast.8), calls=%async_computation.1 | async-start | bytes 1376256 | tf_op jit(solution)/shard_map/all_to_all | solution.py:402
  45.0 15.6 %collective-permute-start = (bf16[256,640]{1,0:T(8,128)(2,1)S(1)}, bf16[256,640]{1,0:T(8,128)(2,1)S(1)}, u32[]{:S(2)}, u32[]{:S(2)}) collective-permute-start(bf16[256,640]{1,0:T(8,128)(2,1)S(1)} %copy-done.4), channel_id=1, source_target_pairs={{0,16},{1,17},{2,18},{3,19},{4,20},{5,21},{6,22},{7,23},{8,24},{9,... | collective-permute-start | bytes 983048 | tf_op jit(solution)/shard_map/ppermute | solution.py:407
  47.7 29.5 %collective-permute-start.1 = (bf16[256,640]{1,0:T(8,128)(2,1)S(1)}, bf16[256,640]{1,0:T(8,128)(2,1)S(1)}, u32[]{:S(2)}, u32[]{:S(2)}) collective-permute-start(bf16[256,640]{1,0:T(8,128)(2,1)S(1)} %copy-done.6), channel_id=1, source_target_pairs={{0,16},{1,17},{2,18},{3,19},{4,20},{5,21},{6,22},{7,23},{8,24},{9,... | collective-permute-start | bytes 983048 | tf_op jit(solution)/shard_map/ppermute | solution.py:408
  81.1 16.4 %all-to-all-start.3 = ((bf16[16,8,2688]{2,1,0:T(8,128)(2,1)}), bf16[16,8,2688]{2,1,0:T(8,128)(2,1)S(1)}, u32[]{:S(2)}, u32[]{:S(2)}) async-start(bf16[16,8,2688]{2,1,0:T(8,128)(2,1)} %bitcast.12), calls=%async_computation.3 | async-start | bytes 1376256 | tf_op jit(solution)/shard_map/all_to_all | solution.py:402
  85.8 1.7 %copy-start.10 = (bf16[128,16,640]{2,1,0:T(8,128)(2,1)S(1)}, bf16[128,16,640]{2,1,0:T(8,128)(2,1)}, u32[]{:S(2)}) copy-start(bf16[128,16,640]{2,1,0:T(8,128)(2,1)} %param.13) | copy-start | bytes 7864324
  87.6 1.7 %copy-start.12 = (bf16[128,16,640]{2,1,0:T(8,128)(2,1)S(1)}, bf16[128,16,640]{2,1,0:T(8,128)(2,1)}, u32[]{:S(2)}) copy-start(bf16[128,16,640]{2,1,0:T(8,128)(2,1)} %param.14) | copy-start | bytes 7864324
  89.3 8.2 %copy-start.8 = (s32[128,1]{0,1:T(1,128)S(1)}, s32[128,1]{0,1:T(1,128)}, u32[]{:S(2)}) copy-start(s32[128,1]{0,1:T(1,128)} %param.17) | copy-start | bytes 1540
  97.5 4.7 %copy-start = (bf16[2560,2560]{1,0:T(8,128)(2,1)S(1)}, bf16[2560,2560]{1,0:T(8,128)(2,1)}, u32[]{:S(2)}) copy-start(bf16[2560,2560]{1,0:T(8,128)(2,1)} %w_hbm.1) | copy-start | bytes 39321604

commit v3 on v2

--- a/solution.py
+++ b/solution.py
@@ -57,31 +57,38 @@
     return (groups - upper * half) * slot_count + rank, upper
 
 
-def place_kernel(half, slot_count, side_ref, groups_ref, q_ref, own_ref, other_ref):
-    n = q_ref.shape[0]
+def place_kernel(half, slot_count, side_ref, groups_ref, q_hbm, out_ref, q_ref, sems):
+    n, width = q_ref.shape
+    chunk = width // sems.shape[0]
+    copies = []
+    for i in range(sems.shape[0]):
+        cols = pl.ds(i * chunk, chunk)
+        copies.append(pltpu.make_async_copy(q_hbm.at[:, cols], q_ref.at[:, cols], sems.at[i]))
+        copies[i].start()
     slot, upper = slots_of(groups_ref[...], half, slot_count)
     hit = slot == iota((n, n), 0)
     side = side_ref[0]
     own = jnp.where(hit & (upper == side), 1.0, 0.0).astype(jnp.bfloat16)
     other = jnp.where(hit & (upper != side), 1.0, 0.0).astype(jnp.bfloat16)
     spread = jnp.concatenate([own, other], axis=0)
-    for base in range(0, q_ref.shape[1], 512):
-        cols = slice(base, base + 512)
+    for i, copy in enumerate(copies):
+        copy.wait()
+        cols = slice(i * chunk, (i + 1) * chunk)
         both = jnp.dot(spread, q_ref[:, cols], preferred_element_type=jnp.float32)
         both = both.astype(jnp.bfloat16)
-        own_ref[:, cols] = both[:n]
-        other_ref[:, cols] = both[n:]
+        out_ref[:, i * chunk : (i + 1) * chunk] = both[:n]
+        out_ref[:, width + i * chunk : width + (i + 1) * chunk] = both[n:]
 
 
 def place(queries, groups, side, half, slot_count):
     n, width = queries.shape
-    shape = jax.ShapeDtypeStruct(queries.shape, queries.dtype)
     return pl.pallas_call(
         functools.partial(place_kernel, half, slot_count),
-        out_shape=(shape, shape),
-        in_specs=[SMEM, VMEM, VMEM],
-        out_specs=(VMEM, VMEM),
-        compiler_params=params(16),
+        out_shape=jax.ShapeDtypeStruct((n, 2 * width), queries.dtype),
+        in_specs=[SMEM, VMEM, ANY],
+        out_specs=VMEM,
+        scratch_shapes=[pltpu.VMEM((n, width), queries.dtype), pltpu.SemaphoreType.DMA((4,))],
+        compiler_params=params(48),
         cost_estimate=pl.CostEstimate(
             flops=4 * n * n * width, bytes_accessed=6 * n * width, transcendentals=0
         ),
@@ -101,11 +108,16 @@
         qs_ref[i, first : first + HD, g * n : (g + 1) * n] = qt_ref[row : row + HD]
 
 
-def prefix_kernel(q_ref, k_ref, v_ref, after_ref, out_ref, qt_ref, vt_ref, qs_ref, ot_ref, lse_ref):
-    del after_ref
-    n, width = q_ref.shape
+def prefix_kernel(
+    part, rows_ref, k_ref, v_ref, before_ref, out_ref, qt_ref, vt_ref, qs_ref, ot_ref, lse_ref
+):
+    n, width = rows_ref.shape
+    width //= 2
     key_width = k_ref.shape[1]
-    transpose_into(qt_ref, q_ref)
+    transpose_into(qt_ref, rows_ref.at[:, part * width : (part + 1) * width])
+    if part:
+        out_ref[:, : width + LANES] = before_ref[...]
+    out_ref = out_ref.at[:, part * (width + LANES) : (part + 1) * (width + LANES)]
     transpose_into(vt_ref, v_ref)
     for k in range(KVH):
         place_queries(qs_ref, k, qt_ref, k, key_width)
@@ -137,13 +149,14 @@
     out_ref[:, width:] = pieces.T.astype(jnp.bfloat16)
 
 
-def prefix_part(rows, keys, values, after):
+def prefix_part(part, rows, keys, values, before):
     n, width = rows.shape
+    width //= 2
     tokens, key_width = keys.shape
     return pl.pallas_call(
-        prefix_kernel,
-        out_shape=jax.ShapeDtypeStruct((n, width + LANES), jnp.bfloat16),
-        in_specs=[VMEM, VMEM, VMEM, ANY],
+        functools.partial(prefix_kernel, part),
+        out_shape=jax.ShapeDtypeStruct((n, (part + 1) * (width + LANES)), jnp.bfloat16),
+        in_specs=[VMEM, VMEM, VMEM, VMEM if part else ANY],
         out_specs=VMEM,
         scratch_shapes=[
             pltpu.VMEM((width, n), jnp.bfloat16),
@@ -154,10 +167,10 @@
         ],
         compiler_params=params(24),
         cost_estimate=pl.CostEstimate(
-            flops=4 * n * 256 * width, bytes_accessed=4 * n * width * 2, transcendentals=n * 256 * H
+            flops=8000 * n * 256 * width, bytes_accessed=4 * n * width * 2, transcendentals=n * 256 * H
         ),
         name="prefix",
-    )(rows, keys, values, after)
+    )(rows, keys, values, before)
 
 
 def fill_bias(bias_ref, pages, lengths, page_size):
@@ -181,23 +194,28 @@
 
 
 def private_kernel(
-    first_head, heads, page_size, q_ref, k_ref, v_ref, pages_ref, lengths_ref, after_ref,
-    out_ref, lse_ref, qt_ref, vt_ref, qs_ref, bias_ref, ot_ref, lses_ref,
-    scores_a, scores_b, top_a, top_b, weights_ref
+    first_head, heads, page_size, q_hbm, k_hbm, v_hbm, pages_ref, lengths_ref, after_ref,
+    out_ref, lse_ref, q_ref, k_ref, v_ref, qt_ref, vt_ref, qs_ref, bias_ref, ot_ref, lses_ref,
+    scores_a, scores_b, top_a, top_b, weights_ref, sems
 ):
     del after_ref
+    copies = [
+        pltpu.make_async_copy(source, target, sems.at[i])
+        for i, (source, target) in enumerate(((q_hbm, q_ref), (k_hbm, k_ref), (v_hbm, v_ref)))
+    ]
+    for copy in copies:
+        copy.start()
     n = q_ref.shape[0]
     tokens, key_width = k_ref.shape
     rows = GROUP * n
     tile = 256
+    fill_bias(bias_ref, pages_ref[...], lengths_ref[...], page_size)
+    copies[0].wait()
     query0 = first_head * GROUP * HD
     transpose_into(qt_ref, q_ref.at[:, query0 : query0 + heads * GROUP * HD])
-    value0 = first_head * HD // LANES * LANES
-    value1 = -(-(first_head + heads) * HD // LANES) * LANES
-    transpose_into(vt_ref.at[value0:value1], v_ref.at[:, value0:value1])
-    fill_bias(bias_ref, pages_ref[...], lengths_ref[...], page_size)
     for i in range(heads):
         place_queries(qs_ref, i, qt_ref, first_head + i, key_width)
+    copies[1].wait()
 
     def score(i, scores_ref, top_ref):
         k = first_head + i
@@ -236,6 +254,10 @@
         return lses
 
     score(0, scores_a, top_a)
+    copies[2].wait()
+    value0 = first_head * HD // LANES * LANES
+    value1 = -(-(first_head + heads) * HD // LANES) * LANES
+    transpose_into(vt_ref.at[value0:value1], v_ref.at[:, value0:value1])
 
     def two(j, lses):
         i = 2 * j
@@ -260,9 +282,12 @@
             jax.ShapeDtypeStruct((n, width), jnp.float32),
             jax.ShapeDtypeStruct((n, LANES), jnp.float32),
         ),
-        in_specs=[VMEM] * 5 + [ANY],
+        in_specs=[ANY] * 3 + [VMEM] * 2 + [ANY],
         out_specs=(VMEM, VMEM),
         scratch_shapes=[
+            pltpu.VMEM(queries.shape, queries.dtype),
+            pltpu.VMEM(keys.shape, keys.dtype),
+            pltpu.VMEM(values.shape, values.dtype),
             pltpu.VMEM((width, n), jnp.bfloat16),
             pltpu.VMEM((key_width, tokens), jnp.bfloat16),
             pltpu.VMEM((heads, WIN, GROUP * n), jnp.bfloat16),
@@ -274,10 +299,11 @@
             pltpu.VMEM((8, GROUP * n), jnp.float32),
             pltpu.VMEM((8, GROUP * n), jnp.float32),
             pltpu.VMEM((tokens, GROUP * n), jnp.bfloat16),
+            pltpu.SemaphoreType.DMA((3,)),
         ],
-        compiler_params=params(36),
+        compiler_params=params(48),
         cost_estimate=pl.CostEstimate(
-            flops=4 * n * tokens * heads * GROUP * WIN,
+            flops=1200 * n * tokens * heads * GROUP * WIN,
             bytes_accessed=4 * tokens * key_width,
             transcendentals=n * tokens * heads * GROUP,
         ),
@@ -301,17 +327,39 @@
     )
 
 
+def load_kernel(w_hbm, after_ref, w_ref, sems):
+    del after_ref
+    chunk = w_ref.shape[1] // sems.shape[0]
+    copies = []
+    for i in range(sems.shape[0]):
+        cols = pl.ds(i * chunk, chunk)
+        copies.append(pltpu.make_async_copy(w_hbm.at[:, cols], w_ref.at[:, cols], sems.at[i]))
+        copies[i].start()
+    for copy in copies:
+        copy.wait()
+
+
+def load(weight, after):
+    return pl.pallas_call(
+        load_kernel,
+        out_shape=jax.ShapeDtypeStruct(weight.shape, weight.dtype),
+        in_specs=[ANY, ANY],
+        out_specs=VMEM,
+        scratch_shapes=[pltpu.SemaphoreType.DMA((5,))],
+        compiler_params=params(32),
+        cost_estimate=pl.CostEstimate(
+            flops=10**10, bytes_accessed=2 * weight.size * 2, transcendentals=0
+        ),
+        name="load",
+    )(weight, after)
+
+
 def finish_kernel(
-    half, slot_count, chunk, side_ref, live_ref, groups_ref, own_ref, other_ref,
-    low_ref, high_ref, low_lse_ref, high_lse_ref, w_hbm, out_ref, w_ref, sems
+    half, slot_count, side_ref, live_ref, groups_ref, back_ref, private_ref, private_lse_ref,
+    w_ref, out_ref
 ):
     n, width = out_ref.shape
-    copies = []
-    for i in range(width // chunk):
-        cols = pl.ds(i * chunk, chunk)
-        copy = pltpu.make_async_copy(w_hbm.at[:, cols], w_ref.at[:, cols], sems.at[i])
-        copy.start()
-        copies.append(copy)
+    part = width + LANES
     slot, upper = slots_of(groups_ref[...], half, slot_count)
     slot, upper = as_column(slot), as_column(upper)
     hit = slot == iota((n, n), 1)
@@ -320,54 +368,47 @@
     other = jnp.where(hit & (upper != side), 1.0, 0.0).astype(jnp.bfloat16)
     pick = jnp.concatenate([own, other], axis=1)
 
-    def picked(cols):
-        both = jnp.concatenate([own_ref[:, cols], other_ref[:, cols]], axis=0)
+    def picked(first, last):
+        both = jnp.concatenate(
+            [back_ref[:, first:last], back_ref[:, part + first : part + last]], axis=0
+        )
         return jnp.dot(pick, both, preferred_element_type=jnp.float32)
 
-    pieces = picked(slice(width, width + LANES))
+    pieces = picked(width, part)
     lane = iota((n, LANES), 1)
     prefix_lse = (
         pieces + pltpu.roll(pieces, LANES - H, 1) + pltpu.roll(pieces, LANES - 2 * H, 1)
     )
     prefix_lse = jnp.where(lane < H, prefix_lse, 0.0)
-    private_lse = jnp.where(
-        lane < H // 2, low_lse_ref[...], pltpu.roll(high_lse_ref[...], H // 2, 1)
-    )
-    private_lse = jnp.where(lane < H, private_lse, 0.0)
+    private_lse = private_lse_ref[...]
     top = jnp.maximum(prefix_lse, private_lse)
     a, b = jnp.exp(prefix_lse - top), jnp.exp(private_lse - top)
     prefix_share = expand_heads(a / (a + b), width)
     private_share = expand_heads(b / (a + b), width)
-    private = jnp.concatenate([low_ref[...], high_ref[...]], axis=1)
-    attended = prefix_share * picked(slice(0, width)) + private_share * private
+    attended = prefix_share * picked(0, width) + private_share * private_ref[...]
     attended = attended.astype(jnp.bfloat16)
     is_live = iota((n, 1), 0) < live_ref[0]
-    for i, copy in enumerate(copies):
-        copy.wait()
-        cols = slice(i * chunk, (i + 1) * chunk)
-        projected = jnp.dot(attended, w_ref[:, cols], preferred_element_type=jnp.float32)
-        out_ref[:, cols] = jnp.where(is_live, projected, 0.0).astype(out_ref.dtype)
-
-
-def finish(side, live, groups, own, other, low, high, low_lse, high_lse, weight, half, slot_count):
-    n = own.shape[0]
+    for first in range(0, width, 512):
+        projected = jnp.dot(
+            attended, w_ref[:, first : first + 512], preferred_element_type=jnp.float32
+        )
+        out_ref[:, first : first + 512] = jnp.where(is_live, projected, 0.0).astype(out_ref.dtype)
+
+
+def finish(side, live, groups, back, private, private_lse, weight, half, slot_count):
+    n = back.shape[0]
     width = weight.shape[1]
-    chunk = 512
     return pl.pallas_call(
-        functools.partial(finish_kernel, half, slot_count, chunk),
+        functools.partial(finish_kernel, half, slot_count),
         out_shape=jax.ShapeDtypeStruct((n, width), jnp.bfloat16),
-        in_specs=[SMEM, SMEM] + [VMEM] * 7 + [ANY],
+        in_specs=[SMEM, SMEM] + [VMEM] * 5,
         out_specs=VMEM,
-        scratch_shapes=[
-            pltpu.VMEM(weight.shape, weight.dtype),
-            pltpu.SemaphoreType.DMA((width // chunk,)),
-        ],
-        compiler_params=params(32),
+        compiler_params=params(24),
         cost_estimate=pl.CostEstimate(
             flops=2 * n * width * width, bytes_accessed=2 * width * width, transcendentals=0
         ),
         name="finish",
-    )(side, live, groups, own, other, low, high, low_lse, high_lse, weight)
+    )(side, live, groups, back, private, private_lse, weight)
 
 
 def per_device(
@@ -406,20 +447,17 @@
 
     far_keys = lax.ppermute(prefix_keys, "req", across)
     far_values = lax.ppermute(prefix_values, "req", across)
-    own, other = place(queries, groups, side, half, slot_count)
-    own_rows, other_rows = exchange(own), exchange(other)
-    private = functools.partial(
-        private_part, queries, flat_keys, flat_values, pages, lengths
-    )
-    low, low_lse = private(own, page_size, 0, KVH // 2)
-    own_out = prefix_part(own_rows, prefix_keys, prefix_values, low_lse)
-    own_back = exchange(own_out)
-    other_out = prefix_part(other_rows, far_keys, far_values, own_out)
-    other_back = exchange(other_out)
-    high, high_lse = private(other_out, page_size, KVH // 2, KVH // 2)
+    placed = place(queries, groups, side, half, slot_count)
+    rows = exchange(placed)
+    private, private_lse = private_part(
+        queries, flat_keys, flat_values, pages, lengths, placed, page_size, 0, KVH
+    )
+    own_out = prefix_part(0, rows, prefix_keys, prefix_values, private_lse)
+    out = prefix_part(1, rows, far_keys, far_values, own_out)
+    back = exchange(out)
+    weight = load(out_weight, out)
     return finish(
-        side, live_rows, groups, own_back, other_back, low, high, low_lse, high_lse,
-        out_weight, half, slot_count,
+        side, live_rows, groups, back, private, private_lse, weight, half, slot_count
     )
 
 

time: 109 us -> 88.7 us (0.81)
  blocking collectives: 18 us -> 0 us
  Pallas kernels: 30 us -> 36.3 us
  waiting for transfers between devices: 29.7 us -> 24.9 us
  starting transfers between devices: 15.7 us -> 13.3 us
    all_to_all x3 -> x2, waiting for transfers between devices: 0.54 us -> 24.9 us  [exchange(): lax.all_to_all(blocks, 'req', split_axis=0, concat_axis=0, tiled=True, ax...]
    all_to_all x1 -> x0, blocking collectives: 18 us -> none  [exchange(): lax.all_to_all(blocks, 'req', split_axis=0, concat_axis=0, tiled=True, ax...]
    ppermute x1, waiting for transfers between devices: 16.5 us -> 0.01 us  [per_device(): far_values = lax.ppermute(prefix_values, 'req', across)]
    ppermute x1, waiting for transfers between devices: 12.6 us -> 0.01 us  [per_device(): far_keys = lax.ppermute(prefix_keys, 'req', across)]
    pallas_call x3 -> x4, Pallas kernels: 13.4 us -> 18.7 us  [the longest x2 10 us: prefix_part(): pl.pallas_call(functools.partial(prefix_kernel, part), out_shape=jax.Shap...]
    all_to_all x3 -> x2, starting transfers between devices: 12.7 us -> 9.22 us  [exchange(): lax.all_to_all(blocks, 'req', split_axis=0, concat_axis=0, tiled=True, ax...]
    ppermute x1, starting transfers between devices: 2.66 us -> 4.04 us  [per_device(): far_keys = lax.ppermute(prefix_keys, 'req', across)]
    unnamed x30 -> x26, local copies, waits for them, and re-layouts: 13.5 us -> 13 us
  transfers between devices with their start and end apart: 5 -> 4, of which waited for: 3 -> 2; matrix products, arithmetic and copies ran while one was open for 0% -> 0% of each run, Pallas kernels for 21% -> 30%
where the time goes in v3:
time: 88.7 us; the launch traced here: 88.2 us
  Pallas kernels  36.3 us (41%)
  waiting for transfers between devices  24.9 us (28%)
  starting transfers between devices  13.3 us (15%)
  local copies, waits for them, and re-layouts  13 us (15%)
    all_to_all x2, waiting for transfers between devices, exchange(): lax.all_to_all(blocks, 'req', split_axis=0, concat_axis=0, tiled=True, ax...  24.9 us
    pallas_call x1, Pallas kernels, private_part(): pl.pallas_call(functools.partial(private_kernel, first_head, heads, page_...  15.2 us
    unnamed x26, local copies, waits for them, and re-layouts  13 us
    pallas_call x2, Pallas kernels, prefix_part(): pl.pallas_call(functools.partial(prefix_kernel, part), out_shape=jax.Shap...  10 us
    all_to_all x2, starting transfers between devices, exchange(): lax.all_to_all(blocks, 'req', split_axis=0, concat_axis=0, tiled=True, ax...  9.22 us
    pallas_call x1, Pallas kernels, load(): pl.pallas_call(load_kernel, out_shape=jax.ShapeDtypeStruct(weight.shape,...  4.94 us
    ppermute x1, starting transfers between devices, per_device(): far_keys = lax.ppermute(prefix_keys, 'req', across)  4.04 us
    pallas_call x1, Pallas kernels, finish(): pl.pallas_call(functools.partial(finish_kernel, half, slot_count), out_sh...  3.77 us
  transfers between devices with their start and end apart: 4, of which 2 were waited for; matrix products, arithmetic and copies ran while one was open for 0% of the time, Pallas kernels for 30%

profile of v3, /device:TPU:0, one launch (start us, length us, event | category | flops | bytes accessed | tf_op | source)
XLA Modules:
  0.0 88.2 jit_solution(1094563196250108414)
XLA Ops:
  0.0 4.0 %collective-permute-start = (bf16[256,640]{1,0:T(8,128)(2,1)}, bf16[256,640]{1,0:T(8,128)(2,1)}, u32[]{:S(2)}, u32[]{:S(2)}) collective-permute-start(bf16[256,640]{1,0:T(8,128)(2,1)} %k_ref.1), channel_id=1, source_target_pairs={{0,16},{1,17},{2,18},{3,19},{4,20},{5,21},{6,22},{7,23},{8,24},{9,... | collective-permute-start | bytes 983048 | tf_op jit(solution)/shard_map/ppermute | solution.py:448
  4.0 0.0 collective-permute-start.1
  4.1 0.0 copy-start.2
  4.1 1.1 %copy-done.2 = bf16[128,2560]{1,0:T(8,128)(2,1)S(1)} copy-done((bf16[128,2560]{1,0:T(8,128)(2,1)S(1)}, bf16[128,2560]{1,0:T(8,128)(2,1)}, u32[]{:S(2)}) %copy-start.2) | copy-done | bytes 655384
  5.2 0.0 copy-start.6
  5.2 0.7 copy-done.6
  5.8 2.3 %place.1.after_ref = bf16[128,5120]{1,0:T(8,128)(2,1)} custom-call(s32[1]{0:T(128)} %bitcast.side_ref, s32[1,128]{1,0:T(1,128)S(1)} %bitcast.11, bf16[128,2560]{1,0:T(8,128)(2,1)S(1)} %copy-done.2), custom_call_target="tpu_custom_call" | custom-call | flops 167772160 | bytes 1966080 | tf_op jit(solution)/shard_map/place/pallas_call | solution.py:85
  8.1 0.0 copy-start.3
  8.1 0.0 copy-start.11
  8.1 0.0 copy-start.12
  8.1 5.3 %all-to-all-start = ((bf16[16,8,5120]{2,1,0:T(8,128)(2,1)}), bf16[16,8,5120]{2,1,0:T(8,128)(2,1)}, u32[]{:S(2)}, u32[]{:S(2)}) async-start(bf16[16,8,5120]{2,1,0:T(8,128)(2,1)} %bitcast.2), calls=%async_computation | async-start | bytes 2621440 | tf_op jit(solution)/shard_map/all_to_all | solution.py:443
  13.5 0.0 copy-done.3
  13.5 0.0 copy-done.11
  13.5 0.0 copy-done.12
  13.5 0.0 copy-start.8
  13.5 1.7 %copy-done.8 = bf16[128,16,640]{2,1,0:T(8,128)(2,1)S(1)} copy-done((bf16[128,16,640]{2,1,0:T(8,128)(2,1)S(1)}, bf16[128,16,640]{2,1,0:T(8,128)(2,1)}, u32[]{:S(2)}) %copy-start.8) | copy-done | bytes 2621464
  15.3 0.0 copy-start.9
  15.3 0.0 copy-start.10
  15.3 15.2 %private.1 = (f32[128,2560]{1,0:T(8,128)S(1)}, f32[128,128]{1,0:T(8,128)S(1)}) custom-call(bf16[128,2560]{1,0:T(8,128)(2,1)S(1)} %copy-done.3, bf16[2048,640]{1,0:T(8,128)(2,1)S(1)} %bitcast.13, bf16[2048,640]{1,0:T(8,128)(2,1)} %bitcast.16, s32[8,128]{1,0:T(8,128)S(1)} %bitcast.14, s32[1,128]{1,0:T(1,128)S(1)} %bitcast.15, bf16[128,5120]{1,0:T(8,128)(2,1)} %place.1.after_ref), custom_call_target="tpu_custom_call" | custom-call | flops 2576980377600 | bytes 5242880 | tf_op jit(solution)/shard_map/private/pallas_call | solution.py:279
  30.5 0.0 copy-start.4
  30.5 15.3 %all-to-all-done = bf16[16,8,5120]{2,1,0:T(8,128)(2,1)} async-done(((bf16[16,8,5120]{2,1,0:T(8,128)(2,1)}), bf16[16,8,5120]{2,1,0:T(8,128)(2,1)}, u32[]{:S(2)}, u32[]{:S(2)}) %all-to-all-start) | async-done | bytes 1310752 | tf_op jit(solution)/shard_map/all_to_all | solution.py:443
  45.8 0.0 copy-done.9
  45.8 0.0 copy-done.10
  45.8 4.4 %prefix.2.before_ref = bf16[128,2688]{1,0:T(8,128)(2,1)S(1)} custom-call(bf16[128,5120]{1,0:T(8,128)(2,1)} %bitcast.3.rows_ref, bf16[256,640]{1,0:T(8,128)(2,1)S(1)} %copy-done.9, bf16[256,640]{1,0:T(8,128)(2,1)S(1)} %copy-done.10, f32[128,128]{1,0:T(8,128)S(1)} %get-tuple-element.7.before_ref.private_lse_ref), custom_call_target="tpu_custom_call" | custom-call | flops 671088640000 | bytes 2621440 | tf_op jit(solution)/shard_map/prefix/pallas_call | solution.py:156
  50.2 0.0 copy-done.4
  50.2 0.0 collective-permute-done.k_ref
  50.2 0.0 collective-permute-done.1.v_ref
  50.2 5.6 %prefix.3.after_ref = bf16[128,5376]{1,0:T(8,128)(2,1)} custom-call(bf16[128,5120]{1,0:T(8,128)(2,1)} %bitcast.3.rows_ref, bf16[256,640]{1,0:T(8,128)(2,1)} %collective-permute-done.k_ref, bf16[256,640]{1,0:T(8,128)(2,1)} %collective-permute-done.1.v_ref, bf16[128,2688]{1,0:T(8,128)(2,1)S(1)} %prefix.2.before_ref), custom_call_target="tpu_custom_call" | custom-call | flops 671088640000 | bytes 2621440 | tf_op jit(solution)/shard_map/prefix/pallas_call | solution.py:156
  55.9 3.9 %all-to-all-start.1 = ((bf16[16,8,5376]{2,1,0:T(8,128)(2,1)}), bf16[16,8,5376]{2,1,0:T(8,128)(2,1)S(1)}, u32[]{:S(2)}, u32[]{:S(2)}) async-start(bf16[16,8,5376]{2,1,0:T(8,128)(2,1)} %bitcast.8), calls=%async_computation.1 | async-start | bytes 2752512 | tf_op jit(solution)/shard_map/all_to_all | solution.py:443
  60.4 0.0 copy-start.5
  60.4 0.0 copy-start.7
  60.5 4.9 %load.1.w_ref = bf16[2560,2560]{1,0:T(8,128)(2,1)S(1)} custom-call(bf16[2560,2560]{1,0:T(8,128)(2,1)} %w_hbm.1, bf16[128,5376]{1,0:T(8,128)(2,1)} %prefix.3.after_ref), custom_call_target="tpu_custom_call" | custom-call | flops 10000000000 | bytes 26214400 | tf_op jit(solution)/shard_map/load/pallas_call | solution.py:343
  65.4 0.0 copy-start
  65.4 4.7 %copy-done = bf16[2560,2560]{1,0:T(8,128)(2,1)} copy-done((bf16[2560,2560]{1,0:T(8,128)(2,1)}, bf16[2560,2560]{1,0:T(8,128)(2,1)S(1)}, u32[]{:S(2)}) %copy-start) | copy-done | bytes 13107224
  70.1 9.6 %all-to-all-done.1 = bf16[16,8,5376]{2,1,0:T(8,128)(2,1)S(1)} async-done(((bf16[16,8,5376]{2,1,0:T(8,128)(2,1)}), bf16[16,8,5376]{2,1,0:T(8,128)(2,1)S(1)}, u32[]{:S(2)}, u32[]{:S(2)}) %all-to-all-start.1) | async-done | bytes 1376288 | tf_op jit(solution)/shard_map/all_to_all | solution.py:443
  79.7 0.0 copy-done.5
  79.7 0.0 copy-done.7
  79.7 0.0 copy-start.1
  79.7 4.7 %copy-done.1 = bf16[2560,2560]{1,0:T(8,128)(2,1)S(1)} copy-done((bf16[2560,2560]{1,0:T(8,128)(2,1)S(1)}, bf16[2560,2560]{1,0:T(8,128)(2,1)}, u32[]{:S(2)}) %copy-start.1) | copy-done | bytes 13107224
  84.4 3.8 %finish.1 = bf16[128,2560]{1,0:T(8,128)(2,1)} custom-call(s32[1]{0:T(128)} %bitcast.side_ref, s32[1]{0:T(128)S(6)} %copy.11.live_ref, s32[1,128]{1,0:T(1,128)S(1)} %bitcast.12, bf16[128,5376]{1,0:T(8,128)(2,1)S(1)} %bitcast.10, f32[128,2560]{1,0:T(8,128)S(1)} %get-tuple-element.8.private_ref, f32[128,128]{1,0:T(8,128)S(1)} %copy-done.5, ...), custom_call_target="tpu_custom_call" | custom-call | flops 1677721600 | bytes 13107200 | tf_op jit(solution)/shard_map/finish/pallas_call | solution.py:401
Async XLA Ops:
  0.0 50.2 %collective-permute-start = (bf16[256,640]{1,0:T(8,128)(2,1)}, bf16[256,640]{1,0:T(8,128)(2,1)}, u32[]{:S(2)}, u32[]{:S(2)}) collective-permute-start(bf16[256,640]{1,0:T(8,128)(2,1)} %k_ref.1), channel_id=1, source_target_pairs={{0,16},{1,17},{2,18},{3,19},{4,20},{5,21},{6,22},{7,23},{8,24},{9,... | collective-permute-start | bytes 983048 | tf_op jit(solution)/shard_map/ppermute | solution.py:448
  4.0 46.2 %collective-permute-start.1 = (bf16[256,640]{1,0:T(8,128)(2,1)}, bf16[256,640]{1,0:T(8,128)(2,1)}, u32[]{:S(2)}, u32[]{:S(2)}) collective-permute-start(bf16[256,640]{1,0:T(8,128)(2,1)} %v_ref.1), channel_id=1, source_target_pairs={{0,16},{1,17},{2,18},{3,19},{4,20},{5,21},{6,22},{7,23},{8,24},{9,... | collective-permute-start | bytes 983048 | tf_op jit(solution)/shard_map/ppermute | solution.py:449
  4.1 1.1 %copy-start.2 = (bf16[128,2560]{1,0:T(8,128)(2,1)S(1)}, bf16[128,2560]{1,0:T(8,128)(2,1)}, u32[]{:S(2)}) copy-start(bf16[128,2560]{1,0:T(8,128)(2,1)} %q_hbm.3) | copy-start | bytes 1966084
  5.2 0.7 copy-start.6
  8.1 5.4 %copy-start.3 = (bf16[128,2560]{1,0:T(8,128)(2,1)S(1)}, bf16[128,2560]{1,0:T(8,128)(2,1)}, u32[]{:S(2)}) copy-start(bf16[128,2560]{1,0:T(8,128)(2,1)} %q_hbm.3) | copy-start | bytes 1966084
  8.1 5.4 %copy-start.11 = (s32[128,8]{0,1:T(8,128)S(1)}, s32[128,8]{0,1:T(8,128)}, u32[]{:S(2)}) copy-start(s32[128,8]{0,1:T(8,128)} %param.15) | copy-start | bytes 12292
  8.1 5.4 %copy-start.12 = (s32[128]{0:T(128)S(1)}, s32[128]{0:T(128)}, u32[]{:S(2)}) copy-start(s32[128]{0:T(128)} %param.16) | copy-start | bytes 1540
  8.1 37.7 %all-to-all-start = ((bf16[16,8,5120]{2,1,0:T(8,128)(2,1)}), bf16[16,8,5120]{2,1,0:T(8,128)(2,1)}, u32[]{:S(2)}, u32[]{:S(2)}) async-start(bf16[16,8,5120]{2,1,0:T(8,128)(2,1)} %bitcast.2), calls=%async_computation | async-start | bytes 2621440 | tf_op jit(solution)/shard_map/all_to_all | solution.py:443
  13.5 1.7 %copy-start.8 = (bf16[128,16,640]{2,1,0:T(8,128)(2,1)S(1)}, bf16[128,16,640]{2,1,0:T(8,128)(2,1)}, u32[]{:S(2)}) copy-start(bf16[128,16,640]{2,1,0:T(8,128)(2,1)} %param.13) | copy-start | bytes 7864324
  15.3 30.6 %copy-start.9 = (bf16[256,640]{1,0:T(8,128)(2,1)S(1)}, bf16[256,640]{1,0:T(8,128)(2,1)}, u32[]{:S(2)}) copy-start(bf16[256,640]{1,0:T(8,128)(2,1)} %k_ref.1) | copy-start | bytes 983044
  15.3 30.6 %copy-start.10 = (bf16[256,640]{1,0:T(8,128)(2,1)S(1)}, bf16[256,640]{1,0:T(8,128)(2,1)}, u32[]{:S(2)}) copy-start(bf16[256,640]{1,0:T(8,128)(2,1)} %v_ref.1) | copy-start | bytes 983044
  30.5 19.7 %copy-start.4 = (f32[128,128]{1,0:T(8,128)}, f32[128,128]{1,0:T(8,128)S(1)}, u32[]{:S(2)}) copy-start(f32[128,128]{1,0:T(8,128)S(1)} %get-tuple-element.7.before_ref.private_lse_ref) | copy-start | bytes 196612
  55.9 23.8 %all-to-all-start.1 = ((bf16[16,8,5376]{2,1,0:T(8,128)(2,1)}), bf16[16,8,5376]{2,1,0:T(8,128)(2,1)S(1)}, u32[]{:S(2)}, u32[]{:S(2)}) async-start(bf16[16,8,5376]{2,1,0:T(8,128)(2,1)} %bitcast.8), calls=%async_computation.1 | async-start | bytes 2752512 | tf_op jit(solution)/shard_map/all_to_all | solution.py:443
  60.4 19.3 %copy-start.5 = (f32[128,128]{1,0:T(8,128)S(1)}, f32[128,128]{1,0:T(8,128)}, u32[]{:S(2)}) copy-start(f32[128,128]{1,0:T(8,128)} %copy-done.4) | copy-start | bytes 196612
  60.4 19.3 %copy-start.7 = (s32[128,1]{0,1:T(1,128)S(1)}, s32[128,1]{0,1:T(1,128)}, u32[]{:S(2)}) copy-start(s32[128,1]{0,1:T(1,128)} %param.17) | copy-start | bytes 1540
  65.4 4.7 %copy-start = (bf16[2560,2560]{1,0:T(8,128)(2,1)}, bf16[2560,2560]{1,0:T(8,128)(2,1)S(1)}, u32[]{:S(2)}) copy-start(bf16[2560,2560]{1,0:T(8,128)(2,1)S(1)} %load.1.w_ref) | copy-start | bytes 39321604
  79.7 4.7 %copy-start.1 = (bf16[2560,2560]{1,0:T(8,128)(2,1)S(1)}, bf16[2560,2560]{1,0:T(8,128)(2,1)}, u32[]{:S(2)}) copy-start(bf16[2560,2560]{1,0:T(8,128)(2,1)} %copy-done) | copy-start | bytes 39321604

commit v4 on v3

v4 whole, which is shorter than its diff:
```python
import functools
import math

import jax
import jax.numpy as jnp
from jax import lax
from jax.experimental import pallas as pl
from jax.experimental.pallas import tpu as pltpu
from jax.sharding import PartitionSpec as P

H = 32
KVH = 8
HD = 80
GROUP = H // KVH
LANES = 128
WIN = 256
SCALE = HD ** (-0.5) * math.log2(math.e)
LN2 = math.log(2.0)
NEVER = -1e30
VMEM = pl.BlockSpec(memory_space=pltpu.VMEM)
SMEM = pl.BlockSpec(memory_space=pltpu.SMEM)
ANY = pl.BlockSpec(memory_space=pl.ANY)


def window(start, width):
    base = min(start // LANES * LANES, width - WIN)
    return base, start - base


def iota(shape, axis):
    return lax.broadcasted_iota(jnp.int32, shape, axis)


def params(mib):
    return pltpu.CompilerParams(vmem_limit_bytes=mib * 1024 * 1024)


def transpose_into(target, source):
    rows, cols = source.shape
    for c in range(0, cols, LANES):
        for r in range(0, rows, LANES):
            target[c : c + LANES, r : r + LANES] = source[r : r + LANES, c : c + LANES].T


def as_column(row):
    n = row.shape[1]
    same = iota((n, n), 0) == iota((n, n), 1)
    return jnp.sum(jnp.where(same, row, 0), axis=1, keepdims=True)


def slots_of(groups, half, slot_count):
    n = groups.shape[1]
    earlier = iota((n, n), 0) < iota((n, n), 1)
    same = (as_column(groups) == groups) & earlier
    rank = jnp.sum(jnp.where(same, 1, 0), axis=0, keepdims=True)
    upper = jnp.where(groups >= half, 1, 0)
    return (groups - upper * half) * slot_count + rank, upper


def place_kernel(
    half, slot_count, side_ref, groups_ref, q_hbm, out_hbm, token_ref, q_ref, out_ref, in_sems, out_sems
):
    token_ref[...] = jnp.zeros_like(token_ref)
    n, width = q_ref.shape
    steps = in_sems.shape[0]
    chunk = width // steps
    arrivals = []
    for i in range(steps):
        cols = pl.ds(i * chunk, chunk)
        arrivals.append(pltpu.make_async_copy(q_hbm.at[:, cols], q_ref.at[:, cols], in_sems.at[i]))
        arrivals[i].start()
    slot, upper = slots_of(groups_ref[...], half, slot_count)
    hit = slot == iota((n, n), 0)
    side = side_ref[0]
    own = jnp.where(hit & (upper == side), 1.0, 0.0).astype(jnp.bfloat16)
    other = jnp.where(hit & (upper != side), 1.0, 0.0).astype(jnp.bfloat16)
    spread = jnp.concatenate([own, other], axis=0)
    departures = []
    for i, arrival in enumerate(arrivals):
        arrival.wait()
        both = jnp.dot(
            spread, q_ref[:, i * chunk : (i + 1) * chunk], preferred_element_type=jnp.float32
        ).astype(jnp.bfloat16)
        for part in range(2):
            cols = pl.ds(part * width + i * chunk, chunk)
            out_ref[:, cols] = both[part * n : (part + 1) * n]
            departures.append(
                pltpu.make_async_copy(
                    out_ref.at[:, cols], out_hbm.at[:, cols], out_sems.at[2 * i + part]
                )
            )
            departures[-1].start()
    for departure in departures:
        departure.wait()


def place(queries, groups, side, half, slot_count):
    n, width = queries.shape
    steps = 4
    return pl.pallas_call(
        functools.partial(place_kernel, half, slot_count),
        out_shape=(
            jax.ShapeDtypeStruct((n, 2 * width), queries.dtype),
            jax.ShapeDtypeStruct((8, LANES), jnp.float32),
        ),
        in_specs=[SMEM, VMEM, ANY],
        out_specs=(ANY, VMEM),
        scratch_shapes=[
            pltpu.VMEM((n, width), queries.dtype),
            pltpu.VMEM((n, 2 * width), queries.dtype),
            pltpu.SemaphoreType.DMA((steps,)),
            pltpu.SemaphoreType.DMA((2 * steps,)),
        ],
        compiler_params=params(60),
        cost_estimate=pl.CostEstimate(
            flops=4 * n * n * width, bytes_accessed=6 * n * width, transcendentals=0
        ),
        name="place",
    )(side, groups, queries)


def clear_queries(qs_ref, i, k, key_width):
    _, first = window(k * HD, key_width)
    width = qs_ref.shape[2]
    if first:
        qs_ref[i, :first] = jnp.zeros((first, width), jnp.bfloat16)
    if first + HD < WIN:
        qs_ref[i, first + HD :] = jnp.zeros((WIN - first - HD, width), jnp.bfloat16)


def fill_queries(qs_ref, i, qt_ref, k, key_width):
    n = qt_ref.shape[1]
    _, first = window(k * HD, key_width)
    for g in range(GROUP):
        row = (k * GROUP + g) * HD
        qs_ref[i, first : first + HD, g * n : (g + 1) * n] = qt_ref[row : row + HD]


def prefix_kernel(
    rows_hbm, near_k, near_v, far_k, far_v, after_ref, out_hbm,
    rows_ref, k_ref, v_ref, qt_ref, vt_ref, qs_ref, ot_ref, lse_ref, scores_ref, out_ref,
    in_sems, out_sems
):
    del after_ref
    n, width = rows_ref.shape
    width //= 2
    part_width = width + LANES
    key_width = k_ref.shape[2]
    arrivals = []
    for part, (keys, values) in enumerate(((near_k, near_v), (far_k, far_v))):
        cols = pl.ds(part * width, width)
        for source, target in (
            (values, v_ref.at[part]),
            (rows_hbm.at[:, cols], rows_ref.at[:, cols]),
            (keys, k_ref.at[part]),
        ):
            arrivals.append(pltpu.make_async_copy(source, target, in_sems.at[len(arrivals)]))
            arrivals[-1].start()
    for u in range(2 * KVH):
        clear_queries(qs_ref, u, u % KVH, key_width)

    def prepare(part):
        arrivals[3 * part].wait()
        transpose_into(vt_ref.at[part], v_ref.at[part])
        arrivals[3 * part + 1].wait()
        transpose_into(qt_ref, rows_ref.at[:, part * width : (part + 1) * width])
        for k in range(KVH):
            fill_queries(qs_ref, part * KVH + k, qt_ref, k, key_width)
        arrivals[3 * part + 2].wait()

    def score(u):
        part, k = divmod(u, KVH)
        base, _ = window(k * HD, key_width)
        scores = jnp.dot(
            k_ref[part, :, base : base + WIN], qs_ref[u], preferred_element_type=jnp.float32
        )
        scores_ref[u % 2] = scores * SCALE

    def weigh(u):
        part, k = divmod(u, KVH)
        scores = scores_ref[u % 2]
        top = jnp.max(scores, axis=0, keepdims=True)
        weights = jnp.exp2(scores - top)
        total = jnp.sum(weights, axis=0, keepdims=True)
        summed = jnp.dot(
            vt_ref[part, k * HD : (k + 1) * HD],
            weights.astype(jnp.bfloat16),
            preferred_element_type=jnp.float32,
        )
        result = (summed * (1.0 / total)).astype(jnp.bfloat16)
        lse = (top + jnp.log2(total)) * LN2
        for g in range(GROUP):
            head = k * GROUP + g
            ot_ref[head * HD : (head + 1) * HD] = result[:, g * n : (g + 1) * n]
            lse_ref[head : head + 1] = lse[:, g * n : (g + 1) * n]

    def send(part):
        cols = pl.ds(part * part_width, part_width)
        view = out_ref.at[:, cols]
        transpose_into(view.at[:, :width], ot_ref)
        lse = lse_ref[...]
        high = lse.astype(jnp.bfloat16).astype(jnp.float32)
        middle = (lse - high).astype(jnp.bfloat16).astype(jnp.float32)
        pieces = jnp.concatenate([high, middle, lse - high - middle, jnp.zeros_like(lse)], axis=0)
        view[:, width:] = pieces.T.astype(jnp.bfloat16)
        copy = pltpu.make_async_copy(view, out_hbm.at[:, cols], out_sems.at[part])
        copy.start()
        return copy

    prepare(0)
    score(0)
    departures = []
    for u in range(2 * KVH):
        if u == KVH - 2:
            prepare(1)
        if u + 1 < 2 * KVH:
            score(u + 1)
        weigh(u)
        if u % KVH == KVH - 1:
            departures.append(send(u // KVH))
    for departure in departures:
        departure.wait()


def prefix_part(rows, near_k, near_v, far_k, far_v, after):
    n, width = rows.shape
    width //= 2
    tokens, key_width = near_k.shape
    return pl.pallas_call(
        prefix_kernel,
        out_shape=jax.ShapeDtypeStruct((n, 2 * (width + LANES)), jnp.bfloat16),
        in_specs=[ANY] * 6,
        out_specs=ANY,
        scratch_shapes=[
            pltpu.VMEM(rows.shape, rows.dtype),
            pltpu.VMEM((2, tokens, key_width), jnp.bfloat16),
            pltpu.VMEM((2, tokens, key_width), jnp.bfloat16),
            pltpu.VMEM((width, n), jnp.bfloat16),
            pltpu.VMEM((2, key_width, tokens), jnp.bfloat16),
            pltpu.VMEM((2 * KVH, WIN, GROUP * n), jnp.bfloat16),
            pltpu.VMEM((width, n), jnp.bfloat16),
            pltpu.VMEM((H, n), jnp.float32),
            pltpu.VMEM((2, tokens, GROUP * n), jnp.float32),
            pltpu.VMEM((n, 2 * (width + LANES)), jnp.bfloat16),
            pltpu.SemaphoreType.DMA((6,)),
            pltpu.SemaphoreType.DMA((2,)),
        ],
        compiler_params=params(60),
        cost_estimate=pl.CostEstimate(
            flops=16000 * n * 256 * width,
            bytes_accessed=8 * n * width * 2,
            transcendentals=n * 512 * H,
        ),
        name="prefix",
    )(rows, near_k, near_v, far_k, far_v, after)


def fill_bias(bias_ref, pages, lengths, page_size):
    most, n = pages.shape
    page_count = bias_ref.shape[0] // page_size
    page = iota((page_count, n), 0)
    full = jnp.zeros((page_count, n), jnp.float32)
    partial = jnp.zeros((page_count, n), jnp.float32)
    for j in range(most):
        same = pages[j : j + 1] == page
        whole = lengths >= (j + 1) * page_size
        some = (lengths > j * page_size) & (lengths < (j + 1) * page_size)
        full += jnp.where(same & whole, 1.0, 0.0)
        partial += jnp.where(same & some, 1.0, 0.0)
    seen = jnp.where(iota((page_size, n), 0) < lengths % page_size, 1.0, 0.0)
    for p in range(page_count):
        multiple = full[p : p + 1] + seen * partial[p : p + 1]
        bias_ref[p * page_size : (p + 1) * page_size] = jnp.where(
            multiple > 0.0, jnp.log2(jnp.maximum(multiple, 1.0)), NEVER
        )


def private_kernel(
    page_size, q_hbm, k_hbm, v_hbm, pages_ref, lengths_ref, after_ref,
    out_ref, lse_ref, q_ref, k_ref, v_ref, qt_ref, vt_ref, qs_ref, bias_ref, ot_ref, lses_ref,
    scores_a, scores_b, top_a, top_b, weights_ref, sems
):
    del after_ref
    copies = [
        pltpu.make_async_copy(source, target, sems.at[i])
        for i, (source, target) in enumerate(((q_hbm, q_ref), (k_hbm, k_ref), (v_hbm, v_ref)))
    ]
    for copy in copies:
        copy.start()
    n = q_ref.shape[0]
    tokens, key_width = k_ref.shape
    rows = GROUP * n
    tile = 256
    fill_bias(bias_ref, pages_ref[...], lengths_ref[...], page_size)
    copies[0].wait()
    transpose_into(qt_ref, q_ref)
    for k in range(KVH):
        clear_queries(qs_ref, k, k, key_width)
        fill_queries(qs_ref, k, qt_ref, k, key_width)
    copies[1].wait()

    def score(k, scores_ref, top_ref):
        base = pl.multiple_of(jnp.minimum(k * HD // LANES * LANES, key_width - WIN), LANES)
        top = None
        for t in range(0, tokens, tile):
            scores = jnp.dot(
                k_ref[t : t + tile, pl.ds(base, WIN)],
                qs_ref[k],
                preferred_element_type=jnp.float32,
            )
            bias = bias_ref[t : t + tile]
            scores = scores * SCALE + jnp.concatenate([bias] * GROUP, axis=1)
            scores_ref[t : t + tile] = scores
            highest = jnp.max(scores.reshape(tile // 8, 8, rows), axis=0)
            top = highest if top is None else jnp.maximum(top, highest)
        top_ref[...] = top

    def weigh(k, scores_ref, top_ref, lses):
        top = jnp.max(top_ref[...], axis=0, keepdims=True)
        total = jnp.zeros((8, rows), jnp.float32)
        for t in range(0, tokens, tile):
            weights = jnp.exp2(scores_ref[t : t + tile] - top)
            total += jnp.sum(weights.reshape(tile // 8, 8, rows), axis=0)
            weights_ref[t : t + tile] = weights.astype(jnp.bfloat16)
        total = jnp.sum(total, axis=0, keepdims=True)
        values = vt_ref[pl.ds(pl.multiple_of(k * HD, 16), HD)]
        summed = jnp.dot(values, weights_ref[...], preferred_element_type=jnp.float32)
        result = summed * (1.0 / total)
        lse = (top + jnp.log2(total)) * LN2
        row = iota(lses.shape, 0)
        for g in range(GROUP):
            head = k * GROUP + g
            ot_ref[pl.ds(pl.multiple_of(head * HD, 16), HD)] = result[:, g * n : (g + 1) * n]
            lses = jnp.where(row == head, lse[:, g * n : (g + 1) * n], lses)
        return lses

    score(0, scores_a, top_a)
    copies[2].wait()
    transpose_into(vt_ref, v_ref)

    def two(j, lses):
        k = 2 * j
        score(k + 1, scores_b, top_b)
        lses = weigh(k, scores_a, top_a, lses)
        score(jnp.minimum(k + 2, KVH - 1), scores_a, top_a)
        return weigh(k + 1, scores_b, top_b, lses)

    lses_ref[...] = jnp.zeros_like(lses_ref)
    lses_ref[:H] = lax.fori_loop(0, KVH // 2, two, jnp.zeros((H, n), jnp.float32))
    lse_ref[...] = lses_ref[...].T
    transpose_into(out_ref, ot_ref)


def private_part(queries, keys, values, pages, lengths, after, page_size):
    n, width = queries.shape
    tokens, key_width = keys.shape
    return pl.pallas_call(
        functools.partial(private_kernel, page_size),
        out_shape=(
            jax.ShapeDtypeStruct((n, width), jnp.float32),
            jax.ShapeDtypeStruct((n, LANES), jnp.float32),
        ),
        in_specs=[ANY] * 3 + [VMEM] * 2 + [ANY],
        out_specs=(VMEM, VMEM),
        scratch_shapes=[
            pltpu.VMEM(queries.shape, queries.dtype),
            pltpu.VMEM(keys.shape, keys.dtype),
            pltpu.VMEM(values.shape, values.dtype),
            pltpu.VMEM((width, n), jnp.bfloat16),
            pltpu.VMEM((key_width, tokens), jnp.bfloat16),
            pltpu.VMEM((KVH, WIN, GROUP * n), jnp.bfloat16),
            pltpu.VMEM((tokens, n), jnp.float32),
            pltpu.VMEM((width, n), jnp.float32),
            pltpu.VMEM((LANES, n), jnp.float32),
            pltpu.VMEM((tokens, GROUP * n), jnp.float32),
            pltpu.VMEM((tokens, GROUP * n), jnp.float32),
            pltpu.VMEM((8, GROUP * n), jnp.float32),
            pltpu.VMEM((8, GROUP * n), jnp.float32),
            pltpu.VMEM((tokens, GROUP * n), jnp.bfloat16),
            pltpu.SemaphoreType.DMA((3,)),
        ],
        compiler_params=params(48),
        cost_estimate=pl.CostEstimate(
            flops=1200 * n * tokens * H * WIN,
            bytes_accessed=4 * tokens * key_width,
            transcendentals=n * tokens * H,
        ),
        name="private",
    )(queries, keys, values, pages, lengths, after)


def expand_heads(share, width):
    n = share.shape[0]
    lane = iota((n, LANES), 1)
    share = jnp.where(lane < H, share, 0.0)
    high = share.astype(jnp.bfloat16).astype(jnp.float32)
    both = (high + pltpu.roll(share - high, H, 1)).astype(jnp.bfloat16)
    row = iota((LANES, width), 0)
    head = jnp.where(row >= H, row - H, row)
    first = head * HD
    column = iota((LANES, width), 1)
    spread = (row < 2 * H) & (column >= first) & (column < first + HD)
    return jnp.dot(
        both, jnp.where(spread, 1.0, 0.0).astype(jnp.bfloat16), preferred_element_type=jnp.float32
    )


def finish_kernel(
    half, slot_count, side_ref, live_ref, groups_ref, back_ref, private_lse_ref, private_hbm, w_hbm,
    out_hbm, private_ref, w_ref, out_ref, in_sems, out_sems
):
    n, width = out_ref.shape
    part = width + LANES
    steps = out_sems.shape[0]
    chunk = width // steps
    private_copy = pltpu.make_async_copy(private_hbm, private_ref, in_sems.at[steps])
    private_copy.start()
    arrivals = []
    for i in range(steps):
        cols = pl.ds(i * chunk, chunk)
        arrivals.append(pltpu.make_async_copy(w_hbm.at[:, cols], w_ref.at[:, cols], in_sems.at[i]))
        arrivals[i].start()
    slot, upper = slots_of(groups_ref[...], half, slot_count)
    slot, upper = as_column(slot), as_column(upper)
    hit = slot == iota((n, n), 1)
    side = side_ref[0]
    own = jnp.where(hit & (upper == side), 1.0, 0.0).astype(jnp.bfloat16)
    other = jnp.where(hit & (upper != side), 1.0, 0.0).astype(jnp.bfloat16)
    pick = jnp.concatenate([own, other], axis=1)

    def picked(first, last):
        both = jnp.concatenate(
            [back_ref[:, first:last], back_ref[:, part + first : part + last]], axis=0
        )
        return jnp.dot(pick, both, preferred_element_type=jnp.float32)

    pieces = picked(width, part)
    lane = iota((n, LANES), 1)
    prefix_lse = (
        pieces + pltpu.roll(pieces, LANES - H, 1) + pltpu.roll(pieces, LANES - 2 * H, 1)
    )
    prefix_lse = jnp.where(lane < H, prefix_lse, 0.0)
    private_lse = private_lse_ref[...]
    top = jnp.maximum(prefix_lse, private_lse)
    a, b = jnp.exp(prefix_lse - top), jnp.exp(private_lse - top)
    prefix_share = expand_heads(a / (a + b), width)
    private_share = expand_heads(b / (a + b), width)
    prefix = picked(0, width)
    private_copy.wait()
    attended = prefix_share * prefix + private_share * private_ref[...]
    attended = attended.astype(jnp.bfloat16)
    is_live = iota((n, 1), 0) < live_ref[0]
    departures = []
    for i, arrival in enumerate(arrivals):
        arrival.wait()
        cols = pl.ds(i * chunk, chunk)
        projected = jnp.dot(attended, w_ref[:, cols], preferred_element_type=jnp.float32)
        out_ref[:, cols] = jnp.where(is_live, projected, 0.0).astype(out_ref.dtype)
        departures.append(
            pltpu.make_async_copy(out_ref.at[:, cols], out_hbm.at[:, cols], out_sems.at[i])
        )
        departures[i].start()
    for departure in departures:
        departure.wait()


def finish(side, live, groups, back, private, private_lse, weight, half, slot_count):
    n = back.shape[0]
    width = weight.shape[1]
    steps = 5
    return pl.pallas_call(
        functools.partial(finish_kernel, half, slot_count),
        out_shape=jax.ShapeDtypeStruct((n, width), jnp.bfloat16),
        in_specs=[SMEM, SMEM] + [VMEM] * 3 + [ANY] * 2,
        out_specs=ANY,
        scratch_shapes=[
            pltpu.VMEM((n, width), jnp.float32),
            pltpu.VMEM(weight.shape, weight.dtype),
            pltpu.VMEM((n, width), jnp.bfloat16),
            pltpu.SemaphoreType.DMA((steps + 1,)),
            pltpu.SemaphoreType.DMA((steps,)),
        ],
        compiler_params=params(52),
        cost_estimate=pl.CostEstimate(
            flops=2 * n * width * width, bytes_accessed=2 * width * width, transcendentals=0
        ),
        name="finish",
    )(side, live, groups, back, private_lse, private, weight)


def per_device(
    queries,
    prefix_keys,
    prefix_values,
    pool_keys,
    pool_values,
    page_table,
    private_length,
    group_ids,
    live_rows,
    out_weight,
):
    devices = lax.axis_size("req")
    half = devices // 2
    row_count, width = queries.shape
    slot_count = 2 * row_count // devices
    page_size = pool_keys.shape[1]
    halves = [list(range(half)), list(range(half, devices))]
    across = [(i, (i + half) % devices) for i in range(devices)]
    side = (lax.axis_index("req") // half).astype(jnp.int32).reshape(1)

    groups = group_ids.reshape(1, row_count)
    lengths = private_length.reshape(1, row_count)
    pages = page_table.T
    flat_keys = pool_keys.reshape(-1, pool_keys.shape[2])
    flat_values = pool_values.reshape(-1, pool_values.shape[2])

    def exchange(rows):
        blocks = rows.reshape(half, slot_count, rows.shape[1])
        blocks = lax.all_to_all(
            blocks, "req", split_axis=0, concat_axis=0, tiled=True, axis_index_groups=halves
        )
        return blocks.reshape(rows.shape)

    far_keys = lax.ppermute(prefix_keys, "req", across)
    far_values = lax.ppermute(prefix_values, "req", across)
    placed, token = place(queries, groups, side, half, slot_count)
    rows = exchange(placed)
    private, private_lse = private_part(
        queries, flat_keys, flat_values, pages, lengths, token, page_size
    )
    out = prefix_part(rows, prefix_keys, prefix_values, far_keys, far_values, private_lse)
    back = exchange(out)
    return finish(
        side, live_rows, groups, back, private, private_lse, out_weight, half, slot_count
    )


def solution(mesh):
    placed = (
        P("req", None),
        P("req", None),
        P("req", None),
        P("req", None, None),
        P("req", None, None),
        P("req", None),
        P("req"),
        P("req", None),
        P("req"),
        P(),
    )
    return jax.shard_map(
        per_device, mesh=mesh, in_specs=placed, out_specs=P("req", None), check_vma=False
    )
```

time: 88.7 us -> 84.8 us (0.956)
  local copies, waits for them, and re-layouts: 13 us -> 3.5 us
  waiting for transfers between devices: 24.9 us -> 32.1 us
  Pallas kernels: 36.3 us -> 34 us
    unnamed x26 -> x18, local copies, waits for them, and re-layouts: 13 us -> 3.5 us
    pallas_call x4 -> x2, Pallas kernels: 30.2 us -> 21.8 us  [the longest x1 15.2 us: private_part(): pl.pallas_call(functools.partial(private_kernel, page_size), out_shape=(j...]
    ppermute x1, waiting for transfers between devices: 0.01 us -> 6.84 us  [per_device(): far_values = lax.ppermute(prefix_values, 'req', across)]
    pallas_call x1, Pallas kernels: 3.77 us -> 8.15 us  [finish(): pl.pallas_call(functools.partial(finish_kernel, half, slot_count), out_sh...]
    ppermute x1, waiting for transfers between devices: 0.01 us -> 1.96 us  [per_device(): far_keys = lax.ppermute(prefix_keys, 'req', across)]
    pallas_call x1, Pallas kernels: 2.28 us -> 4.02 us  [place(): pl.pallas_call(functools.partial(place_kernel, half, slot_count), out_sha...]
    all_to_all x2, waiting for transfers between devices: 24.9 us -> 23.3 us  [exchange(): lax.all_to_all(blocks, 'req', split_axis=0, concat_axis=0, tiled=True, ax...]
    all_to_all x2, starting transfers between devices: 9.22 us -> 10.8 us  [exchange(): lax.all_to_all(blocks, 'req', split_axis=0, concat_axis=0, tiled=True, ax...]
  transfers between devices with their start and end apart: 4 -> 4, of which waited for: 2 -> 4; matrix products, arithmetic and copies ran while one was open for 0% -> 0% of each run, Pallas kernels for 30% -> 18%
where the time goes in v4:
time: 84.8 us; the launch traced here: 84.3 us
  Pallas kernels  34 us (40%)
  waiting for transfers between devices  32.1 us (38%)
  starting transfers between devices  13.8 us (16%)
  local copies, waits for them, and re-layouts  3.5 us (4%)
  between operations  0.92 us (1%)
    all_to_all x2, waiting for transfers between devices, exchange(): lax.all_to_all(blocks, 'req', split_axis=0, concat_axis=0, tiled=True, ax...  23.3 us
    pallas_call x1, Pallas kernels, private_part(): pl.pallas_call(functools.partial(private_kernel, page_size), out_shape=(j...  15.2 us
    all_to_all x2, starting transfers between devices, exchange(): lax.all_to_all(blocks, 'req', split_axis=0, concat_axis=0, tiled=True, ax...  10.8 us
    pallas_call x1, Pallas kernels, finish(): pl.pallas_call(functools.partial(finish_kernel, half, slot_count), out_sh...  8.15 us
    ppermute x1, waiting for transfers between devices, per_device(): far_values = lax.ppermute(prefix_values, 'req', across)  6.84 us
    pallas_call x1, Pallas kernels, prefix_part(): pl.pallas_call(prefix_kernel, out_shape=jax.ShapeDtypeStruct((n, 2 * (wid...  6.58 us
    pallas_call x1, Pallas kernels, place(): pl.pallas_call(functools.partial(place_kernel, half, slot_count), out_sha...  4.02 us
    unnamed x18, local copies, waits for them, and re-layouts  3.5 us
  transfers between devices with their start and end apart: 4, of which 4 were waited for; matrix products, arithmetic and copies ran while one was open for 0% of the time, Pallas kernels for 18%

profile of v4, /device:TPU:0, one launch (start us, length us, event | category | flops | bytes accessed | tf_op | source)
XLA Modules:
  0.0 84.3 jit_solution(12628134653008271957)
XLA Ops:
  0.0 4.0 %place.1 = (bf16[128,5120]{1,0:T(8,128)(2,1)}, f32[8,128]{1,0:T(8,128)}) custom-call(s32[1]{0:T(128)} %bitcast.side_ref, s32[1,128]{1,0:T(1,128)} %bitcast.10, bf16[128,2560]{1,0:T(8,128)(2,1)} %q_hbm.3), custom_call_target="tpu_custom_call" | custom-call | flops 167772160 | bytes 1966080 | tf_op jit(solution)/shard_map/place/pallas_call | solution.py:100
  4.0 0.0 copy-start
  4.0 0.0 copy-start.5
  4.1 0.0 copy-start.6
  4.1 0.0 copy-start.7
  4.1 6.5 %all-to-all-start = ((bf16[16,8,5120]{2,1,0:T(8,128)(2,1)}), bf16[16,8,5120]{2,1,0:T(8,128)(2,1)}, u32[]{:S(2)}, u32[]{:S(2)}) async-start(bf16[16,8,5120]{2,1,0:T(8,128)(2,1)} %bitcast.17), calls=%async_computation | async-start | bytes 2621440 | tf_op jit(solution)/shard_map/all_to_all | solution.py:520
  10.6 2.7 %collective-permute-start = (bf16[256,640]{1,0:T(8,128)(2,1)}, bf16[256,640]{1,0:T(8,128)(2,1)}, u32[]{:S(2)}, u32[]{:S(2)}) collective-permute-start(bf16[256,640]{1,0:T(8,128)(2,1)} %near_k.1), channel_id=1, source_target_pairs={{0,16},{1,17},{2,18},{3,19},{4,20},{5,21},{6,22},{7,23},{8,24},{9,... | collective-permute-start | bytes 983048 | tf_op jit(solution)/shard_map/ppermute | solution.py:525
  13.2 0.3 collective-permute-start.1
  13.6 0.0 copy-done
  13.6 0.0 copy-done.5
  13.6 0.0 copy-done.6
  13.6 0.0 copy-done.7
  13.6 0.0 copy-start.4
  13.6 1.7 %copy-done.4 = bf16[128,16,640]{2,1,0:T(8,128)(2,1)S(1)} copy-done((bf16[128,16,640]{2,1,0:T(8,128)(2,1)S(1)}, bf16[128,16,640]{2,1,0:T(8,128)(2,1)}, u32[]{:S(2)}) %copy-start.4) | copy-done | bytes 2621464
  15.3 15.2 %private.1 = (f32[128,2560]{1,0:T(8,128)S(1)}, f32[128,128]{1,0:T(8,128)S(1)}) custom-call(bf16[128,2560]{1,0:T(8,128)(2,1)S(1)} %copy-done, bf16[2048,640]{1,0:T(8,128)(2,1)S(1)} %bitcast.12, bf16[2048,640]{1,0:T(8,128)(2,1)} %bitcast.18, s32[8,128]{1,0:T(8,128)S(1)} %bitcast.13, s32[1,128]{1,0:T(1,128)S(1)} %bitcast.14, f32[8,128]{1,0:T(8,128)S(1)} %copy-done.6), custom_call_target="tpu_custom_call" | custom-call | flops 2576980377600 | bytes 5242880 | tf_op jit(solution)/shard_map/private/pallas_call | solution.py:357
  30.6 0.0 copy-start.1
  30.6 0.6 copy-done.1
  31.2 2.0 %collective-permute-done.far_k = bf16[256,640]{1,0:T(8,128)(2,1)} collective-permute-done((bf16[256,640]{1,0:T(8,128)(2,1)}, bf16[256,640]{1,0:T(8,128)(2,1)}, u32[]{:S(2)}, u32[]{:S(2)}) %collective-permute-start) | collective-permute-done | bytes 327712 | tf_op jit(solution)/shard_map/ppermute | solution.py:525
  33.2 6.8 %collective-permute-done.1.far_v = bf16[256,640]{1,0:T(8,128)(2,1)} collective-permute-done((bf16[256,640]{1,0:T(8,128)(2,1)}, bf16[256,640]{1,0:T(8,128)(2,1)}, u32[]{:S(2)}, u32[]{:S(2)}) %collective-permute-start.1) | collective-permute-done | bytes 327712 | tf_op jit(solution)/shard_map/ppermute | solution.py:526
  40.0 3.8 %all-to-all-done = bf16[16,8,5120]{2,1,0:T(8,128)(2,1)} async-done(((bf16[16,8,5120]{2,1,0:T(8,128)(2,1)}), bf16[16,8,5120]{2,1,0:T(8,128)(2,1)}, u32[]{:S(2)}, u32[]{:S(2)}) %all-to-all-start) | async-done | bytes 1310752 | tf_op jit(solution)/shard_map/all_to_all | solution.py:520
  43.8 6.6 %prefix.1 = bf16[128,5376]{1,0:T(8,128)(2,1)} custom-call(bf16[128,5120]{1,0:T(8,128)(2,1)} %bitcast.3.rows_hbm, bf16[256,640]{1,0:T(8,128)(2,1)} %near_k.1, bf16[256,640]{1,0:T(8,128)(2,1)} %near_v.1, bf16[256,640]{1,0:T(8,128)(2,1)} %collective-permute-done.far_k, bf16[256,640]{1,0:T(8,128)(2,1)} %collective-permute-done.1.far_v, f32[128,128]{1,0:T(8,128)} %copy-done.1), custom_call_target="tpu_custom_call" | custom-call | flops 1342177280000 | bytes 5242880 | tf_op jit(solution)/shard_map/prefix/pallas_call | solution.py:229
  50.4 0.0 copy-start.2
  50.4 0.0 copy-start.3
  50.4 4.4 %all-to-all-start.1 = ((bf16[16,8,5376]{2,1,0:T(8,128)(2,1)}), bf16[16,8,5376]{2,1,0:T(8,128)(2,1)S(1)}, u32[]{:S(2)}, u32[]{:S(2)}) async-start(bf16[16,8,5376]{2,1,0:T(8,128)(2,1)} %bitcast.16), calls=%async_computation.1 | async-start | bytes 2752512 | tf_op jit(solution)/shard_map/all_to_all | solution.py:520
  55.4 19.5 %all-to-all-done.1 = bf16[16,8,5376]{2,1,0:T(8,128)(2,1)S(1)} async-done(((bf16[16,8,5376]{2,1,0:T(8,128)(2,1)}), bf16[16,8,5376]{2,1,0:T(8,128)(2,1)S(1)}, u32[]{:S(2)}, u32[]{:S(2)}) %all-to-all-start.1) | async-done | bytes 1376288 | tf_op jit(solution)/shard_map/all_to_all | solution.py:520
  74.9 0.0 copy-start.8
  74.9 1.1 %copy-done.8 = bf16[16,8,5376]{2,1,0:T(8,128)(2,1)} copy-done((bf16[16,8,5376]{2,1,0:T(8,128)(2,1)}, bf16[16,8,5376]{2,1,0:T(8,128)(2,1)S(1)}, u32[]{:S(2)}) %copy-start.8) | copy-done | bytes 1376280
  76.0 0.0 copy-done.2
  76.0 0.0 copy-done.3
  76.0 8.1 %finish.1 = bf16[128,2560]{1,0:T(8,128)(2,1)} custom-call(s32[1]{0:T(128)} %bitcast.side_ref, s32[1]{0:T(128)S(6)} %copy.11.live_ref, s32[1,128]{1,0:T(1,128)S(1)} %bitcast.11, bf16[128,5376]{1,0:T(8,128)(2,1)} %bitcast.15, f32[128,128]{1,0:T(8,128)S(1)} %copy-done.2, f32[128,2560]{1,0:T(8,128)S(1)} %get-tuple-element.12.private_hbm, bf16[2560,2560]{1,0:T(8,128)(2,1)} %w_hbm.1), custom_call_target="tpu_custom_call" | custom-call | flops 1677721600 | bytes 13107200 | tf_op jit(solution)/shard_map/finish/pallas_call | solution.py:471
Async XLA Ops:
  4.0 9.5 %copy-start = (bf16[128,2560]{1,0:T(8,128)(2,1)S(1)}, bf16[128,2560]{1,0:T(8,128)(2,1)}, u32[]{:S(2)}) copy-start(bf16[128,2560]{1,0:T(8,128)(2,1)} %q_hbm.3) | copy-start | bytes 1966084
  4.0 9.5 %copy-start.5 = (s32[128,8]{0,1:T(8,128)S(1)}, s32[128,8]{0,1:T(8,128)}, u32[]{:S(2)}) copy-start(s32[128,8]{0,1:T(8,128)} %param.15) | copy-start | bytes 12292
  4.1 9.5 %copy-start.6 = (f32[8,128]{1,0:T(8,128)S(1)}, f32[8,128]{1,0:T(8,128)}, u32[]{:S(2)}) copy-start(f32[8,128]{1,0:T(8,128)} %get-tuple-element.10.after_ref) | copy-start | bytes 12292
  4.1 9.5 %copy-start.7 = (s32[128]{0:T(128)S(1)}, s32[128]{0:T(128)}, u32[]{:S(2)}) copy-start(s32[128]{0:T(128)} %param.16) | copy-start | bytes 1540
  4.1 39.7 %all-to-all-start = ((bf16[16,8,5120]{2,1,0:T(8,128)(2,1)}), bf16[16,8,5120]{2,1,0:T(8,128)(2,1)}, u32[]{:S(2)}, u32[]{:S(2)}) async-start(bf16[16,8,5120]{2,1,0:T(8,128)(2,1)} %bitcast.17), calls=%async_computation | async-start | bytes 2621440 | tf_op jit(solution)/shard_map/all_to_all | solution.py:520
  10.6 22.6 %collective-permute-start = (bf16[256,640]{1,0:T(8,128)(2,1)}, bf16[256,640]{1,0:T(8,128)(2,1)}, u32[]{:S(2)}, u32[]{:S(2)}) collective-permute-start(bf16[256,640]{1,0:T(8,128)(2,1)} %near_k.1), channel_id=1, source_target_pairs={{0,16},{1,17},{2,18},{3,19},{4,20},{5,21},{6,22},{7,23},{8,24},{9,... | collective-permute-start | bytes 983048 | tf_op jit(solution)/shard_map/ppermute | solution.py:525
  13.2 26.8 %collective-permute-start.1 = (bf16[256,640]{1,0:T(8,128)(2,1)}, bf16[256,640]{1,0:T(8,128)(2,1)}, u32[]{:S(2)}, u32[]{:S(2)}) collective-permute-start(bf16[256,640]{1,0:T(8,128)(2,1)} %near_v.1), channel_id=1, source_target_pairs={{0,16},{1,17},{2,18},{3,19},{4,20},{5,21},{6,22},{7,23},{8,24},{9,... | collective-permute-start | bytes 983048 | tf_op jit(solution)/shard_map/ppermute | solution.py:526
  13.6 1.7 %copy-start.4 = (bf16[128,16,640]{2,1,0:T(8,128)(2,1)S(1)}, bf16[128,16,640]{2,1,0:T(8,128)(2,1)}, u32[]{:S(2)}) copy-start(bf16[128,16,640]{2,1,0:T(8,128)(2,1)} %param.13) | copy-start | bytes 7864324
  30.6 0.6 copy-start.1
  50.4 25.6 %copy-start.2 = (f32[128,128]{1,0:T(8,128)S(1)}, f32[128,128]{1,0:T(8,128)}, u32[]{:S(2)}) copy-start(f32[128,128]{1,0:T(8,128)} %copy-done.1) | copy-start | bytes 196612
  50.4 25.6 %copy-start.3 = (s32[128,1]{0,1:T(1,128)S(1)}, s32[128,1]{0,1:T(1,128)}, u32[]{:S(2)}) copy-start(s32[128,1]{0,1:T(1,128)} %param.17) | copy-start | bytes 1540
  50.4 24.5 %all-to-all-start.1 = ((bf16[16,8,5376]{2,1,0:T(8,128)(2,1)}), bf16[16,8,5376]{2,1,0:T(8,128)(2,1)S(1)}, u32[]{:S(2)}, u32[]{:S(2)}) async-start(bf16[16,8,5376]{2,1,0:T(8,128)(2,1)} %bitcast.16), calls=%async_computation.1 | async-start | bytes 2752512 | tf_op jit(solution)/shard_map/all_to_all | solution.py:520
  74.9 1.1 %copy-start.8 = (bf16[16,8,5376]{2,1,0:T(8,128)(2,1)}, bf16[16,8,5376]{2,1,0:T(8,128)(2,1)S(1)}, u32[]{:S(2)}) copy-start(bf16[16,8,5376]{2,1,0:T(8,128)(2,1)S(1)} %all-to-all-done.1) | copy-start | bytes 4128772

commit v5 on v4

--- a/solution.py
+++ b/solution.py
@@ -58,24 +58,27 @@
 
 
 def place_kernel(
-    half, slot_count, side_ref, groups_ref, q_hbm, out_hbm, token_ref, q_ref, out_ref, in_sems, out_sems
+    half, slot_count, groups_hbm, q_hbm, out_ref, token_ref, groups_ref, q_ref,
+    group_sem, in_sems
 ):
-    token_ref[...] = jnp.zeros_like(token_ref)
     n, width = q_ref.shape
     steps = in_sems.shape[0]
     chunk = width // steps
+    groups_copy = pltpu.make_async_copy(groups_hbm, groups_ref, group_sem)
+    groups_copy.start()
     arrivals = []
     for i in range(steps):
         cols = pl.ds(i * chunk, chunk)
         arrivals.append(pltpu.make_async_copy(q_hbm.at[:, cols], q_ref.at[:, cols], in_sems.at[i]))
         arrivals[i].start()
+    token_ref[...] = jnp.zeros_like(token_ref)
+    side = lax.axis_index("req") // half
+    groups_copy.wait()
     slot, upper = slots_of(groups_ref[...], half, slot_count)
     hit = slot == iota((n, n), 0)
-    side = side_ref[0]
     own = jnp.where(hit & (upper == side), 1.0, 0.0).astype(jnp.bfloat16)
     other = jnp.where(hit & (upper != side), 1.0, 0.0).astype(jnp.bfloat16)
     spread = jnp.concatenate([own, other], axis=0)
-    departures = []
     for i, arrival in enumerate(arrivals):
         arrival.wait()
         both = jnp.dot(
@@ -84,39 +87,31 @@
         for part in range(2):
             cols = pl.ds(part * width + i * chunk, chunk)
             out_ref[:, cols] = both[part * n : (part + 1) * n]
-            departures.append(
-                pltpu.make_async_copy(
-                    out_ref.at[:, cols], out_hbm.at[:, cols], out_sems.at[2 * i + part]
-                )
-            )
-            departures[-1].start()
-    for departure in departures:
-        departure.wait()
-
-
-def place(queries, groups, side, half, slot_count):
+
+
+def place(queries, groups, half, slot_count):
     n, width = queries.shape
-    steps = 4
+    steps = 2
     return pl.pallas_call(
         functools.partial(place_kernel, half, slot_count),
         out_shape=(
             jax.ShapeDtypeStruct((n, 2 * width), queries.dtype),
             jax.ShapeDtypeStruct((8, LANES), jnp.float32),
         ),
-        in_specs=[SMEM, VMEM, ANY],
-        out_specs=(ANY, VMEM),
+        in_specs=[ANY, ANY],
+        out_specs=(VMEM, VMEM),
         scratch_shapes=[
+            pltpu.VMEM(groups.shape, groups.dtype),
             pltpu.VMEM((n, width), queries.dtype),
-            pltpu.VMEM((n, 2 * width), queries.dtype),
+            pltpu.SemaphoreType.DMA(()),
             pltpu.SemaphoreType.DMA((steps,)),
-            pltpu.SemaphoreType.DMA((2 * steps,)),
         ],
         compiler_params=params(60),
         cost_estimate=pl.CostEstimate(
             flops=4 * n * n * width, bytes_accessed=6 * n * width, transcendentals=0
         ),
         name="place",
-    )(side, groups, queries)
+    )(groups, queries)
 
 
 def clear_queries(qs_ref, i, k, key_width):
@@ -194,30 +189,42 @@
             ot_ref[head * HD : (head + 1) * HD] = result[:, g * n : (g + 1) * n]
             lse_ref[head : head + 1] = lse[:, g * n : (g + 1) * n]
 
-    def send(part):
-        cols = pl.ds(part * part_width, part_width)
-        view = out_ref.at[:, cols]
-        transpose_into(view.at[:, :width], ot_ref)
+    def depart(cols):
+        departures.append(
+            pltpu.make_async_copy(
+                out_ref.at[:, cols], out_hbm.at[:, cols], out_sems.at[len(departures)]
+            )
+        )
+        departures[-1].start()
+
+    def send(u):
+        part, k = divmod(u, KVH)
+        quarter = width // 4
+        first = k // 2 * quarter
+        cols = pl.ds(part * part_width + first, quarter)
+        transpose_into(out_ref.at[:, cols], ot_ref.at[first : first + quarter])
+        depart(cols)
+        if k < KVH - 1:
+            return
         lse = lse_ref[...]
         high = lse.astype(jnp.bfloat16).astype(jnp.float32)
         middle = (lse - high).astype(jnp.bfloat16).astype(jnp.float32)
         pieces = jnp.concatenate([high, middle, lse - high - middle, jnp.zeros_like(lse)], axis=0)
-        view[:, width:] = pieces.T.astype(jnp.bfloat16)
-        copy = pltpu.make_async_copy(view, out_hbm.at[:, cols], out_sems.at[part])
-        copy.start()
-        return copy
-
+        cols = pl.ds(part * part_width + width, LANES)
+        out_ref[:, cols] = pieces.T.astype(jnp.bfloat16)
+        depart(cols)
+
+    departures = []
     prepare(0)
     score(0)
-    departures = []
     for u in range(2 * KVH):
         if u == KVH - 2:
             prepare(1)
         if u + 1 < 2 * KVH:
             score(u + 1)
         weigh(u)
-        if u % KVH == KVH - 1:
-            departures.append(send(u // KVH))
+        if u % 2:
+            send(u)
     for departure in departures:
         departure.wait()
 
@@ -243,9 +250,9 @@
             pltpu.VMEM((2, tokens, GROUP * n), jnp.float32),
             pltpu.VMEM((n, 2 * (width + LANES)), jnp.bfloat16),
             pltpu.SemaphoreType.DMA((6,)),
-            pltpu.SemaphoreType.DMA((2,)),
+            pltpu.SemaphoreType.DMA((10,)),
         ],
-        compiler_params=params(60),
+        compiler_params=params(24),
         cost_estimate=pl.CostEstimate(
             flops=16000 * n * 256 * width,
             bytes_accessed=8 * n * width * 2,
@@ -405,25 +412,31 @@
     )
 
 
+def column_blocks(width):
+    blocks, first = [], 0
+    while first < width:
+        rest = width - first
+        size = min(512, max(LANES, rest // 2 // LANES * LANES))
+        blocks.append(pl.ds(first, size))
+        first += size
+    return blocks
+
+
 def finish_kernel(
-    half, slot_count, side_ref, live_ref, groups_ref, back_ref, private_lse_ref, private_hbm, w_hbm,
-    out_hbm, private_ref, w_ref, out_ref, in_sems, out_sems
+    half, slot_count, live_ref, groups_ref, back_ref, private_ref, private_lse_ref, w_hbm,
+    out_hbm, w_ref, out_ref, in_sems, out_sems
 ):
     n, width = out_ref.shape
     part = width + LANES
-    steps = out_sems.shape[0]
-    chunk = width // steps
-    private_copy = pltpu.make_async_copy(private_hbm, private_ref, in_sems.at[steps])
-    private_copy.start()
+    blocks = column_blocks(width)
     arrivals = []
-    for i in range(steps):
-        cols = pl.ds(i * chunk, chunk)
+    for i, cols in enumerate(blocks):
         arrivals.append(pltpu.make_async_copy(w_hbm.at[:, cols], w_ref.at[:, cols], in_sems.at[i]))
         arrivals[i].start()
     slot, upper = slots_of(groups_ref[...], half, slot_count)
     slot, upper = as_column(slot), as_column(upper)
     hit = slot == iota((n, n), 1)
-    side = side_ref[0]
+    side = lax.axis_index("req") // half
     own = jnp.where(hit & (upper == side), 1.0, 0.0).astype(jnp.bfloat16)
     other = jnp.where(hit & (upper != side), 1.0, 0.0).astype(jnp.bfloat16)
     pick = jnp.concatenate([own, other], axis=1)
@@ -446,14 +459,12 @@
     prefix_share = expand_heads(a / (a + b), width)
     private_share = expand_heads(b / (a + b), width)
     prefix = picked(0, width)
-    private_copy.wait()
     attended = prefix_share * prefix + private_share * private_ref[...]
     attended = attended.astype(jnp.bfloat16)
     is_live = iota((n, 1), 0) < live_ref[0]
     departures = []
-    for i, arrival in enumerate(arrivals):
+    for i, (arrival, cols) in enumerate(zip(arrivals, blocks)):
         arrival.wait()
-        cols = pl.ds(i * chunk, chunk)
         projected = jnp.dot(attended, w_ref[:, cols], preferred_element_type=jnp.float32)
         out_ref[:, cols] = jnp.where(is_live, projected, 0.0).astype(out_ref.dtype)
         departures.append(
@@ -464,28 +475,27 @@
         departure.wait()
 
 
-def finish(side, live, groups, back, private, private_lse, weight, half, slot_count):
+def finish(live, groups, back, private, private_lse, weight, half, slot_count):
     n = back.shape[0]
     width = weight.shape[1]
-    steps = 5
+    steps = len(column_blocks(width))
     return pl.pallas_call(
         functools.partial(finish_kernel, half, slot_count),
         out_shape=jax.ShapeDtypeStruct((n, width), jnp.bfloat16),
-        in_specs=[SMEM, SMEM] + [VMEM] * 3 + [ANY] * 2,
+        in_specs=[SMEM] + [VMEM] * 4 + [ANY],
         out_specs=ANY,
         scratch_shapes=[
-            pltpu.VMEM((n, width), jnp.float32),
             pltpu.VMEM(weight.shape, weight.dtype),
             pltpu.VMEM((n, width), jnp.bfloat16),
-            pltpu.SemaphoreType.DMA((steps + 1,)),
+            pltpu.SemaphoreType.DMA((steps,)),
             pltpu.SemaphoreType.DMA((steps,)),
         ],
-        compiler_params=params(52),
+        compiler_params=params(50),
         cost_estimate=pl.CostEstimate(
             flops=2 * n * width * width, bytes_accessed=2 * width * width, transcendentals=0
         ),
         name="finish",
-    )(side, live, groups, back, private_lse, private, weight)
+    )(live, groups, back, private, private_lse, weight)
 
 
 def per_device(
@@ -507,7 +517,6 @@
     page_size = pool_keys.shape[1]
     halves = [list(range(half)), list(range(half, devices))]
     across = [(i, (i + half) % devices) for i in range(devices)]
-    side = (lax.axis_index("req") // half).astype(jnp.int32).reshape(1)
 
     groups = group_ids.reshape(1, row_count)
     lengths = private_length.reshape(1, row_count)
@@ -524,7 +533,7 @@
 
     far_keys = lax.ppermute(prefix_keys, "req", across)
     far_values = lax.ppermute(prefix_values, "req", across)
-    placed, token = place(queries, groups, side, half, slot_count)
+    placed, token = place(queries, groups, half, slot_count)
     rows = exchange(placed)
     private, private_lse = private_part(
         queries, flat_keys, flat_values, pages, lengths, token, page_size
@@ -532,7 +541,7 @@
     out = prefix_part(rows, prefix_keys, prefix_values, far_keys, far_values, private_lse)
     back = exchange(out)
     return finish(
-        side, live_rows, groups, back, private, private_lse, out_weight, half, slot_count
+        live_rows, groups, back, private, private_lse, out_weight, half, slot_count
     )
 
 

time: 84.8 us -> 80.9 us (0.954)
  Pallas kernels: 34 us -> 31.9 us
  local copies, waits for them, and re-layouts: 3.5 us -> 1.77 us
    unnamed x18 -> x12, local copies, waits for them, and re-layouts: 3.5 us -> 1.77 us
    pallas_call x1, Pallas kernels: 4.02 us -> 2.79 us  [place(): pl.pallas_call(functools.partial(place_kernel, half, slot_count), out_sha...]
    pallas_call x1, Pallas kernels: 8.15 us -> 6.96 us  [finish(): pl.pallas_call(functools.partial(finish_kernel, half, slot_count), out_sh...]
  transfers between devices with their start and end apart: 4 -> 4, of which waited for: 4 -> 4; matrix products, arithmetic and copies ran while one was open for 0% -> 0% of each run, Pallas kernels for 18% -> 19%
where the time goes in v5:
time: 80.9 us; the launch traced here: 80.6 us
  waiting for transfers between devices  32.3 us (40%)
  Pallas kernels  31.9 us (39%)
  starting transfers between devices  13.7 us (17%)
  local copies, waits for them, and re-layouts  1.77 us (2%)
  between operations  0.9 us (1%)
    all_to_all x2, waiting for transfers between devices, exchange(): lax.all_to_all(blocks, 'req', split_axis=0, concat_axis=0, tiled=True, ax...  23.3 us
    pallas_call x1, Pallas kernels, private_part(): pl.pallas_call(functools.partial(private_kernel, page_size), out_shape=(j...  15.6 us
    all_to_all x2, starting transfers between devices, exchange(): lax.all_to_all(blocks, 'req', split_axis=0, concat_axis=0, tiled=True, ax...  10.7 us
    pallas_call x1, Pallas kernels, finish(): pl.pallas_call(functools.partial(finish_kernel, half, slot_count), out_sh...  6.96 us
    ppermute x1, waiting for transfers between devices, per_device(): far_values = lax.ppermute(prefix_values, 'req', across)  6.83 us
    pallas_call x1, Pallas kernels, prefix_part(): pl.pallas_call(prefix_kernel, out_shape=jax.ShapeDtypeStruct((n, 2 * (wid...  6.51 us
    pallas_call x1, Pallas kernels, place(): pl.pallas_call(functools.partial(place_kernel, half, slot_count), out_sha...  2.79 us
    ppermute x1, starting transfers between devices, per_device(): far_keys = lax.ppermute(prefix_keys, 'req', across)  2.67 us
  transfers between devices with their start and end apart: 4, of which 4 were waited for; matrix products, arithmetic and copies ran while one was open for 0% of the time, Pallas kernels for 19%

profile of v5, /device:TPU:0, one launch (start us, length us, event | category | flops | bytes accessed | tf_op | source)
XLA Modules:
  0.0 80.6 jit_solution(15033691607626588552)
XLA Ops:
  0.0 2.8 %place.1 = (bf16[128,5120]{1,0:T(8,128)(2,1)}, f32[8,128]{1,0:T(8,128)}) custom-call(s32[1,128]{1,0:T(1,128)} %bitcast.10, bf16[128,2560]{1,0:T(8,128)(2,1)} %q_hbm.3), custom_call_target="tpu_custom_call" | custom-call | flops 167772160 | bytes 1966080 | tf_op jit(solution)/shard_map/place/pallas_call | solution.py:95
  2.8 0.0 copy-start
  2.8 0.0 copy-start.3
  2.8 0.0 copy-start.4
  2.8 0.0 copy-start.5
  2.8 6.5 %all-to-all-start = ((bf16[16,8,5120]{2,1,0:T(8,128)(2,1)}), bf16[16,8,5120]{2,1,0:T(8,128)(2,1)}, u32[]{:S(2)}, u32[]{:S(2)}) async-start(bf16[16,8,5120]{2,1,0:T(8,128)(2,1)} %bitcast.15), calls=%async_computation | async-start | bytes 2621440 | tf_op jit(solution)/shard_map/all_to_all | solution.py:529
  9.3 2.7 %collective-permute-start = (bf16[256,640]{1,0:T(8,128)(2,1)}, bf16[256,640]{1,0:T(8,128)(2,1)}, u32[]{:S(2)}, u32[]{:S(2)}) collective-permute-start(bf16[256,640]{1,0:T(8,128)(2,1)} %near_k.1), channel_id=1, source_target_pairs={{0,16},{1,17},{2,18},{3,19},{4,20},{5,21},{6,22},{7,23},{8,24},{9,... | collective-permute-start | bytes 983048 | tf_op jit(solution)/shard_map/ppermute | solution.py:534
  12.0 0.3 collective-permute-start.1
  12.3 0.0 copy-done
  12.3 0.0 copy-done.3
  12.3 0.0 copy-done.4
  12.3 0.0 copy-done.5
  12.3 0.0 copy-start.2
  12.3 1.7 %copy-done.2 = bf16[128,16,640]{2,1,0:T(8,128)(2,1)S(1)} copy-done((bf16[128,16,640]{2,1,0:T(8,128)(2,1)S(1)}, bf16[128,16,640]{2,1,0:T(8,128)(2,1)}, u32[]{:S(2)}) %copy-start.2) | copy-done | bytes 2621464
  14.1 15.6 %private.1 = (f32[128,2560]{1,0:T(8,128)S(1)}, f32[128,128]{1,0:T(8,128)S(1)}) custom-call(bf16[128,2560]{1,0:T(8,128)(2,1)S(1)} %copy-done, bf16[2048,640]{1,0:T(8,128)(2,1)S(1)} %bitcast.12, bf16[2048,640]{1,0:T(8,128)(2,1)} %bitcast.16, s32[8,128]{1,0:T(8,128)S(1)} %bitcast.13, s32[1,128]{1,0:T(1,128)S(1)} %bitcast.14, f32[8,128]{1,0:T(8,128)S(1)} %copy-done.4), custom_call_target="tpu_custom_call" | custom-call | flops 2576980377600 | bytes 5242880 | tf_op jit(solution)/shard_map/private/pallas_call | solution.py:364
  29.7 2.2 %collective-permute-done.far_k = bf16[256,640]{1,0:T(8,128)(2,1)} collective-permute-done((bf16[256,640]{1,0:T(8,128)(2,1)}, bf16[256,640]{1,0:T(8,128)(2,1)}, u32[]{:S(2)}, u32[]{:S(2)}) %collective-permute-start) | collective-permute-done | bytes 327712 | tf_op jit(solution)/shard_map/ppermute | solution.py:534
  31.9 6.8 %collective-permute-done.1.far_v = bf16[256,640]{1,0:T(8,128)(2,1)} collective-permute-done((bf16[256,640]{1,0:T(8,128)(2,1)}, bf16[256,640]{1,0:T(8,128)(2,1)}, u32[]{:S(2)}, u32[]{:S(2)}) %collective-permute-start.1) | collective-permute-done | bytes 327712 | tf_op jit(solution)/shard_map/ppermute | solution.py:535
  38.8 3.8 %all-to-all-done = bf16[16,8,5120]{2,1,0:T(8,128)(2,1)} async-done(((bf16[16,8,5120]{2,1,0:T(8,128)(2,1)}), bf16[16,8,5120]{2,1,0:T(8,128)(2,1)}, u32[]{:S(2)}, u32[]{:S(2)}) %all-to-all-start) | async-done | bytes 1310752 | tf_op jit(solution)/shard_map/all_to_all | solution.py:529
  42.5 6.5 %prefix.1 = bf16[128,5376]{1,0:T(8,128)(2,1)} custom-call(bf16[128,5120]{1,0:T(8,128)(2,1)} %bitcast.2.rows_hbm, bf16[256,640]{1,0:T(8,128)(2,1)} %near_k.1, bf16[256,640]{1,0:T(8,128)(2,1)} %near_v.1, bf16[256,640]{1,0:T(8,128)(2,1)} %collective-permute-done.far_k, bf16[256,640]{1,0:T(8,128)(2,1)} %collective-permute-done.1.far_v, ...), custom_call_target="tpu_custom_call" | custom-call | flops 1342177280000 | bytes 5242880 | tf_op jit(solution)/shard_map/prefix/pallas_call | solution.py:236
  49.1 0.0 copy-start.1
  49.1 4.2 %all-to-all-start.1 = ((bf16[16,8,5376]{2,1,0:T(8,128)(2,1)}), bf16[16,8,5376]{2,1,0:T(8,128)(2,1)S(1)}, u32[]{:S(2)}, u32[]{:S(2)}) async-start(bf16[16,8,5376]{2,1,0:T(8,128)(2,1)} %bitcast.7), calls=%async_computation.1 | async-start | bytes 2752512 | tf_op jit(solution)/shard_map/all_to_all | solution.py:529
  54.0 19.5 %all-to-all-done.1 = bf16[16,8,5376]{2,1,0:T(8,128)(2,1)S(1)} async-done(((bf16[16,8,5376]{2,1,0:T(8,128)(2,1)}), bf16[16,8,5376]{2,1,0:T(8,128)(2,1)S(1)}, u32[]{:S(2)}, u32[]{:S(2)}) %all-to-all-start.1) | async-done | bytes 1376288 | tf_op jit(solution)/shard_map/all_to_all | solution.py:529
  73.4 0.0 copy-done.1
  73.4 7.0 %finish.1 = bf16[128,2560]{1,0:T(8,128)(2,1)} custom-call(s32[1]{0:T(128)S(6)} %copy.11.live_ref, s32[1,128]{1,0:T(1,128)S(1)} %bitcast.11, bf16[128,5376]{1,0:T(8,128)(2,1)S(1)} %bitcast.9, f32[128,2560]{1,0:T(8,128)S(1)} %get-tuple-element.12.private_ref, f32[128,128]{1,0:T(8,128)S(1)} %get-tuple-element.11.after_ref.private_lse_ref, bf16[2560,2560]{1,0:T(8,128)(2,1)} %w_hbm.1), custom_call_target="tpu_custom_call" | custom-call | flops 1677721600 | bytes 13107200 | tf_op jit(solution)/shard_map/finish/pallas_call | solution.py:482
Async XLA Ops:
  2.8 9.5 %copy-start = (bf16[128,2560]{1,0:T(8,128)(2,1)S(1)}, bf16[128,2560]{1,0:T(8,128)(2,1)}, u32[]{:S(2)}) copy-start(bf16[128,2560]{1,0:T(8,128)(2,1)} %q_hbm.3) | copy-start | bytes 1966084
  2.8 9.5 %copy-start.3 = (s32[128,8]{0,1:T(8,128)S(1)}, s32[128,8]{0,1:T(8,128)}, u32[]{:S(2)}) copy-start(s32[128,8]{0,1:T(8,128)} %param.15) | copy-start | bytes 12292
  2.8 9.5 %copy-start.4 = (f32[8,128]{1,0:T(8,128)S(1)}, f32[8,128]{1,0:T(8,128)}, u32[]{:S(2)}) copy-start(f32[8,128]{1,0:T(8,128)} %get-tuple-element.10.after_ref) | copy-start | bytes 12292
  2.8 9.5 %copy-start.5 = (s32[128]{0:T(128)S(1)}, s32[128]{0:T(128)}, u32[]{:S(2)}) copy-start(s32[128]{0:T(128)} %param.16) | copy-start | bytes 1540
  2.8 39.7 %all-to-all-start = ((bf16[16,8,5120]{2,1,0:T(8,128)(2,1)}), bf16[16,8,5120]{2,1,0:T(8,128)(2,1)}, u32[]{:S(2)}, u32[]{:S(2)}) async-start(bf16[16,8,5120]{2,1,0:T(8,128)(2,1)} %bitcast.15), calls=%async_computation | async-start | bytes 2621440 | tf_op jit(solution)/shard_map/all_to_all | solution.py:529
  9.3 22.6 %collective-permute-start = (bf16[256,640]{1,0:T(8,128)(2,1)}, bf16[256,640]{1,0:T(8,128)(2,1)}, u32[]{:S(2)}, u32[]{:S(2)}) collective-permute-start(bf16[256,640]{1,0:T(8,128)(2,1)} %near_k.1), channel_id=1, source_target_pairs={{0,16},{1,17},{2,18},{3,19},{4,20},{5,21},{6,22},{7,23},{8,24},{9,... | collective-permute-start | bytes 983048 | tf_op jit(solution)/shard_map/ppermute | solution.py:534
  12.0 26.8 %collective-permute-start.1 = (bf16[256,640]{1,0:T(8,128)(2,1)}, bf16[256,640]{1,0:T(8,128)(2,1)}, u32[]{:S(2)}, u32[]{:S(2)}) collective-permute-start(bf16[256,640]{1,0:T(8,128)(2,1)} %near_v.1), channel_id=1, source_target_pairs={{0,16},{1,17},{2,18},{3,19},{4,20},{5,21},{6,22},{7,23},{8,24},{9,... | collective-permute-start | bytes 983048 | tf_op jit(solution)/shard_map/ppermute | solution.py:535
  12.3 1.7 %copy-start.2 = (bf16[128,16,640]{2,1,0:T(8,128)(2,1)S(1)}, bf16[128,16,640]{2,1,0:T(8,128)(2,1)}, u32[]{:S(2)}) copy-start(bf16[128,16,640]{2,1,0:T(8,128)(2,1)} %param.13) | copy-start | bytes 7864324
  49.1 24.4 %copy-start.1 = (s32[128,1]{0,1:T(1,128)S(1)}, s32[128,1]{0,1:T(1,128)}, u32[]{:S(2)}) copy-start(s32[128,1]{0,1:T(1,128)} %param.17) | copy-start | bytes 1540
  49.1 24.4 %all-to-all-start.1 = ((bf16[16,8,5376]{2,1,0:T(8,128)(2,1)}), bf16[16,8,5376]{2,1,0:T(8,128)(2,1)S(1)}, u32[]{:S(2)}, u32[]{:S(2)}) async-start(bf16[16,8,5376]{2,1,0:T(8,128)(2,1)} %bitcast.7), calls=%async_computation.1 | async-start | bytes 2752512 | tf_op jit(solution)/shard_map/all_to_all | solution.py:529

commit v6 on v5

--- a/solution.py
+++ b/solution.py
@@ -25,6 +25,12 @@
 def window(start, width):
     base = min(start // LANES * LANES, width - WIN)
     return base, start - base
+
+
+def tight_window(start, width):
+    if start % LANES + HD <= LANES:
+        return start // LANES * LANES, start % LANES, LANES
+    return (*window(start, width), WIN)
 
 
 def iota(shape, axis):
@@ -114,18 +120,16 @@
     )(groups, queries)
 
 
-def clear_queries(qs_ref, i, k, key_width):
-    _, first = window(k * HD, key_width)
+def clear_queries(qs_ref, i, first, size):
     width = qs_ref.shape[2]
     if first:
         qs_ref[i, :first] = jnp.zeros((first, width), jnp.bfloat16)
-    if first + HD < WIN:
-        qs_ref[i, first + HD :] = jnp.zeros((WIN - first - HD, width), jnp.bfloat16)
-
-
-def fill_queries(qs_ref, i, qt_ref, k, key_width):
+    if first + HD < size:
+        qs_ref[i, first + HD : size] = jnp.zeros((size - first - HD, width), jnp.bfloat16)
+
+
+def fill_queries(qs_ref, i, qt_ref, k, first):
     n = qt_ref.shape[1]
-    _, first = window(k * HD, key_width)
     for g in range(GROUP):
         row = (k * GROUP + g) * HD
         qs_ref[i, first : first + HD, g * n : (g + 1) * n] = qt_ref[row : row + HD]
@@ -139,7 +143,6 @@
     del after_ref
     n, width = rows_ref.shape
     width //= 2
-    part_width = width + LANES
     key_width = k_ref.shape[2]
     arrivals = []
     for part, (keys, values) in enumerate(((near_k, near_v), (far_k, far_v))):
@@ -151,8 +154,9 @@
         ):
             arrivals.append(pltpu.make_async_copy(source, target, in_sems.at[len(arrivals)]))
             arrivals[-1].start()
+    windows = [tight_window(k * HD, key_width) for k in range(KVH)]
     for u in range(2 * KVH):
-        clear_queries(qs_ref, u, u % KVH, key_width)
+        clear_queries(qs_ref, u, *windows[u % KVH][1:])
 
     def prepare(part):
         arrivals[3 * part].wait()
@@ -160,14 +164,14 @@
         arrivals[3 * part + 1].wait()
         transpose_into(qt_ref, rows_ref.at[:, part * width : (part + 1) * width])
         for k in range(KVH):
-            fill_queries(qs_ref, part * KVH + k, qt_ref, k, key_width)
+            fill_queries(qs_ref, part * KVH + k, qt_ref, k, windows[k][1])
         arrivals[3 * part + 2].wait()
 
     def score(u):
         part, k = divmod(u, KVH)
-        base, _ = window(k * HD, key_width)
+        base, _, size = windows[k]
         scores = jnp.dot(
-            k_ref[part, :, base : base + WIN], qs_ref[u], preferred_element_type=jnp.float32
+            k_ref[part, :, base : base + size], qs_ref[u, :size], preferred_element_type=jnp.float32
         )
         scores_ref[u % 2] = scores * SCALE
 
@@ -187,7 +191,7 @@
         for g in range(GROUP):
             head = k * GROUP + g
             ot_ref[head * HD : (head + 1) * HD] = result[:, g * n : (g + 1) * n]
-            lse_ref[head : head + 1] = lse[:, g * n : (g + 1) * n]
+            lse_ref[part * H + head : part * H + head + 1] = lse[:, g * n : (g + 1) * n]
 
     def depart(cols):
         departures.append(
@@ -201,16 +205,16 @@
         part, k = divmod(u, KVH)
         quarter = width // 4
         first = k // 2 * quarter
-        cols = pl.ds(part * part_width + first, quarter)
+        cols = pl.ds(part * width + first, quarter)
         transpose_into(out_ref.at[:, cols], ot_ref.at[first : first + quarter])
         depart(cols)
-        if k < KVH - 1:
+        if u < 2 * KVH - 1:
             return
         lse = lse_ref[...]
         high = lse.astype(jnp.bfloat16).astype(jnp.float32)
-        middle = (lse - high).astype(jnp.bfloat16).astype(jnp.float32)
-        pieces = jnp.concatenate([high, middle, lse - high - middle, jnp.zeros_like(lse)], axis=0)
-        cols = pl.ds(part * part_width + width, LANES)
+        rest = lse - high
+        pieces = jnp.concatenate([high[:H], rest[:H], high[H:], rest[H:]], axis=0)
+        cols = pl.ds(2 * width, LANES)
         out_ref[:, cols] = pieces.T.astype(jnp.bfloat16)
         depart(cols)
 
@@ -235,7 +239,7 @@
     tokens, key_width = near_k.shape
     return pl.pallas_call(
         prefix_kernel,
-        out_shape=jax.ShapeDtypeStruct((n, 2 * (width + LANES)), jnp.bfloat16),
+        out_shape=jax.ShapeDtypeStruct((n, 2 * width + LANES), jnp.bfloat16),
         in_specs=[ANY] * 6,
         out_specs=ANY,
         scratch_shapes=[
@@ -246,11 +250,11 @@
             pltpu.VMEM((2, key_width, tokens), jnp.bfloat16),
             pltpu.VMEM((2 * KVH, WIN, GROUP * n), jnp.bfloat16),
             pltpu.VMEM((width, n), jnp.bfloat16),
-            pltpu.VMEM((H, n), jnp.float32),
+            pltpu.VMEM((2 * H, n), jnp.float32),
             pltpu.VMEM((2, tokens, GROUP * n), jnp.float32),
-            pltpu.VMEM((n, 2 * (width + LANES)), jnp.bfloat16),
+            pltpu.VMEM((n, 2 * width + LANES), jnp.bfloat16),
             pltpu.SemaphoreType.DMA((6,)),
-            pltpu.SemaphoreType.DMA((10,)),
+            pltpu.SemaphoreType.DMA((9,)),
         ],
         compiler_params=params(24),
         cost_estimate=pl.CostEstimate(
@@ -302,8 +306,9 @@
     copies[0].wait()
     transpose_into(qt_ref, q_ref)
     for k in range(KVH):
-        clear_queries(qs_ref, k, k, key_width)
-        fill_queries(qs_ref, k, qt_ref, k, key_width)
+        _, first = window(k * HD, key_width)
+        clear_queries(qs_ref, k, first, WIN)
+        fill_queries(qs_ref, k, qt_ref, k, first)
     copies[1].wait()
 
     def score(k, scores_ref, top_ref):
@@ -412,26 +417,25 @@
     )
 
 
-def column_blocks(width):
+def row_blocks(rows):
     blocks, first = [], 0
-    while first < width:
-        rest = width - first
+    while first < rows:
+        rest = rows - first
         size = min(512, max(LANES, rest // 2 // LANES * LANES))
-        blocks.append(pl.ds(first, size))
+        blocks.append(slice(first, first + size))
         first += size
     return blocks
 
 
 def finish_kernel(
     half, slot_count, live_ref, groups_ref, back_ref, private_ref, private_lse_ref, w_hbm,
-    out_hbm, w_ref, out_ref, in_sems, out_sems
+    out_hbm, w_ref, sum_ref, out_ref, in_sems, out_sems
 ):
     n, width = out_ref.shape
-    part = width + LANES
-    blocks = column_blocks(width)
+    blocks = row_blocks(width)
     arrivals = []
-    for i, cols in enumerate(blocks):
-        arrivals.append(pltpu.make_async_copy(w_hbm.at[:, cols], w_ref.at[:, cols], in_sems.at[i]))
+    for i, block in enumerate(blocks):
+        arrivals.append(pltpu.make_async_copy(w_hbm.at[block], w_ref.at[block], in_sems.at[i]))
         arrivals[i].start()
     slot, upper = slots_of(groups_ref[...], half, slot_count)
     slot, upper = as_column(slot), as_column(upper)
@@ -439,38 +443,47 @@
     side = lax.axis_index("req") // half
     own = jnp.where(hit & (upper == side), 1.0, 0.0).astype(jnp.bfloat16)
     other = jnp.where(hit & (upper != side), 1.0, 0.0).astype(jnp.bfloat16)
-    pick = jnp.concatenate([own, other], axis=1)
-
-    def picked(first, last):
-        both = jnp.concatenate(
-            [back_ref[:, first:last], back_ref[:, part + first : part + last]], axis=0
-        )
-        return jnp.dot(pick, both, preferred_element_type=jnp.float32)
-
-    pieces = picked(width, part)
+    tile = back_ref[:, 2 * width :]
     lane = iota((n, LANES), 1)
-    prefix_lse = (
-        pieces + pltpu.roll(pieces, LANES - H, 1) + pltpu.roll(pieces, LANES - 2 * H, 1)
+    pieces = jnp.where(
+        lane < 2 * H,
+        jnp.dot(own, tile, preferred_element_type=jnp.float32),
+        jnp.dot(other, tile, preferred_element_type=jnp.float32),
     )
+    prefix_lse = pieces
+    for i in range(1, LANES // H):
+        prefix_lse += pltpu.roll(pieces, LANES - i * H, 1)
     prefix_lse = jnp.where(lane < H, prefix_lse, 0.0)
     private_lse = private_lse_ref[...]
     top = jnp.maximum(prefix_lse, private_lse)
     a, b = jnp.exp(prefix_lse - top), jnp.exp(private_lse - top)
     prefix_share = expand_heads(a / (a + b), width)
     private_share = expand_heads(b / (a + b), width)
-    prefix = picked(0, width)
+    pick = jnp.concatenate([own, other], axis=1)
+    both = jnp.concatenate([back_ref[:, :width], back_ref[:, width : 2 * width]], axis=0)
+    prefix = jnp.dot(pick, both, preferred_element_type=jnp.float32)
     attended = prefix_share * prefix + private_share * private_ref[...]
     attended = attended.astype(jnp.bfloat16)
     is_live = iota((n, 1), 0) < live_ref[0]
     departures = []
-    for i, (arrival, cols) in enumerate(zip(arrivals, blocks)):
+    for i, (arrival, block) in enumerate(zip(arrivals, blocks)):
         arrival.wait()
-        projected = jnp.dot(attended, w_ref[:, cols], preferred_element_type=jnp.float32)
-        out_ref[:, cols] = jnp.where(is_live, projected, 0.0).astype(out_ref.dtype)
-        departures.append(
-            pltpu.make_async_copy(out_ref.at[:, cols], out_hbm.at[:, cols], out_sems.at[i])
-        )
-        departures[i].start()
+        for j in range(out_sems.shape[0]):
+            chunk = width // out_sems.shape[0]
+            cols = pl.ds(j * chunk, chunk)
+            projected = jnp.dot(
+                attended[:, block], w_ref[block, cols], preferred_element_type=jnp.float32
+            )
+            if i:
+                projected += sum_ref[:, cols]
+            if i < len(blocks) - 1:
+                sum_ref[:, cols] = projected
+                continue
+            out_ref[:, cols] = jnp.where(is_live, projected, 0.0).astype(out_ref.dtype)
+            departures.append(
+                pltpu.make_async_copy(out_ref.at[:, cols], out_hbm.at[:, cols], out_sems.at[j])
+            )
+            departures[-1].start()
     for departure in departures:
         departure.wait()
 
@@ -478,7 +491,7 @@
 def finish(live, groups, back, private, private_lse, weight, half, slot_count):
     n = back.shape[0]
     width = weight.shape[1]
-    steps = len(column_blocks(width))
+    steps = len(row_blocks(width))
     return pl.pallas_call(
         functools.partial(finish_kernel, half, slot_count),
         out_shape=jax.ShapeDtypeStruct((n, width), jnp.bfloat16),
@@ -486,9 +499,10 @@
         out_specs=ANY,
         scratch_shapes=[
             pltpu.VMEM(weight.shape, weight.dtype),
+            pltpu.VMEM((n, width), jnp.float32),
             pltpu.VMEM((n, width), jnp.bfloat16),
             pltpu.SemaphoreType.DMA((steps,)),
-            pltpu.SemaphoreType.DMA((steps,)),
+            pltpu.SemaphoreType.DMA((5,)),
         ],
         compiler_params=params(50),
         cost_estimate=pl.CostEstimate(

time: 80.9 us -> 79.5 us (0.983)
  Pallas kernels: 31.9 us -> 30.8 us
    pallas_call x1, Pallas kernels: 6.96 us -> 6.09 us  [finish(): pl.pallas_call(functools.partial(finish_kernel, half, slot_count), out_sh...]
  transfers between devices with their start and end apart: 4 -> 4, of which waited for: 4 -> 4; matrix products, arithmetic and copies ran while one was open for 0% -> 0% of each run, Pallas kernels for 19% -> 20%
where the time goes in v6:
time: 79.5 us; the launch traced here: 79.1 us
  waiting for transfers between devices  31.9 us (40%)
  Pallas kernels  30.8 us (39%)
  starting transfers between devices  13.7 us (17%)
  local copies, waits for them, and re-layouts  1.77 us (2%)
  between operations  0.9 us (1%)
    all_to_all x2, waiting for transfers between devices, exchange(): lax.all_to_all(blocks, 'req', split_axis=0, concat_axis=0, tiled=True, ax...  22.9 us
    pallas_call x1, Pallas kernels, private_part(): pl.pallas_call(functools.partial(private_kernel, page_size), out_shape=(j...  15.6 us
    all_to_all x2, starting transfers between devices, exchange(): lax.all_to_all(blocks, 'req', split_axis=0, concat_axis=0, tiled=True, ax...  10.7 us
    ppermute x1, waiting for transfers between devices, per_device(): far_values = lax.ppermute(prefix_values, 'req', across)  6.83 us
    pallas_call x1, Pallas kernels, prefix_part(): pl.pallas_call(prefix_kernel, out_shape=jax.ShapeDtypeStruct((n, 2 * widt...  6.32 us
    pallas_call x1, Pallas kernels, finish(): pl.pallas_call(functools.partial(finish_kernel, half, slot_count), out_sh...  6.09 us
    pallas_call x1, Pallas kernels, place(): pl.pallas_call(functools.partial(place_kernel, half, slot_count), out_sha...  2.79 us
    ppermute x1, starting transfers between devices, per_device(): far_keys = lax.ppermute(prefix_keys, 'req', across)  2.67 us
  transfers between devices with their start and end apart: 4, of which 4 were waited for; matrix products, arithmetic and copies ran while one was open for 0% of the time, Pallas kernels for 20%

profile of v6, /device:TPU:0, one launch (start us, length us, event | category | flops | bytes accessed | tf_op | source)
XLA Modules:
  0.0 79.1 jit_solution(8459852039910524026)
XLA Ops:
  0.0 2.8 %place.1 = (bf16[128,5120]{1,0:T(8,128)(2,1)}, f32[8,128]{1,0:T(8,128)}) custom-call(s32[1,128]{1,0:T(1,128)} %bitcast.10, bf16[128,2560]{1,0:T(8,128)(2,1)} %q_hbm.3), custom_call_target="tpu_custom_call" | custom-call | flops 167772160 | bytes 1966080 | tf_op jit(solution)/shard_map/place/pallas_call | solution.py:101
  2.8 0.0 copy-start
  2.8 0.0 copy-start.3
  2.8 0.0 copy-start.4
  2.8 0.0 copy-start.5
  2.8 6.5 %all-to-all-start = ((bf16[16,8,5120]{2,1,0:T(8,128)(2,1)}), bf16[16,8,5120]{2,1,0:T(8,128)(2,1)}, u32[]{:S(2)}, u32[]{:S(2)}) async-start(bf16[16,8,5120]{2,1,0:T(8,128)(2,1)} %bitcast.15), calls=%async_computation | async-start | bytes 2621440 | tf_op jit(solution)/shard_map/all_to_all | solution.py:543
  9.3 2.7 %collective-permute-start = (bf16[256,640]{1,0:T(8,128)(2,1)}, bf16[256,640]{1,0:T(8,128)(2,1)}, u32[]{:S(2)}, u32[]{:S(2)}) collective-permute-start(bf16[256,640]{1,0:T(8,128)(2,1)} %near_k.1), channel_id=1, source_target_pairs={{0,16},{1,17},{2,18},{3,19},{4,20},{5,21},{6,22},{7,23},{8,24},{9,... | collective-permute-start | bytes 983048 | tf_op jit(solution)/shard_map/ppermute | solution.py:548
  12.0 0.3 collective-permute-start.1
  12.3 0.0 copy-done
  12.3 0.0 copy-done.3
  12.3 0.0 copy-done.4
  12.3 0.0 copy-done.5
  12.3 0.0 copy-start.2
  12.3 1.7 %copy-done.2 = bf16[128,16,640]{2,1,0:T(8,128)(2,1)S(1)} copy-done((bf16[128,16,640]{2,1,0:T(8,128)(2,1)S(1)}, bf16[128,16,640]{2,1,0:T(8,128)(2,1)}, u32[]{:S(2)}) %copy-start.2) | copy-done | bytes 2621464
  14.1 15.6 %private.1 = (f32[128,2560]{1,0:T(8,128)S(1)}, f32[128,128]{1,0:T(8,128)S(1)}) custom-call(bf16[128,2560]{1,0:T(8,128)(2,1)S(1)} %copy-done, bf16[2048,640]{1,0:T(8,128)(2,1)S(1)} %bitcast.12, bf16[2048,640]{1,0:T(8,128)(2,1)} %bitcast.16, s32[8,128]{1,0:T(8,128)S(1)} %bitcast.13, s32[1,128]{1,0:T(1,128)S(1)} %bitcast.14, f32[8,128]{1,0:T(8,128)S(1)} %copy-done.4), custom_call_target="tpu_custom_call" | custom-call | flops 2576980377600 | bytes 5242880 | tf_op jit(solution)/shard_map/private/pallas_call | solution.py:369
  29.7 2.2 %collective-permute-done.far_k = bf16[256,640]{1,0:T(8,128)(2,1)} collective-permute-done((bf16[256,640]{1,0:T(8,128)(2,1)}, bf16[256,640]{1,0:T(8,128)(2,1)}, u32[]{:S(2)}, u32[]{:S(2)}) %collective-permute-start) | collective-permute-done | bytes 327712 | tf_op jit(solution)/shard_map/ppermute | solution.py:548
  31.9 6.8 %collective-permute-done.1.far_v = bf16[256,640]{1,0:T(8,128)(2,1)} collective-permute-done((bf16[256,640]{1,0:T(8,128)(2,1)}, bf16[256,640]{1,0:T(8,128)(2,1)}, u32[]{:S(2)}, u32[]{:S(2)}) %collective-permute-start.1) | collective-permute-done | bytes 327712 | tf_op jit(solution)/shard_map/ppermute | solution.py:549
  38.8 3.8 %all-to-all-done = bf16[16,8,5120]{2,1,0:T(8,128)(2,1)} async-done(((bf16[16,8,5120]{2,1,0:T(8,128)(2,1)}), bf16[16,8,5120]{2,1,0:T(8,128)(2,1)}, u32[]{:S(2)}, u32[]{:S(2)}) %all-to-all-start) | async-done | bytes 1310752 | tf_op jit(solution)/shard_map/all_to_all | solution.py:543
  42.5 6.3 %prefix.1 = bf16[128,5248]{1,0:T(8,128)(2,1)} custom-call(bf16[128,5120]{1,0:T(8,128)(2,1)} %bitcast.2.rows_hbm, bf16[256,640]{1,0:T(8,128)(2,1)} %near_k.1, bf16[256,640]{1,0:T(8,128)(2,1)} %near_v.1, bf16[256,640]{1,0:T(8,128)(2,1)} %collective-permute-done.far_k, bf16[256,640]{1,0:T(8,128)(2,1)} %collective-permute-done.1.far_v, ...), custom_call_target="tpu_custom_call" | custom-call | flops 1342177280000 | bytes 5242880 | tf_op jit(solution)/shard_map/prefix/pallas_call | solution.py:240
  48.9 0.0 copy-start.1
  48.9 4.2 %all-to-all-start.1 = ((bf16[16,8,5248]{2,1,0:T(8,128)(2,1)}), bf16[16,8,5248]{2,1,0:T(8,128)(2,1)S(1)}, u32[]{:S(2)}, u32[]{:S(2)}) async-start(bf16[16,8,5248]{2,1,0:T(8,128)(2,1)} %bitcast.7), calls=%async_computation.1 | async-start | bytes 2686976 | tf_op jit(solution)/shard_map/all_to_all | solution.py:543
  53.8 19.1 %all-to-all-done.1 = bf16[16,8,5248]{2,1,0:T(8,128)(2,1)S(1)} async-done(((bf16[16,8,5248]{2,1,0:T(8,128)(2,1)}), bf16[16,8,5248]{2,1,0:T(8,128)(2,1)S(1)}, u32[]{:S(2)}, u32[]{:S(2)}) %all-to-all-start.1) | async-done | bytes 1343520 | tf_op jit(solution)/shard_map/all_to_all | solution.py:543
  72.9 0.0 copy-done.1
  72.9 6.1 %finish.1 = bf16[128,2560]{1,0:T(8,128)(2,1)} custom-call(s32[1]{0:T(128)S(6)} %copy.11.live_ref, s32[1,128]{1,0:T(1,128)S(1)} %bitcast.11, bf16[128,5248]{1,0:T(8,128)(2,1)S(1)} %bitcast.9, f32[128,2560]{1,0:T(8,128)S(1)} %get-tuple-element.12.private_ref, f32[128,128]{1,0:T(8,128)S(1)} %get-tuple-element.11.after_ref.private_lse_ref, bf16[2560,2560]{1,0:T(8,128)(2,1)} %w_hbm.1), custom_call_target="tpu_custom_call" | custom-call | flops 1677721600 | bytes 13107200 | tf_op jit(solution)/shard_map/finish/pallas_call | solution.py:495
Async XLA Ops:
  2.8 9.5 %copy-start = (bf16[128,2560]{1,0:T(8,128)(2,1)S(1)}, bf16[128,2560]{1,0:T(8,128)(2,1)}, u32[]{:S(2)}) copy-start(bf16[128,2560]{1,0:T(8,128)(2,1)} %q_hbm.3) | copy-start | bytes 1966084
  2.8 9.5 %copy-start.3 = (s32[128,8]{0,1:T(8,128)S(1)}, s32[128,8]{0,1:T(8,128)}, u32[]{:S(2)}) copy-start(s32[128,8]{0,1:T(8,128)} %param.15) | copy-start | bytes 12292
  2.8 9.5 %copy-start.4 = (f32[8,128]{1,0:T(8,128)S(1)}, f32[8,128]{1,0:T(8,128)}, u32[]{:S(2)}) copy-start(f32[8,128]{1,0:T(8,128)} %get-tuple-element.10.after_ref) | copy-start | bytes 12292
  2.8 9.5 %copy-start.5 = (s32[128]{0:T(128)S(1)}, s32[128]{0:T(128)}, u32[]{:S(2)}) copy-start(s32[128]{0:T(128)} %param.16) | copy-start | bytes 1540
  2.8 39.7 %all-to-all-start = ((bf16[16,8,5120]{2,1,0:T(8,128)(2,1)}), bf16[16,8,5120]{2,1,0:T(8,128)(2,1)}, u32[]{:S(2)}, u32[]{:S(2)}) async-start(bf16[16,8,5120]{2,1,0:T(8,128)(2,1)} %bitcast.15), calls=%async_computation | async-start | bytes 2621440 | tf_op jit(solution)/shard_map/all_to_all | solution.py:543
  9.3 22.6 %collective-permute-start = (bf16[256,640]{1,0:T(8,128)(2,1)}, bf16[256,640]{1,0:T(8,128)(2,1)}, u32[]{:S(2)}, u32[]{:S(2)}) collective-permute-start(bf16[256,640]{1,0:T(8,128)(2,1)} %near_k.1), channel_id=1, source_target_pairs={{0,16},{1,17},{2,18},{3,19},{4,20},{5,21},{6,22},{7,23},{8,24},{9,... | collective-permute-start | bytes 983048 | tf_op jit(solution)/shard_map/ppermute | solution.py:548
  12.0 26.8 %collective-permute-start.1 = (bf16[256,640]{1,0:T(8,128)(2,1)}, bf16[256,640]{1,0:T(8,128)(2,1)}, u32[]{:S(2)}, u32[]{:S(2)}) collective-permute-start(bf16[256,640]{1,0:T(8,128)(2,1)} %near_v.1), channel_id=1, source_target_pairs={{0,16},{1,17},{2,18},{3,19},{4,20},{5,21},{6,22},{7,23},{8,24},{9,... | collective-permute-start | bytes 983048 | tf_op jit(solution)/shard_map/ppermute | solution.py:549
  12.3 1.7 %copy-start.2 = (bf16[128,16,640]{2,1,0:T(8,128)(2,1)S(1)}, bf16[128,16,640]{2,1,0:T(8,128)(2,1)}, u32[]{:S(2)}) copy-start(bf16[128,16,640]{2,1,0:T(8,128)(2,1)} %param.13) | copy-start | bytes 7864324
  48.9 24.0 %copy-start.1 = (s32[128,1]{0,1:T(1,128)S(1)}, s32[128,1]{0,1:T(1,128)}, u32[]{:S(2)}) copy-start(s32[128,1]{0,1:T(1,128)} %param.17) | copy-start | bytes 1540
  48.9 24.0 %all-to-all-start.1 = ((bf16[16,8,5248]{2,1,0:T(8,128)(2,1)}), bf16[16,8,5248]{2,1,0:T(8,128)(2,1)S(1)}, u32[]{:S(2)}, u32[]{:S(2)}) async-start(bf16[16,8,5248]{2,1,0:T(8,128)(2,1)} %bitcast.7), calls=%async_computation.1 | async-start | bytes 2686976 | tf_op jit(solution)/shard_map/all_to_all | solution.py:543

commit v7 on v6

--- a/solution.py
+++ b/solution.py
@@ -54,13 +54,17 @@
     return jnp.sum(jnp.where(same, row, 0), axis=1, keepdims=True)
 
 
-def slots_of(groups, half, slot_count):
+def slots_of(groups, half, side, slot_count):
     n = groups.shape[1]
+    quarter = half // 2
     earlier = iota((n, n), 0) < iota((n, n), 1)
     same = (as_column(groups) == groups) & earlier
     rank = jnp.sum(jnp.where(same, 1, 0), axis=0, keepdims=True)
     upper = jnp.where(groups >= half, 1, 0)
-    return (groups - upper * half) * slot_count + rank, upper
+    far = jnp.where(upper != side, 1, 0)
+    host = groups - upper * half + far * quarter
+    host = jnp.where(host >= half, host - half, host)
+    return host * slot_count + rank, far
 
 
 def place_kernel(
@@ -80,10 +84,10 @@
     token_ref[...] = jnp.zeros_like(token_ref)
     side = lax.axis_index("req") // half
     groups_copy.wait()
-    slot, upper = slots_of(groups_ref[...], half, slot_count)
+    slot, far = slots_of(groups_ref[...], half, side, slot_count)
     hit = slot == iota((n, n), 0)
-    own = jnp.where(hit & (upper == side), 1.0, 0.0).astype(jnp.bfloat16)
-    other = jnp.where(hit & (upper != side), 1.0, 0.0).astype(jnp.bfloat16)
+    own = jnp.where(hit & (far == 0), 1.0, 0.0).astype(jnp.bfloat16)
+    other = jnp.where(hit & (far == 1), 1.0, 0.0).astype(jnp.bfloat16)
     spread = jnp.concatenate([own, other], axis=0)
     for i, arrival in enumerate(arrivals):
         arrival.wait()
@@ -136,7 +140,7 @@
 
 
 def prefix_kernel(
-    rows_hbm, near_k, near_v, far_k, far_v, after_ref, out_hbm,
+    quarter, rows_hbm, near_k, near_v, outer_k, outer_v, inner_k, inner_v, after_ref, out_hbm,
     rows_ref, k_ref, v_ref, qt_ref, vt_ref, qs_ref, ot_ref, lse_ref, scores_ref, out_ref,
     in_sems, out_sems
 ):
@@ -144,16 +148,25 @@
     n, width = rows_ref.shape
     width //= 2
     key_width = k_ref.shape[2]
+    place = lax.axis_index("req") // quarter
+    is_outer = (place == 0) | (place == 3)
     arrivals = []
-    for part, (keys, values) in enumerate(((near_k, near_v), (far_k, far_v))):
-        cols = pl.ds(part * width, width)
-        for source, target in (
-            (values, v_ref.at[part]),
-            (rows_hbm.at[:, cols], rows_ref.at[:, cols]),
-            (keys, k_ref.at[part]),
-        ):
-            arrivals.append(pltpu.make_async_copy(source, target, in_sems.at[len(arrivals)]))
+
+    def arrive(target, source, inner=None):
+        sem = in_sems.at[len(arrivals)]
+        arrivals.append(pltpu.make_async_copy(source, target, sem))
+        if inner is None:
             arrivals[-1].start()
+            return
+        pl.when(is_outer)(arrivals[-1].start)
+        pl.when(jnp.logical_not(is_outer))(pltpu.make_async_copy(inner, target, sem).start)
+
+    arrive(v_ref.at[0], near_v)
+    arrive(rows_ref.at[:, :width], rows_hbm.at[:, :width])
+    arrive(k_ref.at[0], near_k)
+    arrive(v_ref.at[1], outer_v, inner_v)
+    arrive(rows_ref.at[:, width:], rows_hbm.at[:, width:])
+    arrive(k_ref.at[1], outer_k, inner_k)
     windows = [tight_window(k * HD, key_width) for k in range(KVH)]
     for u in range(2 * KVH):
         clear_queries(qs_ref, u, *windows[u % KVH][1:])
@@ -162,9 +175,9 @@
         arrivals[3 * part].wait()
         transpose_into(vt_ref.at[part], v_ref.at[part])
         arrivals[3 * part + 1].wait()
-        transpose_into(qt_ref, rows_ref.at[:, part * width : (part + 1) * width])
+        transpose_into(qt_ref.at[part * width : (part + 1) * width], rows_ref.at[:, part * width : (part + 1) * width])
         for k in range(KVH):
-            fill_queries(qs_ref, part * KVH + k, qt_ref, k, windows[k][1])
+            fill_queries(qs_ref, part * KVH + k, qt_ref.at[part * width : (part + 1) * width], k, windows[k][1])
         arrivals[3 * part + 2].wait()
 
     def score(u):
@@ -221,9 +234,8 @@
     departures = []
     prepare(0)
     score(0)
+    prepare(1)
     for u in range(2 * KVH):
-        if u == KVH - 2:
-            prepare(1)
         if u + 1 < 2 * KVH:
             score(u + 1)
         weigh(u)
@@ -233,20 +245,20 @@
         departure.wait()
 
 
-def prefix_part(rows, near_k, near_v, far_k, far_v, after):
+def prefix_part(quarter, rows, near, outer, inner, after):
     n, width = rows.shape
     width //= 2
-    tokens, key_width = near_k.shape
+    tokens, key_width = near[0].shape
     return pl.pallas_call(
-        prefix_kernel,
+        functools.partial(prefix_kernel, quarter),
         out_shape=jax.ShapeDtypeStruct((n, 2 * width + LANES), jnp.bfloat16),
-        in_specs=[ANY] * 6,
+        in_specs=[ANY] * 8,
         out_specs=ANY,
         scratch_shapes=[
             pltpu.VMEM(rows.shape, rows.dtype),
             pltpu.VMEM((2, tokens, key_width), jnp.bfloat16),
             pltpu.VMEM((2, tokens, key_width), jnp.bfloat16),
-            pltpu.VMEM((width, n), jnp.bfloat16),
+            pltpu.VMEM((2 * width, n), jnp.bfloat16),
             pltpu.VMEM((2, key_width, tokens), jnp.bfloat16),
             pltpu.VMEM((2 * KVH, WIN, GROUP * n), jnp.bfloat16),
             pltpu.VMEM((width, n), jnp.bfloat16),
@@ -263,7 +275,7 @@
             transcendentals=n * 512 * H,
         ),
         name="prefix",
-    )(rows, near_k, near_v, far_k, far_v, after)
+    )(rows, *near, *outer, *inner, after)
 
 
 def fill_bias(bias_ref, pages, lengths, page_size):
@@ -287,11 +299,12 @@
 
 
 def private_kernel(
-    page_size, q_hbm, k_hbm, v_hbm, pages_ref, lengths_ref, after_ref,
-    out_ref, lse_ref, q_ref, k_ref, v_ref, qt_ref, vt_ref, qs_ref, bias_ref, ot_ref, lses_ref,
-    scores_a, scores_b, top_a, top_b, weights_ref, sems
+    page_size, q_hbm, k_hbm, v_hbm, pages_ref, lengths_ref, *refs
 ):
-    del after_ref
+    (
+        out_ref, lse_ref, q_ref, k_ref, v_ref, qt_ref, vt_ref, qs_ref, bias_ref, ot_ref, lses_ref,
+        scores_a, scores_b, top_a, top_b, weights_ref, sems,
+    ) = refs[-17:]
     copies = [
         pltpu.make_async_copy(source, target, sems.at[i])
         for i, (source, target) in enumerate(((q_hbm, q_ref), (k_hbm, k_ref), (v_hbm, v_ref)))
@@ -372,7 +385,7 @@
             jax.ShapeDtypeStruct((n, width), jnp.float32),
             jax.ShapeDtypeStruct((n, LANES), jnp.float32),
         ),
-        in_specs=[ANY] * 3 + [VMEM] * 2 + [ANY],
+        in_specs=[ANY] * 3 + [VMEM] * 2 + [ANY] * len(after),
         out_specs=(VMEM, VMEM),
         scratch_shapes=[
             pltpu.VMEM(queries.shape, queries.dtype),
@@ -398,7 +411,7 @@
             transcendentals=n * tokens * H,
         ),
         name="private",
-    )(queries, keys, values, pages, lengths, after)
+    )(queries, keys, values, pages, lengths, *after)
 
 
 def expand_heads(share, width):
@@ -437,12 +450,12 @@
     for i, block in enumerate(blocks):
         arrivals.append(pltpu.make_async_copy(w_hbm.at[block], w_ref.at[block], in_sems.at[i]))
         arrivals[i].start()
-    slot, upper = slots_of(groups_ref[...], half, slot_count)
-    slot, upper = as_column(slot), as_column(upper)
+    side = lax.axis_index("req") // half
+    slot, far = slots_of(groups_ref[...], half, side, slot_count)
+    slot, far = as_column(slot), as_column(far)
     hit = slot == iota((n, n), 1)
-    side = lax.axis_index("req") // half
-    own = jnp.where(hit & (upper == side), 1.0, 0.0).astype(jnp.bfloat16)
-    other = jnp.where(hit & (upper != side), 1.0, 0.0).astype(jnp.bfloat16)
+    own = jnp.where(hit & (far == 0), 1.0, 0.0).astype(jnp.bfloat16)
+    other = jnp.where(hit & (far == 1), 1.0, 0.0).astype(jnp.bfloat16)
     tile = back_ref[:, 2 * width :]
     lane = iota((n, LANES), 1)
     pieces = jnp.where(
@@ -530,7 +543,10 @@
     slot_count = 2 * row_count // devices
     page_size = pool_keys.shape[1]
     halves = [list(range(half)), list(range(half, devices))]
-    across = [(i, (i + half) % devices) for i in range(devices)]
+    quarter = devices // 4
+    mirror = [(i, (3 - i // quarter) * quarter + i % quarter) for i in range(devices)]
+    outer_pairs = [pair for pair in mirror if pair[0] // quarter in (0, 3)]
+    inner_pairs = [pair for pair in mirror if pair[0] // quarter in (1, 2)]
 
     groups = group_ids.reshape(1, row_count)
     lengths = private_length.reshape(1, row_count)
@@ -545,14 +561,15 @@
         )
         return blocks.reshape(rows.shape)
 
-    far_keys = lax.ppermute(prefix_keys, "req", across)
-    far_values = lax.ppermute(prefix_values, "req", across)
+    prompt = (prefix_keys, prefix_values)
+    outer = [lax.ppermute(x, "req", outer_pairs) for x in prompt]
+    inner = [lax.ppermute(x, "req", inner_pairs) for x in prompt]
     placed, token = place(queries, groups, half, slot_count)
     rows = exchange(placed)
     private, private_lse = private_part(
-        queries, flat_keys, flat_values, pages, lengths, token, page_size
+        queries, flat_keys, flat_values, pages, lengths, (token, outer[0]), page_size
     )
-    out = prefix_part(rows, prefix_keys, prefix_values, far_keys, far_values, private_lse)
+    out = prefix_part(quarter, rows, prompt, outer, inner, private_lse)
     back = exchange(out)
     return finish(
         live_rows, groups, back, private, private_lse, out_weight, half, slot_count

time: 79.5 us -> 74.7 us (0.940)
  waiting for transfers between devices: 31.9 us -> 21.1 us
  starting transfers between devices: 13.7 us -> 20.1 us
    ppermute x2 -> x4, waiting for transfers between devices: 9.04 us -> 0.01 us  [the longest x2 0.01 us: per_device(): outer = [lax.ppermute(x, 'req', outer_pairs) for x in prompt]]
    ppermute x2 -> x4, starting transfers between devices: 2.99 us -> 11.7 us  [the longest x2 8.86 us: per_device(): outer = [lax.ppermute(x, 'req', outer_pairs) for x in prompt]]
    all_to_all x2, starting transfers between devices: 10.7 us -> 8.43 us  [exchange(): lax.all_to_all(blocks, 'req', split_axis=0, concat_axis=0, tiled=True, ax...]
    all_to_all x2, waiting for transfers between devices: 22.9 us -> 21.1 us  [exchange(): lax.all_to_all(blocks, 'req', split_axis=0, concat_axis=0, tiled=True, ax...]
    unnamed x12 -> x16, local copies, waits for them, and re-layouts: 1.77 us -> 1.77 us
  transfers between devices with their start and end apart: 4 -> 6, of which waited for: 4 -> 2; matrix products, arithmetic and copies ran while one was open for 0% -> 0% of each run, Pallas kernels for 20% -> 24%
where the time goes in v7:
time: 74.7 us; the launch traced here: 74.3 us
  Pallas kernels  30.3 us (41%)
  waiting for transfers between devices  21.1 us (28%)
  starting transfers between devices  20.1 us (27%)
  local copies, waits for them, and re-layouts  1.77 us (2%)
  between operations  0.98 us (1%)
    all_to_all x2, waiting for transfers between devices, exchange(): lax.all_to_all(blocks, 'req', split_axis=0, concat_axis=0, tiled=True, ax...  21.1 us
    pallas_call x1, Pallas kernels, private_part(): pl.pallas_call(functools.partial(private_kernel, page_size), out_shape=(j...  15.2 us
    ppermute x2, starting transfers between devices, per_device(): outer = [lax.ppermute(x, 'req', outer_pairs) for x in prompt]  8.86 us
    all_to_all x2, starting transfers between devices, exchange(): lax.all_to_all(blocks, 'req', split_axis=0, concat_axis=0, tiled=True, ax...  8.43 us
    pallas_call x1, Pallas kernels, prefix_part(): pl.pallas_call(functools.partial(prefix_kernel, quarter), out_shape=jax.S...  6.18 us
    pallas_call x1, Pallas kernels, finish(): pl.pallas_call(functools.partial(finish_kernel, half, slot_count), out_sh...  6.09 us
    ppermute x2, starting transfers between devices, per_device(): inner = [lax.ppermute(x, 'req', inner_pairs) for x in prompt]  2.79 us
    pallas_call x1, Pallas kernels, place(): pl.pallas_call(functools.partial(place_kernel, half, slot_count), out_sha...  2.78 us
  transfers between devices with their start and end apart: 6, of which 2 were waited for; matrix products, arithmetic and copies ran while one was open for 0% of the time, Pallas kernels for 24%

profile of v7, /device:TPU:0, one launch (start us, length us, event | category | flops | bytes accessed | tf_op | source)
XLA Modules:
  0.0 74.3 jit_solution(902453465333647226)
XLA Ops:
  0.0 6.9 %collective-permute-start = (bf16[256,640]{1,0:T(8,128)(2,1)}, bf16[256,640]{1,0:T(8,128)(2,1)S(1)}, u32[]{:S(2)}, u32[]{:S(2)}) collective-permute-start(bf16[256,640]{1,0:T(8,128)(2,1)} %near_k.1), channel_id=1, source_target_pairs={{0,24},{1,25},{2,26},{3,27},{4,28},{5,29},{6,30},{7,31},{24,0},{25... | collective-permute-start | bytes 983048 | tf_op jit(solution)/shard_map/ppermute | solution.py:565
  7.0 1.4 %collective-permute-start.2 = (bf16[256,640]{1,0:T(8,128)(2,1)}, bf16[256,640]{1,0:T(8,128)(2,1)}, u32[]{:S(2)}, u32[]{:S(2)}) collective-permute-start(bf16[256,640]{1,0:T(8,128)(2,1)} %near_k.1), channel_id=1, source_target_pairs={{8,16},{9,17},{10,18},{11,19},{12,20},{13,21},{14,22},{15,23},{16,... | collective-permute-start | bytes 983048 | tf_op jit(solution)/shard_map/ppermute | solution.py:566
  8.4 1.9 %collective-permute-start.1 = (bf16[256,640]{1,0:T(8,128)(2,1)}, bf16[256,640]{1,0:T(8,128)(2,1)}, u32[]{:S(2)}, u32[]{:S(2)}) collective-permute-start(bf16[256,640]{1,0:T(8,128)(2,1)} %near_v.1), channel_id=1, source_target_pairs={{0,24},{1,25},{2,26},{3,27},{4,28},{5,29},{6,30},{7,31},{24,0},{25... | collective-permute-start | bytes 983048 | tf_op jit(solution)/shard_map/ppermute | solution.py:565
  10.3 1.4 %collective-permute-start.3 = (bf16[256,640]{1,0:T(8,128)(2,1)}, bf16[256,640]{1,0:T(8,128)(2,1)}, u32[]{:S(2)}, u32[]{:S(2)}) collective-permute-start(bf16[256,640]{1,0:T(8,128)(2,1)} %near_v.1), channel_id=1, source_target_pairs={{8,16},{9,17},{10,18},{11,19},{12,20},{13,21},{14,22},{15,23},{16,... | collective-permute-start | bytes 983048 | tf_op jit(solution)/shard_map/ppermute | solution.py:566
  11.7 2.8 %place.1 = (bf16[128,5120]{1,0:T(8,128)(2,1)}, f32[8,128]{1,0:T(8,128)}) custom-call(s32[1,128]{1,0:T(1,128)} %bitcast.10, bf16[128,2560]{1,0:T(8,128)(2,1)} %q_hbm.3), custom_call_target="tpu_custom_call" | custom-call | flops 167772160 | bytes 1966080 | tf_op jit(solution)/shard_map/place/pallas_call | solution.py:105
  14.5 0.0 copy-start
  14.5 0.0 copy-start.5
  14.5 0.0 copy-start.6
  14.5 0.0 copy-start.7
  14.5 4.5 %all-to-all-start = ((bf16[16,8,5120]{2,1,0:T(8,128)(2,1)}), bf16[16,8,5120]{2,1,0:T(8,128)(2,1)}, u32[]{:S(2)}, u32[]{:S(2)}) async-start(bf16[16,8,5120]{2,1,0:T(8,128)(2,1)} %bitcast.15), calls=%async_computation | async-start | bytes 2621440 | tf_op jit(solution)/shard_map/all_to_all | solution.py:559
  19.0 0.0 collective-permute-done.refs_1_.outer_k
  19.1 0.0 copy-done
  19.1 0.0 copy-done.5
  19.1 0.0 copy-done.6
  19.1 0.0 copy-done.7
  19.1 0.0 copy-start.2
  19.1 1.7 %copy-done.2 = bf16[128,16,640]{2,1,0:T(8,128)(2,1)S(1)} copy-done((bf16[128,16,640]{2,1,0:T(8,128)(2,1)S(1)}, bf16[128,16,640]{2,1,0:T(8,128)(2,1)}, u32[]{:S(2)}) %copy-start.2) | copy-done | bytes 2621464
  20.8 0.0 copy-start.3
  20.8 0.0 copy-start.4
  20.8 15.2 %private.1 = (f32[128,2560]{1,0:T(8,128)S(1)}, f32[128,128]{1,0:T(8,128)S(1)}) custom-call(bf16[128,2560]{1,0:T(8,128)(2,1)S(1)} %copy-done, bf16[2048,640]{1,0:T(8,128)(2,1)S(1)} %bitcast.12, bf16[2048,640]{1,0:T(8,128)(2,1)} %bitcast.16, s32[8,128]{1,0:T(8,128)S(1)} %bitcast.13, s32[1,128]{1,0:T(1,128)S(1)} %bitcast.14, f32[8,128]{1,0:T(8,128)S(1)} %copy-done.6, ...), custom_call_target="tpu_custom_call" | custom-call | flops 2576980377600 | bytes 5242880 | tf_op jit(solution)/shard_map/private/pallas_call | solution.py:382
  36.1 0.0 collective-permute-done.1.outer_v
  36.1 0.0 collective-permute-done.2.inner_k
  36.1 0.0 collective-permute-done.3.inner_v
  36.1 2.3 %all-to-all-done = bf16[16,8,5120]{2,1,0:T(8,128)(2,1)} async-done(((bf16[16,8,5120]{2,1,0:T(8,128)(2,1)}), bf16[16,8,5120]{2,1,0:T(8,128)(2,1)}, u32[]{:S(2)}, u32[]{:S(2)}) %all-to-all-start) | async-done | bytes 1310752 | tf_op jit(solution)/shard_map/all_to_all | solution.py:559
  38.4 0.0 copy-done.3
  38.4 0.0 copy-done.4
  38.4 6.2 %prefix.1 = bf16[128,5248]{1,0:T(8,128)(2,1)} custom-call(bf16[128,5120]{1,0:T(8,128)(2,1)} %bitcast.2.rows_hbm, bf16[256,640]{1,0:T(8,128)(2,1)S(1)} %copy-done.3, bf16[256,640]{1,0:T(8,128)(2,1)S(1)} %copy-done.4, bf16[256,640]{1,0:T(8,128)(2,1)S(1)} %collective-permute-done.refs_1_.outer_k, bf16[256,640]{1,0:T(8,128)(2,1)} %collective-permute-done.1.outer_v, ...), custom_call_target="tpu_custom_call" | custom-call | flops 1342177280000 | bytes 5242880 | tf_op jit(solution)/shard_map/prefix/pallas_call | solution.py:252
  44.6 0.0 copy-start.1
  44.6 3.9 %all-to-all-start.1 = ((bf16[16,8,5248]{2,1,0:T(8,128)(2,1)}), bf16[16,8,5248]{2,1,0:T(8,128)(2,1)S(1)}, u32[]{:S(2)}, u32[]{:S(2)}) async-start(bf16[16,8,5248]{2,1,0:T(8,128)(2,1)} %bitcast.7), calls=%async_computation.1 | async-start | bytes 2686976 | tf_op jit(solution)/shard_map/all_to_all | solution.py:559
  49.2 18.9 %all-to-all-done.1 = bf16[16,8,5248]{2,1,0:T(8,128)(2,1)S(1)} async-done(((bf16[16,8,5248]{2,1,0:T(8,128)(2,1)}), bf16[16,8,5248]{2,1,0:T(8,128)(2,1)S(1)}, u32[]{:S(2)}, u32[]{:S(2)}) %all-to-all-start.1) | async-done | bytes 1343520 | tf_op jit(solution)/shard_map/all_to_all | solution.py:559
  68.0 0.0 copy-done.1
  68.0 6.1 %finish.1 = bf16[128,2560]{1,0:T(8,128)(2,1)} custom-call(s32[1]{0:T(128)S(6)} %copy.11.live_ref, s32[1,128]{1,0:T(1,128)S(1)} %bitcast.11, bf16[128,5248]{1,0:T(8,128)(2,1)S(1)} %bitcast.9, f32[128,2560]{1,0:T(8,128)S(1)} %get-tuple-element.12.private_ref, f32[128,128]{1,0:T(8,128)S(1)} %get-tuple-element.11.after_ref.private_lse_ref, bf16[2560,2560]{1,0:T(8,128)(2,1)} %w_hbm.1), custom_call_target="tpu_custom_call" | custom-call | flops 1677721600 | bytes 13107200 | tf_op jit(solution)/shard_map/finish/pallas_call | solution.py:508
Async XLA Ops:
  0.0 19.1 %collective-permute-start = (bf16[256,640]{1,0:T(8,128)(2,1)}, bf16[256,640]{1,0:T(8,128)(2,1)S(1)}, u32[]{:S(2)}, u32[]{:S(2)}) collective-permute-start(bf16[256,640]{1,0:T(8,128)(2,1)} %near_k.1), channel_id=1, source_target_pairs={{0,24},{1,25},{2,26},{3,27},{4,28},{5,29},{6,30},{7,31},{24,0},{25... | collective-permute-start | bytes 983048 | tf_op jit(solution)/shard_map/ppermute | solution.py:565
  7.0 29.2 %collective-permute-start.2 = (bf16[256,640]{1,0:T(8,128)(2,1)}, bf16[256,640]{1,0:T(8,128)(2,1)}, u32[]{:S(2)}, u32[]{:S(2)}) collective-permute-start(bf16[256,640]{1,0:T(8,128)(2,1)} %near_k.1), channel_id=1, source_target_pairs={{8,16},{9,17},{10,18},{11,19},{12,20},{13,21},{14,22},{15,23},{16,... | collective-permute-start | bytes 983048 | tf_op jit(solution)/shard_map/ppermute | solution.py:566
  8.4 27.8 %collective-permute-start.1 = (bf16[256,640]{1,0:T(8,128)(2,1)}, bf16[256,640]{1,0:T(8,128)(2,1)}, u32[]{:S(2)}, u32[]{:S(2)}) collective-permute-start(bf16[256,640]{1,0:T(8,128)(2,1)} %near_v.1), channel_id=1, source_target_pairs={{0,24},{1,25},{2,26},{3,27},{4,28},{5,29},{6,30},{7,31},{24,0},{25... | collective-permute-start | bytes 983048 | tf_op jit(solution)/shard_map/ppermute | solution.py:565
  10.3 25.9 %collective-permute-start.3 = (bf16[256,640]{1,0:T(8,128)(2,1)}, bf16[256,640]{1,0:T(8,128)(2,1)}, u32[]{:S(2)}, u32[]{:S(2)}) collective-permute-start(bf16[256,640]{1,0:T(8,128)(2,1)} %near_v.1), channel_id=1, source_target_pairs={{8,16},{9,17},{10,18},{11,19},{12,20},{13,21},{14,22},{15,23},{16,... | collective-permute-start | bytes 983048 | tf_op jit(solution)/shard_map/ppermute | solution.py:566
  14.5 4.6 %copy-start = (bf16[128,2560]{1,0:T(8,128)(2,1)S(1)}, bf16[128,2560]{1,0:T(8,128)(2,1)}, u32[]{:S(2)}) copy-start(bf16[128,2560]{1,0:T(8,128)(2,1)} %q_hbm.3) | copy-start | bytes 1966084
  14.5 4.6 %copy-start.5 = (s32[128,8]{0,1:T(8,128)S(1)}, s32[128,8]{0,1:T(8,128)}, u32[]{:S(2)}) copy-start(s32[128,8]{0,1:T(8,128)} %param.15) | copy-start | bytes 12292
  14.5 4.6 %copy-start.6 = (f32[8,128]{1,0:T(8,128)S(1)}, f32[8,128]{1,0:T(8,128)}, u32[]{:S(2)}) copy-start(f32[8,128]{1,0:T(8,128)} %get-tuple-element.10.refs_0_) | copy-start | bytes 12292
  14.5 4.6 %copy-start.7 = (s32[128]{0:T(128)S(1)}, s32[128]{0:T(128)}, u32[]{:S(2)}) copy-start(s32[128]{0:T(128)} %param.16) | copy-start | bytes 1540
  14.5 23.9 %all-to-all-start = ((bf16[16,8,5120]{2,1,0:T(8,128)(2,1)}), bf16[16,8,5120]{2,1,0:T(8,128)(2,1)}, u32[]{:S(2)}, u32[]{:S(2)}) async-start(bf16[16,8,5120]{2,1,0:T(8,128)(2,1)} %bitcast.15), calls=%async_computation | async-start | bytes 2621440 | tf_op jit(solution)/shard_map/all_to_all | solution.py:559
  19.1 1.7 %copy-start.2 = (bf16[128,16,640]{2,1,0:T(8,128)(2,1)S(1)}, bf16[128,16,640]{2,1,0:T(8,128)(2,1)}, u32[]{:S(2)}) copy-start(bf16[128,16,640]{2,1,0:T(8,128)(2,1)} %param.13) | copy-start | bytes 7864324
  20.8 17.6 %copy-start.3 = (bf16[256,640]{1,0:T(8,128)(2,1)S(1)}, bf16[256,640]{1,0:T(8,128)(2,1)}, u32[]{:S(2)}) copy-start(bf16[256,640]{1,0:T(8,128)(2,1)} %near_k.1) | copy-start | bytes 983044
  20.8 17.6 %copy-start.4 = (bf16[256,640]{1,0:T(8,128)(2,1)S(1)}, bf16[256,640]{1,0:T(8,128)(2,1)}, u32[]{:S(2)}) copy-start(bf16[256,640]{1,0:T(8,128)(2,1)} %near_v.1) | copy-start | bytes 983044
  44.6 23.4 %copy-start.1 = (s32[128,1]{0,1:T(1,128)S(1)}, s32[128,1]{0,1:T(1,128)}, u32[]{:S(2)}) copy-start(s32[128,1]{0,1:T(1,128)} %param.17) | copy-start | bytes 1540
  44.6 23.4 %all-to-all-start.1 = ((bf16[16,8,5248]{2,1,0:T(8,128)(2,1)}), bf16[16,8,5248]{2,1,0:T(8,128)(2,1)S(1)}, u32[]{:S(2)}, u32[]{:S(2)}) async-start(bf16[16,8,5248]{2,1,0:T(8,128)(2,1)} %bitcast.7), calls=%async_computation.1 | async-start | bytes 2686976 | tf_op jit(solution)/shard_map/all_to_all | solution.py:559

commit v8 on v7

--- a/solution.py
+++ b/solution.py
@@ -434,7 +434,7 @@
     blocks, first = [], 0
     while first < rows:
         rest = rows - first
-        size = min(512, max(LANES, rest // 2 // LANES * LANES))
+        size = min(1024, max(WIN, rest // 2 // WIN * WIN))
         blocks.append(slice(first, first + size))
         first += size
     return blocks

time: 74.7 us -> 74.7 us (level)
  no operation moved by 1% of the time
where the time goes in v8:
time: 74.7 us; the launch traced here: 74.3 us
  Pallas kernels  30.3 us (41%)
  waiting for transfers between devices  21.1 us (28%)
  starting transfers between devices  20.1 us (27%)
  local copies, waits for them, and re-layouts  1.77 us (2%)
  between operations  0.98 us (1%)
    all_to_all x2, waiting for transfers between devices, exchange(): lax.all_to_all(blocks, 'req', split_axis=0, concat_axis=0, tiled=True, ax...  21.1 us
    pallas_call x1, Pallas kernels, private_part(): pl.pallas_call(functools.partial(private_kernel, page_size), out_shape=(j...  15.2 us
    ppermute x2, starting transfers between devices, per_device(): outer = [lax.ppermute(x, 'req', outer_pairs) for x in prompt]  8.86 us
    all_to_all x2, starting transfers between devices, exchange(): lax.all_to_all(blocks, 'req', split_axis=0, concat_axis=0, tiled=True, ax...  8.43 us
    pallas_call x1, Pallas kernels, prefix_part(): pl.pallas_call(functools.partial(prefix_kernel, quarter), out_shape=jax.S...  6.18 us
    pallas_call x1, Pallas kernels, finish(): pl.pallas_call(functools.partial(finish_kernel, half, slot_count), out_sh...  6.09 us
    ppermute x2, starting transfers between devices, per_device(): inner = [lax.ppermute(x, 'req', inner_pairs) for x in prompt]  2.79 us
    pallas_call x1, Pallas kernels, place(): pl.pallas_call(functools.partial(place_kernel, half, slot_count), out_sha...  2.78 us
  transfers between devices with their start and end apart: 6, of which 2 were waited for; matrix products, arithmetic and copies ran while one was open for 0% of the time, Pallas kernels for 24%

profile of v8, /device:TPU:0, one launch (start us, length us, event | category | flops | bytes accessed | tf_op | source)
XLA Modules:
  0.0 74.3 jit_solution(7131241466536778180)
XLA Ops:
  0.0 6.9 %collective-permute-start = (bf16[256,640]{1,0:T(8,128)(2,1)}, bf16[256,640]{1,0:T(8,128)(2,1)S(1)}, u32[]{:S(2)}, u32[]{:S(2)}) collective-permute-start(bf16[256,640]{1,0:T(8,128)(2,1)} %near_k.1), channel_id=1, source_target_pairs={{0,24},{1,25},{2,26},{3,27},{4,28},{5,29},{6,30},{7,31},{24,0},{25... | collective-permute-start | bytes 983048 | tf_op jit(solution)/shard_map/ppermute | solution.py:565
  7.0 1.4 %collective-permute-start.2 = (bf16[256,640]{1,0:T(8,128)(2,1)}, bf16[256,640]{1,0:T(8,128)(2,1)}, u32[]{:S(2)}, u32[]{:S(2)}) collective-permute-start(bf16[256,640]{1,0:T(8,128)(2,1)} %near_k.1), channel_id=1, source_target_pairs={{8,16},{9,17},{10,18},{11,19},{12,20},{13,21},{14,22},{15,23},{16,... | collective-permute-start | bytes 983048 | tf_op jit(solution)/shard_map/ppermute | solution.py:566
  8.4 1.9 %collective-permute-start.1 = (bf16[256,640]{1,0:T(8,128)(2,1)}, bf16[256,640]{1,0:T(8,128)(2,1)}, u32[]{:S(2)}, u32[]{:S(2)}) collective-permute-start(bf16[256,640]{1,0:T(8,128)(2,1)} %near_v.1), channel_id=1, source_target_pairs={{0,24},{1,25},{2,26},{3,27},{4,28},{5,29},{6,30},{7,31},{24,0},{25... | collective-permute-start | bytes 983048 | tf_op jit(solution)/shard_map/ppermute | solution.py:565
  10.3 1.4 %collective-permute-start.3 = (bf16[256,640]{1,0:T(8,128)(2,1)}, bf16[256,640]{1,0:T(8,128)(2,1)}, u32[]{:S(2)}, u32[]{:S(2)}) collective-permute-start(bf16[256,640]{1,0:T(8,128)(2,1)} %near_v.1), channel_id=1, source_target_pairs={{8,16},{9,17},{10,18},{11,19},{12,20},{13,21},{14,22},{15,23},{16,... | collective-permute-start | bytes 983048 | tf_op jit(solution)/shard_map/ppermute | solution.py:566
  11.7 2.8 %place.1 = (bf16[128,5120]{1,0:T(8,128)(2,1)}, f32[8,128]{1,0:T(8,128)}) custom-call(s32[1,128]{1,0:T(1,128)} %bitcast.10, bf16[128,2560]{1,0:T(8,128)(2,1)} %q_hbm.3), custom_call_target="tpu_custom_call" | custom-call | flops 167772160 | bytes 1966080 | tf_op jit(solution)/shard_map/place/pallas_call | solution.py:105
  14.5 0.0 copy-start
  14.5 0.0 copy-start.5
  14.5 0.0 copy-start.6
  14.5 0.0 copy-start.7
  14.5 4.5 %all-to-all-start = ((bf16[16,8,5120]{2,1,0:T(8,128)(2,1)}), bf16[16,8,5120]{2,1,0:T(8,128)(2,1)}, u32[]{:S(2)}, u32[]{:S(2)}) async-start(bf16[16,8,5120]{2,1,0:T(8,128)(2,1)} %bitcast.15), calls=%async_computation | async-start | bytes 2621440 | tf_op jit(solution)/shard_map/all_to_all | solution.py:559
  19.0 0.0 collective-permute-done.refs_1_.outer_k
  19.1 0.0 copy-done
  19.1 0.0 copy-done.5
  19.1 0.0 copy-done.6
  19.1 0.0 copy-done.7
  19.1 0.0 copy-start.2
  19.1 1.7 %copy-done.2 = bf16[128,16,640]{2,1,0:T(8,128)(2,1)S(1)} copy-done((bf16[128,16,640]{2,1,0:T(8,128)(2,1)S(1)}, bf16[128,16,640]{2,1,0:T(8,128)(2,1)}, u32[]{:S(2)}) %copy-start.2) | copy-done | bytes 2621464
  20.8 0.0 copy-start.3
  20.8 0.0 copy-start.4
  20.8 15.2 %private.1 = (f32[128,2560]{1,0:T(8,128)S(1)}, f32[128,128]{1,0:T(8,128)S(1)}) custom-call(bf16[128,2560]{1,0:T(8,128)(2,1)S(1)} %copy-done, bf16[2048,640]{1,0:T(8,128)(2,1)S(1)} %bitcast.12, bf16[2048,640]{1,0:T(8,128)(2,1)} %bitcast.16, s32[8,128]{1,0:T(8,128)S(1)} %bitcast.13, s32[1,128]{1,0:T(1,128)S(1)} %bitcast.14, f32[8,128]{1,0:T(8,128)S(1)} %copy-done.6, ...), custom_call_target="tpu_custom_call" | custom-call | flops 2576980377600 | bytes 5242880 | tf_op jit(solution)/shard_map/private/pallas_call | solution.py:382
  36.1 0.0 collective-permute-done.1.outer_v
  36.1 0.0 collective-permute-done.2.inner_k
  36.1 0.0 collective-permute-done.3.inner_v
  36.1 2.3 %all-to-all-done = bf16[16,8,5120]{2,1,0:T(8,128)(2,1)} async-done(((bf16[16,8,5120]{2,1,0:T(8,128)(2,1)}), bf16[16,8,5120]{2,1,0:T(8,128)(2,1)}, u32[]{:S(2)}, u32[]{:S(2)}) %all-to-all-start) | async-done | bytes 1310752 | tf_op jit(solution)/shard_map/all_to_all | solution.py:559
  38.4 0.0 copy-done.3
  38.4 0.0 copy-done.4
  38.4 6.2 %prefix.1 = bf16[128,5248]{1,0:T(8,128)(2,1)} custom-call(bf16[128,5120]{1,0:T(8,128)(2,1)} %bitcast.2.rows_hbm, bf16[256,640]{1,0:T(8,128)(2,1)S(1)} %copy-done.3, bf16[256,640]{1,0:T(8,128)(2,1)S(1)} %copy-done.4, bf16[256,640]{1,0:T(8,128)(2,1)S(1)} %collective-permute-done.refs_1_.outer_k, bf16[256,640]{1,0:T(8,128)(2,1)} %collective-permute-done.1.outer_v, ...), custom_call_target="tpu_custom_call" | custom-call | flops 1342177280000 | bytes 5242880 | tf_op jit(solution)/shard_map/prefix/pallas_call | solution.py:252
  44.6 0.0 copy-start.1
  44.6 3.9 %all-to-all-start.1 = ((bf16[16,8,5248]{2,1,0:T(8,128)(2,1)}), bf16[16,8,5248]{2,1,0:T(8,128)(2,1)S(1)}, u32[]{:S(2)}, u32[]{:S(2)}) async-start(bf16[16,8,5248]{2,1,0:T(8,128)(2,1)} %bitcast.7), calls=%async_computation.1 | async-start | bytes 2686976 | tf_op jit(solution)/shard_map/all_to_all | solution.py:559
  49.2 18.9 %all-to-all-done.1 = bf16[16,8,5248]{2,1,0:T(8,128)(2,1)S(1)} async-done(((bf16[16,8,5248]{2,1,0:T(8,128)(2,1)}), bf16[16,8,5248]{2,1,0:T(8,128)(2,1)S(1)}, u32[]{:S(2)}, u32[]{:S(2)}) %all-to-all-start.1) | async-done | bytes 1343520 | tf_op jit(solution)/shard_map/all_to_all | solution.py:559
  68.0 0.0 copy-done.1
  68.0 6.1 %finish.1 = bf16[128,2560]{1,0:T(8,128)(2,1)} custom-call(s32[1]{0:T(128)S(6)} %copy.11.live_ref, s32[1,128]{1,0:T(1,128)S(1)} %bitcast.11, bf16[128,5248]{1,0:T(8,128)(2,1)S(1)} %bitcast.9, f32[128,2560]{1,0:T(8,128)S(1)} %get-tuple-element.12.private_ref, f32[128,128]{1,0:T(8,128)S(1)} %get-tuple-element.11.after_ref.private_lse_ref, bf16[2560,2560]{1,0:T(8,128)(2,1)} %w_hbm.1), custom_call_target="tpu_custom_call" | custom-call | flops 1677721600 | bytes 13107200 | tf_op jit(solution)/shard_map/finish/pallas_call | solution.py:508
Async XLA Ops:
  0.0 19.1 %collective-permute-start = (bf16[256,640]{1,0:T(8,128)(2,1)}, bf16[256,640]{1,0:T(8,128)(2,1)S(1)}, u32[]{:S(2)}, u32[]{:S(2)}) collective-permute-start(bf16[256,640]{1,0:T(8,128)(2,1)} %near_k.1), channel_id=1, source_target_pairs={{0,24},{1,25},{2,26},{3,27},{4,28},{5,29},{6,30},{7,31},{24,0},{25... | collective-permute-start | bytes 983048 | tf_op jit(solution)/shard_map/ppermute | solution.py:565
  7.0 29.2 %collective-permute-start.2 = (bf16[256,640]{1,0:T(8,128)(2,1)}, bf16[256,640]{1,0:T(8,128)(2,1)}, u32[]{:S(2)}, u32[]{:S(2)}) collective-permute-start(bf16[256,640]{1,0:T(8,128)(2,1)} %near_k.1), channel_id=1, source_target_pairs={{8,16},{9,17},{10,18},{11,19},{12,20},{13,21},{14,22},{15,23},{16,... | collective-permute-start | bytes 983048 | tf_op jit(solution)/shard_map/ppermute | solution.py:566
  8.4 27.8 %collective-permute-start.1 = (bf16[256,640]{1,0:T(8,128)(2,1)}, bf16[256,640]{1,0:T(8,128)(2,1)}, u32[]{:S(2)}, u32[]{:S(2)}) collective-permute-start(bf16[256,640]{1,0:T(8,128)(2,1)} %near_v.1), channel_id=1, source_target_pairs={{0,24},{1,25},{2,26},{3,27},{4,28},{5,29},{6,30},{7,31},{24,0},{25... | collective-permute-start | bytes 983048 | tf_op jit(solution)/shard_map/ppermute | solution.py:565
  10.3 25.9 %collective-permute-start.3 = (bf16[256,640]{1,0:T(8,128)(2,1)}, bf16[256,640]{1,0:T(8,128)(2,1)}, u32[]{:S(2)}, u32[]{:S(2)}) collective-permute-start(bf16[256,640]{1,0:T(8,128)(2,1)} %near_v.1), channel_id=1, source_target_pairs={{8,16},{9,17},{10,18},{11,19},{12,20},{13,21},{14,22},{15,23},{16,... | collective-permute-start | bytes 983048 | tf_op jit(solution)/shard_map/ppermute | solution.py:566
  14.5 4.6 %copy-start = (bf16[128,2560]{1,0:T(8,128)(2,1)S(1)}, bf16[128,2560]{1,0:T(8,128)(2,1)}, u32[]{:S(2)}) copy-start(bf16[128,2560]{1,0:T(8,128)(2,1)} %q_hbm.3) | copy-start | bytes 1966084
  14.5 4.6 %copy-start.5 = (s32[128,8]{0,1:T(8,128)S(1)}, s32[128,8]{0,1:T(8,128)}, u32[]{:S(2)}) copy-start(s32[128,8]{0,1:T(8,128)} %param.15) | copy-start | bytes 12292
  14.5 4.6 %copy-start.6 = (f32[8,128]{1,0:T(8,128)S(1)}, f32[8,128]{1,0:T(8,128)}, u32[]{:S(2)}) copy-start(f32[8,128]{1,0:T(8,128)} %get-tuple-element.10.refs_0_) | copy-start | bytes 12292
  14.5 4.6 %copy-start.7 = (s32[128]{0:T(128)S(1)}, s32[128]{0:T(128)}, u32[]{:S(2)}) copy-start(s32[128]{0:T(128)} %param.16) | copy-start | bytes 1540
  14.5 23.9 %all-to-all-start = ((bf16[16,8,5120]{2,1,0:T(8,128)(2,1)}), bf16[16,8,5120]{2,1,0:T(8,128)(2,1)}, u32[]{:S(2)}, u32[]{:S(2)}) async-start(bf16[16,8,5120]{2,1,0:T(8,128)(2,1)} %bitcast.15), calls=%async_computation | async-start | bytes 2621440 | tf_op jit(solution)/shard_map/all_to_all | solution.py:559
  19.1 1.7 %copy-start.2 = (bf16[128,16,640]{2,1,0:T(8,128)(2,1)S(1)}, bf16[128,16,640]{2,1,0:T(8,128)(2,1)}, u32[]{:S(2)}) copy-start(bf16[128,16,640]{2,1,0:T(8,128)(2,1)} %param.13) | copy-start | bytes 7864324
  20.8 17.6 %copy-start.3 = (bf16[256,640]{1,0:T(8,128)(2,1)S(1)}, bf16[256,640]{1,0:T(8,128)(2,1)}, u32[]{:S(2)}) copy-start(bf16[256,640]{1,0:T(8,128)(2,1)} %near_k.1) | copy-start | bytes 983044
  20.8 17.6 %copy-start.4 = (bf16[256,640]{1,0:T(8,128)(2,1)S(1)}, bf16[256,640]{1,0:T(8,128)(2,1)}, u32[]{:S(2)}) copy-start(bf16[256,640]{1,0:T(8,128)(2,1)} %near_v.1) | copy-start | bytes 983044
  44.6 23.4 %copy-start.1 = (s32[128,1]{0,1:T(1,128)S(1)}, s32[128,1]{0,1:T(1,128)}, u32[]{:S(2)}) copy-start(s32[128,1]{0,1:T(1,128)} %param.17) | copy-start | bytes 1540
  44.6 23.4 %all-to-all-start.1 = ((bf16[16,8,5248]{2,1,0:T(8,128)(2,1)}), bf16[16,8,5248]{2,1,0:T(8,128)(2,1)S(1)}, u32[]{:S(2)}, u32[]{:S(2)}) async-start(bf16[16,8,5248]{2,1,0:T(8,128)(2,1)} %bitcast.7), calls=%async_computation.1 | async-start | bytes 2686976 | tf_op jit(solution)/shard_map/all_to_all | solution.py:559

commit v9 on v7

--- a/solution.py
+++ b/solution.py
@@ -101,7 +101,7 @@
 
 def place(queries, groups, half, slot_count):
     n, width = queries.shape
-    steps = 2
+    steps = 1
     return pl.pallas_call(
         functools.partial(place_kernel, half, slot_count),
         out_shape=(

time: 74.7 us -> 74.8 us (level)
  no operation moved by 1% of the time
where the time goes in v9:
time: 74.8 us; the launch traced here: 74.4 us
  Pallas kernels  30.2 us (40%)
  waiting for transfers between devices  21.3 us (28%)
  starting transfers between devices  20.1 us (27%)
  local copies, waits for them, and re-layouts  1.77 us (2%)
  between operations  0.98 us (1%)
    all_to_all x2, waiting for transfers between devices, exchange(): lax.all_to_all(blocks, 'req', split_axis=0, concat_axis=0, tiled=True, ax...  21.3 us
    pallas_call x1, Pallas kernels, private_part(): pl.pallas_call(functools.partial(private_kernel, page_size), out_shape=(j...  15.2 us
    ppermute x2, starting transfers between devices, per_device(): outer = [lax.ppermute(x, 'req', outer_pairs) for x in prompt]  8.86 us
    all_to_all x2, starting transfers between devices, exchange(): lax.all_to_all(blocks, 'req', split_axis=0, concat_axis=0, tiled=True, ax...  8.43 us
    pallas_call x1, Pallas kernels, prefix_part(): pl.pallas_call(functools.partial(prefix_kernel, quarter), out_shape=jax.S...  6.19 us
    pallas_call x1, Pallas kernels, finish(): pl.pallas_call(functools.partial(finish_kernel, half, slot_count), out_sh...  6.09 us
    ppermute x2, starting transfers between devices, per_device(): inner = [lax.ppermute(x, 'req', inner_pairs) for x in prompt]  2.79 us
    pallas_call x1, Pallas kernels, place(): pl.pallas_call(functools.partial(place_kernel, half, slot_count), out_sha...  2.69 us
  transfers between devices with their start and end apart: 6, of which 2 were waited for; matrix products, arithmetic and copies ran while one was open for 0% of the time, Pallas kernels for 24%

profile of v9, /device:TPU:0, one launch (start us, length us, event | category | flops | bytes accessed | tf_op | source)
XLA Modules:
  0.0 74.4 jit_solution(10847757022222494815)
XLA Ops:
  0.0 6.9 %collective-permute-start = (bf16[256,640]{1,0:T(8,128)(2,1)}, bf16[256,640]{1,0:T(8,128)(2,1)S(1)}, u32[]{:S(2)}, u32[]{:S(2)}) collective-permute-start(bf16[256,640]{1,0:T(8,128)(2,1)} %near_k.1), channel_id=1, source_target_pairs={{0,24},{1,25},{2,26},{3,27},{4,28},{5,29},{6,30},{7,31},{24,0},{25... | collective-permute-start | bytes 983048 | tf_op jit(solution)/shard_map/ppermute | solution.py:565
  7.0 1.4 %collective-permute-start.2 = (bf16[256,640]{1,0:T(8,128)(2,1)}, bf16[256,640]{1,0:T(8,128)(2,1)}, u32[]{:S(2)}, u32[]{:S(2)}) collective-permute-start(bf16[256,640]{1,0:T(8,128)(2,1)} %near_k.1), channel_id=1, source_target_pairs={{8,16},{9,17},{10,18},{11,19},{12,20},{13,21},{14,22},{15,23},{16,... | collective-permute-start | bytes 983048 | tf_op jit(solution)/shard_map/ppermute | solution.py:566
  8.4 1.9 %collective-permute-start.1 = (bf16[256,640]{1,0:T(8,128)(2,1)}, bf16[256,640]{1,0:T(8,128)(2,1)}, u32[]{:S(2)}, u32[]{:S(2)}) collective-permute-start(bf16[256,640]{1,0:T(8,128)(2,1)} %near_v.1), channel_id=1, source_target_pairs={{0,24},{1,25},{2,26},{3,27},{4,28},{5,29},{6,30},{7,31},{24,0},{25... | collective-permute-start | bytes 983048 | tf_op jit(solution)/shard_map/ppermute | solution.py:565
  10.3 1.4 %collective-permute-start.3 = (bf16[256,640]{1,0:T(8,128)(2,1)}, bf16[256,640]{1,0:T(8,128)(2,1)}, u32[]{:S(2)}, u32[]{:S(2)}) collective-permute-start(bf16[256,640]{1,0:T(8,128)(2,1)} %near_v.1), channel_id=1, source_target_pairs={{8,16},{9,17},{10,18},{11,19},{12,20},{13,21},{14,22},{15,23},{16,... | collective-permute-start | bytes 983048 | tf_op jit(solution)/shard_map/ppermute | solution.py:566
  11.7 2.7 %place.1 = (bf16[128,5120]{1,0:T(8,128)(2,1)}, f32[8,128]{1,0:T(8,128)}) custom-call(s32[1,128]{1,0:T(1,128)} %bitcast.10, bf16[128,2560]{1,0:T(8,128)(2,1)} %q_hbm.3), custom_call_target="tpu_custom_call" | custom-call | flops 167772160 | bytes 1966080 | tf_op jit(solution)/shard_map/place/pallas_call | solution.py:105
  14.4 0.0 copy-start
  14.4 0.0 copy-start.5
  14.4 0.0 copy-start.6
  14.4 0.0 copy-start.7
  14.4 4.5 %all-to-all-start = ((bf16[16,8,5120]{2,1,0:T(8,128)(2,1)}), bf16[16,8,5120]{2,1,0:T(8,128)(2,1)}, u32[]{:S(2)}, u32[]{:S(2)}) async-start(bf16[16,8,5120]{2,1,0:T(8,128)(2,1)} %bitcast.15), calls=%async_computation | async-start | bytes 2621440 | tf_op jit(solution)/shard_map/all_to_all | solution.py:559
  19.0 0.0 collective-permute-done.refs_1_.outer_k
  19.0 0.0 copy-done
  19.0 0.0 copy-done.5
  19.0 0.0 copy-done.6
  19.0 0.0 copy-done.7
  19.0 0.0 copy-start.2
  19.0 1.7 %copy-done.2 = bf16[128,16,640]{2,1,0:T(8,128)(2,1)S(1)} copy-done((bf16[128,16,640]{2,1,0:T(8,128)(2,1)S(1)}, bf16[128,16,640]{2,1,0:T(8,128)(2,1)}, u32[]{:S(2)}) %copy-start.2) | copy-done | bytes 2621464
  20.7 0.0 copy-start.3
  20.7 0.0 copy-start.4
  20.7 15.2 %private.1 = (f32[128,2560]{1,0:T(8,128)S(1)}, f32[128,128]{1,0:T(8,128)S(1)}) custom-call(bf16[128,2560]{1,0:T(8,128)(2,1)S(1)} %copy-done, bf16[2048,640]{1,0:T(8,128)(2,1)S(1)} %bitcast.12, bf16[2048,640]{1,0:T(8,128)(2,1)} %bitcast.16, s32[8,128]{1,0:T(8,128)S(1)} %bitcast.13, s32[1,128]{1,0:T(1,128)S(1)} %bitcast.14, f32[8,128]{1,0:T(8,128)S(1)} %copy-done.6, ...), custom_call_target="tpu_custom_call" | custom-call | flops 2576980377600 | bytes 5242880 | tf_op jit(solution)/shard_map/private/pallas_call | solution.py:382
  36.0 0.0 collective-permute-done.1.outer_v
  36.0 0.0 collective-permute-done.2.inner_k
  36.0 0.0 collective-permute-done.3.inner_v
  36.0 2.5 %all-to-all-done = bf16[16,8,5120]{2,1,0:T(8,128)(2,1)} async-done(((bf16[16,8,5120]{2,1,0:T(8,128)(2,1)}), bf16[16,8,5120]{2,1,0:T(8,128)(2,1)}, u32[]{:S(2)}, u32[]{:S(2)}) %all-to-all-start) | async-done | bytes 1310752 | tf_op jit(solution)/shard_map/all_to_all | solution.py:559
  38.5 0.0 copy-done.3
  38.5 0.0 copy-done.4
  38.5 6.2 %prefix.1 = bf16[128,5248]{1,0:T(8,128)(2,1)} custom-call(bf16[128,5120]{1,0:T(8,128)(2,1)} %bitcast.2.rows_hbm, bf16[256,640]{1,0:T(8,128)(2,1)S(1)} %copy-done.3, bf16[256,640]{1,0:T(8,128)(2,1)S(1)} %copy-done.4, bf16[256,640]{1,0:T(8,128)(2,1)S(1)} %collective-permute-done.refs_1_.outer_k, bf16[256,640]{1,0:T(8,128)(2,1)} %collective-permute-done.1.outer_v, ...), custom_call_target="tpu_custom_call" | custom-call | flops 1342177280000 | bytes 5242880 | tf_op jit(solution)/shard_map/prefix/pallas_call | solution.py:252
  44.7 0.0 copy-start.1
  44.7 3.9 %all-to-all-start.1 = ((bf16[16,8,5248]{2,1,0:T(8,128)(2,1)}), bf16[16,8,5248]{2,1,0:T(8,128)(2,1)S(1)}, u32[]{:S(2)}, u32[]{:S(2)}) async-start(bf16[16,8,5248]{2,1,0:T(8,128)(2,1)} %bitcast.7), calls=%async_computation.1 | async-start | bytes 2686976 | tf_op jit(solution)/shard_map/all_to_all | solution.py:559
  49.3 18.9 %all-to-all-done.1 = bf16[16,8,5248]{2,1,0:T(8,128)(2,1)S(1)} async-done(((bf16[16,8,5248]{2,1,0:T(8,128)(2,1)}), bf16[16,8,5248]{2,1,0:T(8,128)(2,1)S(1)}, u32[]{:S(2)}, u32[]{:S(2)}) %all-to-all-start.1) | async-done | bytes 1343520 | tf_op jit(solution)/shard_map/all_to_all | solution.py:559
  68.1 0.0 copy-done.1
  68.1 6.1 %finish.1 = bf16[128,2560]{1,0:T(8,128)(2,1)} custom-call(s32[1]{0:T(128)S(6)} %copy.11.live_ref, s32[1,128]{1,0:T(1,128)S(1)} %bitcast.11, bf16[128,5248]{1,0:T(8,128)(2,1)S(1)} %bitcast.9, f32[128,2560]{1,0:T(8,128)S(1)} %get-tuple-element.12.private_ref, f32[128,128]{1,0:T(8,128)S(1)} %get-tuple-element.11.after_ref.private_lse_ref, bf16[2560,2560]{1,0:T(8,128)(2,1)} %w_hbm.1), custom_call_target="tpu_custom_call" | custom-call | flops 1677721600 | bytes 13107200 | tf_op jit(solution)/shard_map/finish/pallas_call | solution.py:508
Async XLA Ops:
  0.0 19.0 %collective-permute-start = (bf16[256,640]{1,0:T(8,128)(2,1)}, bf16[256,640]{1,0:T(8,128)(2,1)S(1)}, u32[]{:S(2)}, u32[]{:S(2)}) collective-permute-start(bf16[256,640]{1,0:T(8,128)(2,1)} %near_k.1), channel_id=1, source_target_pairs={{0,24},{1,25},{2,26},{3,27},{4,28},{5,29},{6,30},{7,31},{24,0},{25... | collective-permute-start | bytes 983048 | tf_op jit(solution)/shard_map/ppermute | solution.py:565
  7.0 29.1 %collective-permute-start.2 = (bf16[256,640]{1,0:T(8,128)(2,1)}, bf16[256,640]{1,0:T(8,128)(2,1)}, u32[]{:S(2)}, u32[]{:S(2)}) collective-permute-start(bf16[256,640]{1,0:T(8,128)(2,1)} %near_k.1), channel_id=1, source_target_pairs={{8,16},{9,17},{10,18},{11,19},{12,20},{13,21},{14,22},{15,23},{16,... | collective-permute-start | bytes 983048 | tf_op jit(solution)/shard_map/ppermute | solution.py:566
  8.4 27.7 %collective-permute-start.1 = (bf16[256,640]{1,0:T(8,128)(2,1)}, bf16[256,640]{1,0:T(8,128)(2,1)}, u32[]{:S(2)}, u32[]{:S(2)}) collective-permute-start(bf16[256,640]{1,0:T(8,128)(2,1)} %near_v.1), channel_id=1, source_target_pairs={{0,24},{1,25},{2,26},{3,27},{4,28},{5,29},{6,30},{7,31},{24,0},{25... | collective-permute-start | bytes 983048 | tf_op jit(solution)/shard_map/ppermute | solution.py:565
  10.3 25.8 %collective-permute-start.3 = (bf16[256,640]{1,0:T(8,128)(2,1)}, bf16[256,640]{1,0:T(8,128)(2,1)}, u32[]{:S(2)}, u32[]{:S(2)}) collective-permute-start(bf16[256,640]{1,0:T(8,128)(2,1)} %near_v.1), channel_id=1, source_target_pairs={{8,16},{9,17},{10,18},{11,19},{12,20},{13,21},{14,22},{15,23},{16,... | collective-permute-start | bytes 983048 | tf_op jit(solution)/shard_map/ppermute | solution.py:566
  14.4 4.6 %copy-start = (bf16[128,2560]{1,0:T(8,128)(2,1)S(1)}, bf16[128,2560]{1,0:T(8,128)(2,1)}, u32[]{:S(2)}) copy-start(bf16[128,2560]{1,0:T(8,128)(2,1)} %q_hbm.3) | copy-start | bytes 1966084
  14.4 4.6 %copy-start.5 = (s32[128,8]{0,1:T(8,128)S(1)}, s32[128,8]{0,1:T(8,128)}, u32[]{:S(2)}) copy-start(s32[128,8]{0,1:T(8,128)} %param.15) | copy-start | bytes 12292
  14.4 4.6 %copy-start.6 = (f32[8,128]{1,0:T(8,128)S(1)}, f32[8,128]{1,0:T(8,128)}, u32[]{:S(2)}) copy-start(f32[8,128]{1,0:T(8,128)} %get-tuple-element.10.refs_0_) | copy-start | bytes 12292
  14.4 4.6 %copy-start.7 = (s32[128]{0:T(128)S(1)}, s32[128]{0:T(128)}, u32[]{:S(2)}) copy-start(s32[128]{0:T(128)} %param.16) | copy-start | bytes 1540
  14.4 24.1 %all-to-all-start = ((bf16[16,8,5120]{2,1,0:T(8,128)(2,1)}), bf16[16,8,5120]{2,1,0:T(8,128)(2,1)}, u32[]{:S(2)}, u32[]{:S(2)}) async-start(bf16[16,8,5120]{2,1,0:T(8,128)(2,1)} %bitcast.15), calls=%async_computation | async-start | bytes 2621440 | tf_op jit(solution)/shard_map/all_to_all | solution.py:559
  19.0 1.7 %copy-start.2 = (bf16[128,16,640]{2,1,0:T(8,128)(2,1)S(1)}, bf16[128,16,640]{2,1,0:T(8,128)(2,1)}, u32[]{:S(2)}) copy-start(bf16[128,16,640]{2,1,0:T(8,128)(2,1)} %param.13) | copy-start | bytes 7864324
  20.7 17.7 %copy-start.3 = (bf16[256,640]{1,0:T(8,128)(2,1)S(1)}, bf16[256,640]{1,0:T(8,128)(2,1)}, u32[]{:S(2)}) copy-start(bf16[256,640]{1,0:T(8,128)(2,1)} %near_k.1) | copy-start | bytes 983044
  20.7 17.7 %copy-start.4 = (bf16[256,640]{1,0:T(8,128)(2,1)S(1)}, bf16[256,640]{1,0:T(8,128)(2,1)}, u32[]{:S(2)}) copy-start(bf16[256,640]{1,0:T(8,128)(2,1)} %near_v.1) | copy-start | bytes 983044
  44.7 23.4 %copy-start.1 = (s32[128,1]{0,1:T(1,128)S(1)}, s32[128,1]{0,1:T(1,128)}, u32[]{:S(2)}) copy-start(s32[128,1]{0,1:T(1,128)} %param.17) | copy-start | bytes 1540
  44.7 23.4 %all-to-all-start.1 = ((bf16[16,8,5248]{2,1,0:T(8,128)(2,1)}), bf16[16,8,5248]{2,1,0:T(8,128)(2,1)S(1)}, u32[]{:S(2)}, u32[]{:S(2)}) async-start(bf16[16,8,5248]{2,1,0:T(8,128)(2,1)} %bitcast.7), calls=%async_computation.1 | async-start | bytes 2686976 | tf_op jit(solution)/shard_map/all_to_all | solution.py:559
